TPU v7x, 32 devices: a whole 2x2x4 slice. The times are simulated.
32 devices in a mesh: dp: 4 (over y, x), ctx: 8 (over z, core).
Axes of the slice: x: 2, y: 2, z: 4, core: 2. Of those that a mesh axis runs over, the one named last changes fastest.
Arguments:
- tokens: bfloat16 [8, 1024, 1024], P('dp', 'ctx'), may hold values from -6 to 6
- segments: int32 [8, 1024], P('dp', 'ctx'), may hold values from 0 to 18, as said below
- cotangent: bfloat16 [8, 1024, 1024], P('dp', 'ctx'), may hold values from -6 to 6
- triple_weight: bfloat16 [2, 1024, 3072], P(None, ('dp', 'ctx')), may hold values from -0.1875 to 0.1875
- triple_bias: bfloat16 [2, 3072], P(None, ('dp', 'ctx')), may hold values from -1.75 to 1.75
- proj_weight: bfloat16 [2, 1024, 1024], P(None, ('dp', 'ctx')), may hold values from -1 to 1
- proj_bias: bfloat16 [2, 1024], P(None, ('dp', 'ctx')), may hold values from -1.75 to 1.75
- inner_weight: bfloat16 [2, 1024, 4096], P(None, ('dp', 'ctx')), may hold values from -0.1875 to 0.1875
- inner_bias: bfloat16 [2, 4096], P(None, ('dp', 'ctx')), may hold values from -1.75 to 1.75
- outer_weight: bfloat16 [2, 4096, 1024], P(None, ('dp', 'ctx')), may hold values from -0.09375 to 0.09375
- outer_bias: bfloat16 [2, 1024], P(None, ('dp', 'ctx')), may hold values from -1.75 to 1.75
- first_gain: bfloat16 [2, 1024], P(None, ('dp', 'ctx')), may hold values from 0.25 to 1.75
- first_shift: bfloat16 [2, 1024], P(None, ('dp', 'ctx')), may hold values from -1.75 to 1.75
- second_gain: bfloat16 [2, 1024], P(None, ('dp', 'ctx')), may hold values from 0.25 to 1.75
- second_shift: bfloat16 [2, 1024], P(None, ('dp', 'ctx')), may hold values from -1.75 to 1.75
Outputs:
- output: bfloat16 [8, 1024, 1024], P('dp', 'ctx')
- tokens_grad: bfloat16 [8, 1024, 1024], P('dp', 'ctx')
- triple_weight_grad: float32 [2, 1024, 3072], P(None, ('dp', 'ctx'))
- triple_bias_grad: float32 [2, 2048], P(None, ('dp', 'ctx'))
- value_bias_grad: float32 [2, 1024], P(None, ('dp', 'ctx'))
- proj_weight_grad: float32 [2, 1024, 1024], P(None, ('dp', 'ctx'))
- proj_bias_grad: float32 [2, 1024], P(None, ('dp', 'ctx'))
- inner_weight_grad: float32 [2, 1024, 4096], P(None, ('dp', 'ctx'))
- inner_bias_grad: float32 [2, 4096], P(None, ('dp', 'ctx'))
- outer_weight_grad: float32 [2, 4096, 1024], P(None, ('dp', 'ctx'))
- outer_bias_grad: float32 [2, 1024], P(None, ('dp', 'ctx'))
- first_gain_grad: float32 [2, 1024], P(None, ('dp', 'ctx'))
- first_shift_grad: float32 [2, 1024], P(None, ('dp', 'ctx'))
- second_gain_grad: float32 [2, 1024], P(None, ('dp', 'ctx'))
- second_shift_grad: float32 [2, 1024], P(None, ('dp', 'ctx'))
Inputs may be any that keep to these rules, and one draw needn't show every extreme that they name: `segments`: along each sequence the numbers never fall, except for a trailing run of zeros that marks padding; each document is a run of one number; documents before the padding hold 60 to 800 tokens, the last one before the padding possibly fewer, and that last one is numbered 1024 // 60 + 1; of the 2 sequences of each index of dp, one is a single document without padding and the others are packed documents with padding.
All inputs are finite; a program needn't handle non-finite values.
Results may differ from a plain program's by a relative error of at most 0.019.
Values may be sent and summed in bfloat16 or wider, within the bound.
A program may use at most 320 MiB of HBM per device.

v0:
```python
import math

import jax
import jax.numpy as jnp
from jax import lax
from jax.sharding import PartitionSpec as P

HD = 64
ROT = 16
MICRO = 2


EPSILON = 1e-05
NEG_LARGE = -1e30


def norm_parts(hidden, gain_vector, shift_vector):
    centred = hidden - jnp.mean(hidden, axis=-1, keepdims=True)
    inverse = lax.rsqrt(jnp.mean(centred * centred, axis=-1, keepdims=True) + EPSILON)
    normed = centred * inverse
    return (normed * gain_vector + shift_vector, normed, inverse)


def norm_backward(grad_out, normed, inverse, gain_vector):
    scaled = grad_out * gain_vector
    inner_part = (
        scaled
        - jnp.mean(scaled, axis=-1, keepdims=True)
        - normed * jnp.mean(scaled * normed, axis=-1, keepdims=True)
    )
    return (inner_part * inverse, jnp.sum(grad_out * normed, axis=0), jnp.sum(grad_out, axis=0))


def rotary_tables(positions, half_rot):
    frequency = 10000.0 ** (-(2.0 * jnp.arange(half_rot, dtype=jnp.float32)) / (2 * half_rot))
    angles = positions.astype(jnp.float32)[:, None] * frequency[None, :]
    return (jnp.cos(angles)[:, None, :], jnp.sin(angles)[:, None, :])


def rotate(head_values, cosine, sine_table, direction):
    half_rot = cosine.shape[-1]
    front = head_values[..., :half_rot]
    behind = head_values[..., half_rot : 2 * half_rot]
    return jnp.concatenate(
        [
            front * cosine - direction * behind * sine_table,
            behind * cosine + direction * front * sine_table,
            head_values[..., 2 * half_rot :],
        ],
        axis=-1,
    )


def key_block(context, block_start, block_len):
    key_all, value_all, segs_all = context
    batch_size = key_all.shape[0]
    head_count = key_all.shape[2] // HD
    key_rows = lax.dynamic_slice_in_dim(key_all, block_start, block_len, 1).reshape(
        batch_size, block_len, head_count, HD
    )
    value_rows = lax.dynamic_slice_in_dim(value_all, block_start, block_len, 1).reshape(
        batch_size, block_len, head_count, HD
    )
    key_segs = lax.dynamic_slice_in_dim(segs_all, block_start, block_len, 1)
    key_pos = block_start + jnp.arange(block_len, dtype=jnp.int32)
    return (key_rows, value_rows, key_segs, key_pos)


def allowed_mask(query_pos, query_segs, key_pos, key_segs):
    causal = key_pos[None, None, :] <= query_pos[None, :, None]
    same_doc = query_segs[:, :, None] == key_segs[:, None, :]
    live = (query_segs[:, :, None] != 0) | (key_pos[None, None, :] == query_pos[None, :, None])
    return (causal & same_doc & live)[:, None]


def raw_scores(queries, key_rows):
    return jnp.einsum("bqhd,bkhd->bhqk", queries, key_rows, preferred_element_type=jnp.float32) * (
        1.0 / math.sqrt(HD)
    )


def block_length():
    return 512


def softmax_totals(queries, query_pos, query_segs, context):
    length = context[0].shape[1]
    block_len = block_length()
    batch_size, row_count, head_count = (queries.shape[0], queries.shape[1], queries.shape[2])

    def step(block_index, state_now):
        block_start = block_index * block_len
        key_rows, value_rows, key_segs, key_pos = key_block(context, block_start, block_len)
        allowed_pairs = allowed_mask(query_pos, query_segs, key_pos, key_segs)

        def compute(running_state):
            row_peak, row_total = running_state
            scores = raw_scores(queries, key_rows)
            new_peak = jnp.maximum(
                row_peak, jnp.max(jnp.where(allowed_pairs, scores, NEG_LARGE), axis=-1)
            )
            terms = jnp.where(allowed_pairs, jnp.exp(scores - new_peak[..., None]), 0.0)
            return (new_peak, row_total * jnp.exp(row_peak - new_peak) + jnp.sum(terms, axis=-1))

        return compute(state_now)

    start_state = (
        jnp.full((batch_size, head_count, row_count), NEG_LARGE, jnp.float32),
        jnp.zeros((batch_size, head_count, row_count), jnp.float32),
    )
    row_peak, row_total = lax.fori_loop(0, length // block_len, step, start_state)
    return row_peak + jnp.log(row_total)


def attention_output(queries, log_totals, query_pos, query_segs, context):
    length = context[0].shape[1]
    block_len = block_length()

    def step(block_index, state_now):
        block_start = block_index * block_len
        key_rows, value_rows, key_segs, key_pos = key_block(context, block_start, block_len)
        allowed_pairs = allowed_mask(query_pos, query_segs, key_pos, key_segs)

        def compute(running_state):
            scores = raw_scores(queries, key_rows)
            weights_low = jnp.where(
                allowed_pairs, jnp.exp(scores - log_totals[..., None]), 0.0
            ).astype(jnp.bfloat16)
            return running_state + jnp.einsum(
                "bhqk,bkhd->bqhd", weights_low, value_rows, preferred_element_type=jnp.float32
            )

        return compute(state_now)

    return lax.fori_loop(0, length // block_len, step, jnp.zeros(queries.shape, jnp.float32))


def attention_backward(queries, grad_heads, attended, log_totals, query_pos, query_segs, context):
    key_all = context[0]
    batch_size, length, model_width = key_all.shape
    block_len = block_length()
    score_scale = 1.0 / math.sqrt(HD)
    delta = jnp.transpose(jnp.sum(grad_heads.astype(jnp.float32) * attended, axis=-1), (0, 2, 1))

    def step(block_index, state_now):
        block_start = block_index * block_len
        key_rows, value_rows, key_segs, key_pos = key_block(context, block_start, block_len)
        allowed_pairs = allowed_mask(query_pos, query_segs, key_pos, key_segs)

        def compute(running_state):
            grad_query, grad_keys, grad_values = running_state
            scores = raw_scores(queries, key_rows)
            weights_full = jnp.where(allowed_pairs, jnp.exp(scores - log_totals[..., None]), 0.0)
            grad_weights = jnp.einsum(
                "bqhd,bkhd->bhqk", grad_heads, value_rows, preferred_element_type=jnp.float32
            )
            grad_scores = (weights_full * (grad_weights - delta[..., None])).astype(jnp.bfloat16)
            grad_query = (
                grad_query
                + jnp.einsum(
                    "bhqk,bkhd->bqhd", grad_scores, key_rows, preferred_element_type=jnp.float32
                )
                * score_scale
            )
            key_part = (
                jnp.einsum(
                    "bhqk,bqhd->bkhd", grad_scores, queries, preferred_element_type=jnp.float32
                )
                * score_scale
            )
            value_part = jnp.einsum(
                "bhqk,bqhd->bkhd",
                weights_full.astype(jnp.bfloat16),
                grad_heads,
                preferred_element_type=jnp.float32,
            )
            grad_keys = lax.dynamic_update_slice_in_dim(
                grad_keys, key_part.reshape(batch_size, block_len, model_width), block_start, 1
            )
            grad_values = lax.dynamic_update_slice_in_dim(
                grad_values, value_part.reshape(batch_size, block_len, model_width), block_start, 1
            )
            return (grad_query, grad_keys, grad_values)

        return compute(state_now)

    start_state = (
        jnp.zeros(queries.shape, jnp.float32),
        jnp.zeros((batch_size, length, model_width), jnp.float32),
        jnp.zeros((batch_size, length, model_width), jnp.float32),
    )
    return lax.fori_loop(0, length // block_len, step, start_state)


def forward_layer(flat, query_segs, query_pos, cosine, sine_table, params):
    (
        triple_matrix,
        triple_offset,
        proj_matrix,
        proj_offset,
        inner_matrix,
        inner_offset,
        outer_matrix,
        outer_offset,
        gain_one,
        shift_one,
        gain_two,
        shift_two,
    ) = params
    batch_size, seq_dev = query_segs.shape
    row_count, model_width = flat.shape
    head_count = model_width // HD
    normed_one, unit_one, inverse_one = norm_parts(
        flat, gain_one.astype(jnp.float32), shift_one.astype(jnp.float32)
    )
    low_one = normed_one.astype(jnp.bfloat16)
    triple = jnp.dot(
        low_one, triple_matrix, preferred_element_type=jnp.float32
    ) + triple_offset.astype(jnp.float32)
    triple = triple.reshape(batch_size, seq_dev, 3, head_count, HD)
    queries = rotate(triple[:, :, 0], cosine, sine_table, 1.0).astype(jnp.bfloat16)
    key_local = (
        rotate(triple[:, :, 1], cosine, sine_table, 1.0)
        .astype(jnp.bfloat16)
        .reshape(batch_size, seq_dev, model_width)
    )
    value_local = triple[:, :, 2].astype(jnp.bfloat16).reshape(batch_size, seq_dev, model_width)
    context = (
        lax.all_gather(key_local, "ctx", axis=1, tiled=True),
        lax.all_gather(value_local, "ctx", axis=1, tiled=True),
        lax.all_gather(query_segs, "ctx", axis=1, tiled=True),
    )
    log_totals = softmax_totals(queries, query_pos, query_segs, context)
    attended = attention_output(queries, log_totals, query_pos, query_segs, context)
    attended_low = attended.astype(jnp.bfloat16).reshape(row_count, model_width)
    branch_attend = jnp.dot(
        attended_low, proj_matrix, preferred_element_type=jnp.float32
    ) + proj_offset.astype(jnp.float32)
    normed_two, unit_two, inverse_two = norm_parts(
        flat, gain_two.astype(jnp.float32), shift_two.astype(jnp.float32)
    )
    low_two = normed_two.astype(jnp.bfloat16)
    inner_pre = jnp.dot(
        low_two, inner_matrix, preferred_element_type=jnp.float32
    ) + inner_offset.astype(jnp.float32)
    activated = jax.nn.gelu(inner_pre, approximate=False).astype(jnp.bfloat16)
    branch_mixer = jnp.dot(
        activated, outer_matrix, preferred_element_type=jnp.float32
    ) + outer_offset.astype(jnp.float32)
    result = flat + (branch_attend + branch_mixer)
    kept = (
        unit_one,
        inverse_one,
        low_one,
        unit_two,
        inverse_two,
        low_two,
        queries,
        context,
        attended,
        attended_low,
        log_totals,
        inner_pre,
        activated,
    )
    return (result, kept)


def backward_layer(grad, kept, params, query_pos, query_segs, cosine, sine_table):
    (
        triple_matrix,
        triple_offset,
        proj_matrix,
        proj_offset,
        inner_matrix,
        inner_offset,
        outer_matrix,
        outer_offset,
        gain_one,
        shift_one,
        gain_two,
        shift_two,
    ) = params
    (
        unit_one,
        inverse_one,
        low_one,
        unit_two,
        inverse_two,
        low_two,
        queries,
        context,
        attended,
        attended_low,
        log_totals,
        inner_pre,
        activated,
    ) = kept
    batch_size, seq_dev = query_segs.shape
    row_count, model_width = grad.shape
    head_count = model_width // HD
    grad_low = grad.astype(jnp.bfloat16)
    outer_matrix_grad = jnp.einsum(
        "rf,rd->fd", activated, grad_low, preferred_element_type=jnp.float32
    )
    outer_offset_grad = jnp.sum(grad_low.astype(jnp.float32), axis=0)
    proj_matrix_grad = jnp.einsum(
        "ri,rj->ij", attended_low, grad_low, preferred_element_type=jnp.float32
    )
    grad_act = jnp.einsum("rd,fd->rf", grad_low, outer_matrix, preferred_element_type=jnp.float32)
    gelu_pull = jax.vjp(lambda pre_values: jax.nn.gelu(pre_values, approximate=False), inner_pre)[1]
    grad_pre = gelu_pull(grad_act)[0].astype(jnp.bfloat16)
    inner_matrix_grad = jnp.einsum(
        "rd,rf->df", low_two, grad_pre, preferred_element_type=jnp.float32
    )
    inner_offset_grad = jnp.sum(grad_pre.astype(jnp.float32), axis=0)
    grad_two = jnp.einsum("rf,df->rd", grad_pre, inner_matrix, preferred_element_type=jnp.float32)
    back_two, gain_two_grad, shift_two_grad = norm_backward(
        grad_two, unit_two, inverse_two, gain_two.astype(jnp.float32)
    )
    grad_heads = jnp.einsum("rj,ij->ri", grad_low, proj_matrix, preferred_element_type=jnp.float32)
    grad_heads = grad_heads.astype(jnp.bfloat16).reshape(batch_size, seq_dev, head_count, HD)
    grad_query, grad_key_all, grad_value_all = attention_backward(
        queries, grad_heads, attended, log_totals, query_pos, query_segs, context
    )
    grad_key, grad_value = (
        lax.psum_scatter(
            grad_key_all.astype(jnp.bfloat16), "ctx", scatter_dimension=1, tiled=True
        ).astype(jnp.float32),
        lax.psum_scatter(
            grad_value_all.astype(jnp.bfloat16), "ctx", scatter_dimension=1, tiled=True
        ).astype(jnp.float32),
    )
    grad_query = rotate(grad_query, cosine, sine_table, -1.0)
    grad_key = rotate(
        grad_key.reshape(batch_size, seq_dev, head_count, HD), cosine, sine_table, -1.0
    )
    grad_triple = jnp.stack(
        [grad_query, grad_key, grad_value.reshape(batch_size, seq_dev, head_count, HD)], axis=2
    )
    grad_triple = grad_triple.reshape(row_count, 3 * model_width).astype(jnp.bfloat16)
    triple_matrix_grad = jnp.einsum(
        "rd,rt->dt", low_one, grad_triple, preferred_element_type=jnp.float32
    )
    triple_offset_grad = jnp.sum(grad_triple.astype(jnp.float32), axis=0)
    query_key_grad = triple_offset_grad[: 2 * model_width]
    value_offset_grad = triple_offset_grad[2 * model_width :]
    grad_one = jnp.einsum(
        "rt,dt->rd", grad_triple, triple_matrix, preferred_element_type=jnp.float32
    )
    back_one, gain_one_grad, shift_one_grad = norm_backward(
        grad_one, unit_one, inverse_one, gain_one.astype(jnp.float32)
    )
    grad_in = grad + back_one + back_two
    grad_terms = (
        triple_matrix_grad,
        query_key_grad,
        value_offset_grad,
        proj_matrix_grad,
        outer_offset_grad,
        inner_matrix_grad,
        inner_offset_grad,
        outer_matrix_grad,
        outer_offset_grad,
        gain_one_grad,
        shift_one_grad,
        gain_two_grad,
        shift_two_grad,
    )
    return (grad_in, grad_terms)


def reduce_end(grad_terms):
    (
        triple_matrix_grad,
        query_key_grad,
        value_offset_grad,
        proj_matrix_grad,
        proj_offset_grad,
        inner_matrix_grad,
        inner_offset_grad,
        outer_matrix_grad,
        outer_offset_grad,
        gain_one_grad,
        shift_one_grad,
        gain_two_grad,
        shift_two_grad,
    ) = grad_terms
    return (
        lax.psum_scatter(triple_matrix_grad, ("dp", "ctx"), scatter_dimension=0, tiled=True),
        lax.psum_scatter(query_key_grad, ("dp", "ctx"), scatter_dimension=0, tiled=True),
        lax.psum_scatter(value_offset_grad, ("dp", "ctx"), scatter_dimension=0, tiled=True),
        lax.psum_scatter(proj_matrix_grad, ("dp", "ctx"), scatter_dimension=0, tiled=True),
        lax.psum_scatter(proj_offset_grad, ("dp", "ctx"), scatter_dimension=0, tiled=True),
        lax.psum_scatter(inner_matrix_grad, ("dp", "ctx"), scatter_dimension=0, tiled=True),
        lax.psum_scatter(inner_offset_grad, ("dp", "ctx"), scatter_dimension=0, tiled=True),
        lax.psum_scatter(outer_matrix_grad, ("dp", "ctx"), scatter_dimension=0, tiled=True),
        lax.psum_scatter(outer_offset_grad, ("dp", "ctx"), scatter_dimension=0, tiled=True),
        lax.psum_scatter(gain_one_grad, ("dp", "ctx"), scatter_dimension=0, tiled=True),
        lax.psum_scatter(shift_one_grad, ("dp", "ctx"), scatter_dimension=0, tiled=True),
        lax.psum_scatter(gain_two_grad, ("dp", "ctx"), scatter_dimension=0, tiled=True),
        lax.psum_scatter(shift_two_grad, ("dp", "ctx"), scatter_dimension=0, tiled=True),
    )


def add_terms(left_terms, right_terms):
    return jax.tree.map(lambda former, latter: former + latter, left_terms, right_terms)


def per_device(
    tokens,
    segments,
    cotangent,
    triple_weight,
    triple_bias,
    proj_weight,
    proj_bias,
    inner_weight,
    inner_bias,
    outer_weight,
    outer_bias,
    first_gain,
    first_shift,
    second_gain,
    second_shift,
):
    layer_count = triple_weight.shape[0]
    local_count, seq_dev, model_width = tokens.shape
    group_rows = local_count // MICRO
    query_pos = lax.axis_index("ctx") * seq_dev + jnp.arange(seq_dev, dtype=jnp.int32)
    cosine, sine_table = rotary_tables(query_pos, ROT // 2)
    output_parts = []
    input_parts = []
    summed = [None] * layer_count
    for micro_index in range(MICRO):
        first_row = micro_index * group_rows
        segs_now = segments[first_row : first_row + group_rows]
        hidden = (
            tokens[first_row : first_row + group_rows]
            .astype(jnp.float32)
            .reshape(group_rows * seq_dev, model_width)
        )
        gathered_list = []
        kept_list = []
        for which_layer in range(layer_count):
            params = (
                lax.all_gather(triple_weight[which_layer], ("dp", "ctx"), axis=0, tiled=True),
                lax.all_gather(triple_bias[which_layer], ("dp", "ctx"), axis=0, tiled=True),
                lax.all_gather(proj_weight[which_layer], ("dp", "ctx"), axis=0, tiled=True),
                lax.all_gather(proj_bias[which_layer], ("dp", "ctx"), axis=0, tiled=True),
                lax.all_gather(inner_weight[which_layer], ("dp", "ctx"), axis=0, tiled=True),
                lax.all_gather(inner_bias[which_layer], ("dp", "ctx"), axis=0, tiled=True),
                lax.all_gather(outer_weight[which_layer], ("dp", "ctx"), axis=0, tiled=True),
                lax.all_gather(outer_bias[which_layer], ("dp", "ctx"), axis=0, tiled=True),
                lax.all_gather(first_gain[which_layer], ("dp", "ctx"), axis=0, tiled=True),
                lax.all_gather(first_shift[which_layer], ("dp", "ctx"), axis=0, tiled=True),
                lax.all_gather(second_gain[which_layer], ("dp", "ctx"), axis=0, tiled=True),
                lax.all_gather(second_shift[which_layer], ("dp", "ctx"), axis=0, tiled=True),
            )
            hidden, kept = forward_layer(hidden, segs_now, query_pos, cosine, sine_table, params)
            gathered_list.append(params)
            kept_list.append(kept)
        output_parts.append(hidden.astype(jnp.bfloat16).reshape(group_rows, seq_dev, model_width))
        grad = (
            cotangent[first_row : first_row + group_rows]
            .astype(jnp.float32)
            .reshape(group_rows * seq_dev, model_width)
        )
        for which_layer in reversed(range(layer_count)):
            params = gathered_list[which_layer]
            grad, grad_terms = backward_layer(
                grad, kept_list[which_layer], params, query_pos, segs_now, cosine, sine_table
            )
            if summed[which_layer] is None:
                summed[which_layer] = grad_terms
            else:
                summed[which_layer] = add_terms(summed[which_layer], grad_terms)
        input_parts.append(grad.astype(jnp.bfloat16).reshape(group_rows, seq_dev, model_width))
    summed = [reduce_end(layer_terms) for layer_terms in summed]
    output = jnp.concatenate(output_parts, axis=0)
    tokens_grad = jnp.concatenate(input_parts, axis=0)
    stacked = tuple(
        (
            jnp.stack([summed[which_layer][member] for which_layer in range(layer_count)], axis=0)
            for member in range(13)
        )
    )
    return (output, tokens_grad) + stacked


def solution(mesh):
    in_specs = (
        P("dp", "ctx", None),
        P("dp", "ctx"),
        P("dp", "ctx", None),
        P(None, ("dp", "ctx"), None),
        P(None, ("dp", "ctx")),
        P(None, ("dp", "ctx"), None),
        P(None, ("dp", "ctx")),
        P(None, ("dp", "ctx"), None),
        P(None, ("dp", "ctx")),
        P(None, ("dp", "ctx"), None),
        P(None, ("dp", "ctx")),
        P(None, ("dp", "ctx")),
        P(None, ("dp", "ctx")),
        P(None, ("dp", "ctx")),
        P(None, ("dp", "ctx")),
    )
    out_specs = (
        P("dp", "ctx", None),
        P("dp", "ctx", None),
        P(None, ("dp", "ctx"), None),
        P(None, ("dp", "ctx")),
        P(None, ("dp", "ctx")),
        P(None, ("dp", "ctx"), None),
        P(None, ("dp", "ctx")),
        P(None, ("dp", "ctx"), None),
        P(None, ("dp", "ctx")),
        P(None, ("dp", "ctx"), None),
        P(None, ("dp", "ctx")),
        P(None, ("dp", "ctx")),
        P(None, ("dp", "ctx")),
        P(None, ("dp", "ctx")),
        P(None, ("dp", "ctx")),
    )
    return jax.shard_map(
        per_device, mesh=mesh, in_specs=in_specs, out_specs=out_specs, check_vma=False
    )
```

profile of v0, /device:TPU:5, one launch (start us, length us, event | category | flops | bytes accessed | tf_op | source)
XLA Modules:
  0.0 2712.2 jit_solution(13063647778848835836)
XLA Ops:
  27.6 41.5 %all-reduce.31 = (bf16[1024]{0:T(1024)(128)(2,1)S(1)}, bf16[1024]{0:T(1024)(128)(2,1)S(1)}, bf16[1024]{0:T(1024)(128)(2,1)S(1)}, bf16[3072]{0:T(1024)(128)(2,1)S...) all-reduce(bf16[1024]{0:T(1024)(128)(2,1)S(1)} %dynamic-update-slic, ...), channel_id=13, replica_groups=mesh['dp'=4,'ctx'=8] {'dp','ctx'}, use_global_device_ids=true, to_apply=%add.6 | all-reduce | flops 18432 | bytes 73728
  97.2 39.0 %all-gather.9 = bf16[1,4096]{1,0:T(2,128)(2,1)S(1)} all-gather(bf16[1,128]{1,0:T(2,128)(2,1)S(1)} %get-tuple-element.3078), channel_id=11, replica_groups=mesh['dp'=4,'ctx'=8] {'dp','ctx'}, dimensions={1}, use_global_device_ids=true | all-gather | bytes 8448 | tf_op jit(solution)/shard_map/all_gather | solution.py:452
  153.6 15.5 while.192
  181.0 51.8 %all-gather.61.cloned.1.call-done = bf16[1,1024,4096]{2,1,0:T(8,128)(2,1)} async-done(((bf16[1,32,4096]{2,1,0:T(8,128)(2,1)}), bf16[1,1024,4096]{2,1,0:T(8,128)(2,1)}) %all-gather.61.cloned.1.call-update) | async-done | bytes 8388624 | tf_op jit(solution)/shard_map/all_gather | solution.py:451
  242.0 70.3 %all-gather.63.cloned.1.call-done = bf16[1,4096,1024]{2,1,0:T(8,128)(2,1)} async-done(((bf16[1,128,1024]{2,1,0:T(8,128)(2,1)}), bf16[1,4096,1024]{2,1,0:T(8,128)(2,1)}) %all-gather.63.cloned.1.call-update) | async-done | bytes 8388624 | tf_op jit(solution)/shard_map/all_gather | solution.py:453
  316.9 53.3 %all-gather.59.cloned.1.call-done = bf16[1,1024,1024]{2,1,0:T(8,128)(2,1)} async-done(((bf16[1,32,1024]{2,1,0:T(8,128)(2,1)}), bf16[1,1024,1024]{2,1,0:T(8,128)(2,1)}) %all-gather.59.cloned.1.call-update) | async-done | bytes 2097168 | tf_op jit(solution)/shard_map/all_gather | solution.py:449
  372.6 68.9 %all-gather.65.cloned.1.call-done = bf16[1,1024,3072]{2,1,0:T(8,128)(2,1)} async-done(((bf16[1,32,3072]{2,1,0:T(8,128)(2,1)}), bf16[1,1024,3072]{2,1,0:T(8,128)(2,1)}) %all-gather.65.cloned.1.call-update) | async-done | bytes 6291472 | tf_op jit(solution)/shard_map/all_gather | solution.py:447
  480.1 15.8 while.196
  495.9 16.3 all-gather.49.cloned.1.call-done
  512.2 14.2 while.197
  544.5 26.4 all-gather.67.cloned.1.call-done
  578.9 23.1 all-gather.55.cloned.1.call-done
  602.0 17.5 while.198
  619.5 13.9 all-gather.53.cloned.1.call-done
  647.2 32.3 %while.202 = (s32[]{:T(128)}, f32[1,128,16,64]{1,3,2,0:T(8,128)}, bf16[1,1024,1024]{1,2,0:T(8,128)(2,1)}, bf16[1,1024,1024]{1,2,0:T(8,128)(2,1)}, bf16[1,1024,10...) while((s32[]{:T(128)}, f32[1,128,16,64]{1,3,2,0:T(8,128)}, ...), condition=%wide.region_52.53_spmd.clone, body=%wide.region_51.52_spmd.clone.sunk | while | flops 683410176 | bytes 68391520 | solution.py:192
  695.4 15.5 while.194
  738.3 29.5 %while.200 = (s32[]{:T(128)}, f32[1,128,16,64]{1,3,2,0:T(8,128)}, bf16[1,1024,1024]{1,2,0:T(8,128)(2,1)}, bf16[1,1024,1024]{1,2,0:T(8,128)(2,1)}, bf16[1,1024,10...) while((s32[]{:T(128)}, f32[1,128,16,64]{1,3,2,0:T(8,128)}, ...), condition=%wide.region_34.35_spmd.clone, body=%wide.region_33.34_spmd.clone.sunk | while | flops 683410176 | bytes 68391520 | solution.py:192
  783.6 37.3 %all-gather.21 = bf16[1,4096]{1,0:T(2,128)(2,1)S(1)} all-gather(bf16[1,128]{1,0:T(2,128)(2,1)S(1)} %copy-done.184), channel_id=23, replica_groups=mesh['dp'=4,'ctx'=8] {'dp','ctx'}, dimensions={1}, use_global_device_ids=true | all-gather | bytes 8448 | tf_op jit(solution)/shard_map/all_gather | solution.py:452
  840.8 14.7 all-gather.71.cloned.1.call-done
  866.6 22.2 reduce-scatter.57.cloned.1.call-done
  892.0 33.5 %reduce-scatter.59.cloned.1.call-done = bf16[128,1024]{1,0:T(8,128)(2,1)} async-done(((bf16[1024,1024]{1,0:T(8,128)(2,1)}), bf16[128,1024]{1,0:T(8,128)(2,1)}) %reduce-scatter.59.cloned.1.call-update) | async-done | bytes 262160
  952.1 28.6 %while.203 = (s32[]{:T(128)}, f32[1,128,16,64]{1,3,2,0:T(8,128)}, bf16[1,1024,1024]{1,2,0:T(8,128)(2,1)}, bf16[1,1024,1024]{1,2,0:T(8,128)(2,1)}, bf16[1,1024,10...) while((s32[]{:T(128)}, f32[1,128,16,64]{1,3,2,0:T(8,128)}, ...), condition=%wide.region_61.62_spmd.clone, body=%wide.region_60.61_spmd.clone.sunk | while | flops 683410176 | bytes 68391520 | solution.py:192
  1062.4 28.7 %while.201 = (s32[]{:T(128)}, f32[1,128,16,64]{1,3,2,0:T(8,128)}, bf16[1,1024,1024]{1,2,0:T(8,128)(2,1)}, bf16[1,1024,1024]{1,2,0:T(8,128)(2,1)}, bf16[1,1024,10...) while((s32[]{:T(128)}, f32[1,128,16,64]{1,3,2,0:T(8,128)}, ...), condition=%wide.region_43.44_spmd.clone, body=%wide.region_42.43_spmd.clone.sunk | while | flops 683410176 | bytes 68391520 | solution.py:192
  1315.6 32.4 %all-reduce.34.cloned.1.call-done = (f32[2048]{0:T(1024)}, f32[2048]{0:T(1024)}, f32[1024]{0:T(1024)}, f32[1024]{0:T(1024)}, f32[1024]{0:T(1024)}, /*index=5*/f3...) async-done(((f32[2048]{0:T(1024)}, f32[2048]{0:T(1024)}, ...) | async-done | bytes 98320
  1364.0 128.3 %reduce-scatter.39.cloned.1.call-done = f32[32,1024]{1,0:T(8,128)} async-done(((f32[1024,1024]{1,0:T(8,128)}), f32[32,1024]{1,0:T(8,128)}) %reduce-scatter.39.cloned.1.call-update) | async-done | bytes 131088 | tf_op jit(solution)/shard_map/reduce_scatter | solution.py:393
  1492.3 141.7 %reduce-scatter.37.cloned.1.call-done = f32[32,1024]{1,0:T(8,128)} async-done(((f32[1024,1024]{1,0:T(8,128)}), f32[32,1024]{1,0:T(8,128)}) %reduce-scatter.37.cloned.1.call-update) | async-done | bytes 131088 | tf_op jit(solution)/shard_map/reduce_scatter | solution.py:393
  1635.7 159.7 %reduce-scatter.35.cloned.1.call-done = f32[32,3072]{1,0:T(8,128)} async-done(((f32[1024,3072]{1,0:T(8,128)}), f32[32,3072]{1,0:T(8,128)}) %reduce-scatter.35.cloned.1.call-update) | async-done | bytes 393232 | tf_op jit(solution)/shard_map/reduce_scatter | solution.py:390
  1795.4 161.5 %reduce-scatter.33.cloned.1.call-done = f32[32,3072]{1,0:T(8,128)} async-done(((f32[1024,3072]{1,0:T(8,128)}), f32[32,3072]{1,0:T(8,128)}) %reduce-scatter.33.cloned.1.call-update) | async-done | bytes 393232 | tf_op jit(solution)/shard_map/reduce_scatter | solution.py:390
  1959.0 183.4 %reduce-scatter.47.cloned.1.call-done = f32[128,1024]{1,0:T(8,128)} async-done(((f32[4096,1024]{1,0:T(8,128)}), f32[128,1024]{1,0:T(8,128)}) %reduce-scatter.47.cloned.1.call-update) | async-done | bytes 524304 | tf_op jit(solution)/shard_map/reduce_scatter | solution.py:397
  2142.4 186.7 %reduce-scatter.45.cloned.1.call-done = f32[128,1024]{1,0:T(8,128)} async-done(((f32[4096,1024]{1,0:T(8,128)}), f32[128,1024]{1,0:T(8,128)}) %reduce-scatter.45.cloned.1.call-update) | async-done | bytes 524304 | tf_op jit(solution)/shard_map/reduce_scatter | solution.py:397
  2331.3 184.4 %reduce-scatter.43.cloned.1.call-done = f32[32,4096]{1,0:T(8,128)} async-done(((f32[1024,4096]{1,0:T(8,128)}), f32[32,4096]{1,0:T(8,128)}) %reduce-scatter.43.cloned.1.call-update) | async-done | bytes 524304 | tf_op jit(solution)/shard_map/reduce_scatter | solution.py:395
  2515.7 186.5 %reduce-scatter.41.cloned.1.call-done = f32[32,4096]{1,0:T(8,128)} async-done(((f32[1024,4096]{1,0:T(8,128)}), f32[32,4096]{1,0:T(8,128)}) %reduce-scatter.41.cloned.1.call-update) | async-done | bytes 524304 | tf_op jit(solution)/shard_map/reduce_scatter | solution.py:395
  (1080 shorter events, 841.3 us)
Async XLA Ops:
  7.2 76.4 %all-gather.57.cloned.1.call-start = ((), (), s32[]{:S(2)}) async-start(), calls=%async_computation.32 | async-start | bytes 6488064 | tf_op jit(solution)/shard_map/all_gather | solution.py:447
  9.1 144.5 %all-gather.43.cloned.1.call-start = ((), (), s32[]{:S(2)}) async-start(), calls=%async_computation.17 | async-start | bytes 2359296 | tf_op jit(solution)/shard_map/all_gather | solution.py:229
  91.4 78.4 %all-gather.41.cloned.1.call-start = ((), (), s32[]{:S(2)}) async-start(), calls=%async_computation.16 | async-start | bytes 2359296 | tf_op jit(solution)/shard_map/all_gather | solution.py:230
  93.2 139.6 %all-gather.61.cloned.1.call-start = ((), (), s32[]{:S(2)}) async-start(), calls=%async_computation.34 | async-start | bytes 8650752 | tf_op jit(solution)/shard_map/all_gather | solution.py:451
  94.1 218.1 %all-gather.63.cloned.1.call-start = ((), (), s32[]{:S(2)}) async-start(), calls=%async_computation.35 | async-start | bytes 8650752 | tf_op jit(solution)/shard_map/all_gather | solution.py:453
  95.1 275.2 %all-gather.59.cloned.1.call-start = ((), (), s32[]{:S(2)}) async-start(), calls=%async_computation.33 | async-start | bytes 2162688 | tf_op jit(solution)/shard_map/all_gather | solution.py:449
  95.8 345.7 %all-gather.65.cloned.1.call-start = ((), (), s32[]{:S(2)}) async-start(), calls=%async_computation.36 | async-start | bytes 6488064 | tf_op jit(solution)/shard_map/all_gather | solution.py:447
  96.6 383.6 %all-gather.51.cloned.1.call-start = ((), (), s32[]{:S(2)}) async-start(), calls=%async_computation.21 | async-start | bytes 2359296 | tf_op jit(solution)/shard_map/all_gather | solution.py:229
  452.8 118.2 %all-gather.67.cloned.1.call-start = ((), (), s32[]{:S(2)}) async-start(), calls=%async_computation.37 | async-start | bytes 2162688 | tf_op jit(solution)/shard_map/all_gather | solution.py:449
  453.4 148.6 %all-gather.55.cloned.1.call-start = ((), (), s32[]{:S(2)}) async-start(), calls=%async_computation.23 | async-start | bytes 2359296 | tf_op jit(solution)/shard_map/all_gather | solution.py:229
  537.7 95.7 %all-gather.53.cloned.1.call-start = ((), (), s32[]{:S(2)}) async-start(), calls=%async_computation.22 | async-start | bytes 2359296 | tf_op jit(solution)/shard_map/all_gather | solution.py:230
  539.5 155.3 %all-gather.47.cloned.1.call-start = ((), (), s32[]{:S(2)}) async-start(), calls=%async_computation.19 | async-start | bytes 2359296 | tf_op jit(solution)/shard_map/all_gather | solution.py:229
  541.4 169.5 %all-gather.45.cloned.1.call-start = ((), (), s32[]{:S(2)}) async-start(), calls=%async_computation.18 | async-start | bytes 2359296 | tf_op jit(solution)/shard_map/all_gather | solution.py:230
  543.2 290.4 %all-gather.69.cloned.1.call-start = ((), (), s32[]{:S(2)}) async-start(), calls=%async_computation.38 | async-start | bytes 8650752 | tf_op jit(solution)/shard_map/all_gather | solution.py:451
  543.8 311.7 %all-gather.71.cloned.1.call-start = ((), (), s32[]{:S(2)}) async-start(), calls=%async_computation.39 | async-start | bytes 8650752 | tf_op jit(solution)/shard_map/all_gather | solution.py:453
  544.4 344.4 %reduce-scatter.57.cloned.1.call-start = ((), (), s32[]{:S(2)}) async-start(), calls=%async_computation.44 | async-start | bytes 2359296
  694.7 230.8 %reduce-scatter.59.cloned.1.call-start = ((), (), s32[]{:S(2)}) async-start(), calls=%async_computation.45 | async-start | bytes 2359296
  735.1 279.1 %reduce-scatter.49.cloned.1.call-start = ((), (), s32[]{:S(2)}) async-start(), calls=%async_computation.40 | async-start | bytes 2359296
  783.0 236.2 %reduce-scatter.51.cloned.1.call-start = ((), (), s32[]{:S(2)}) async-start(), calls=%async_computation.41 | async-start | bytes 2359296
  833.6 202.3 %reduce-scatter.61.cloned.1.call-start = ((), (), s32[]{:S(2)}) async-start(), calls=%async_computation.46 | async-start | bytes 2359296
  995.9 148.4 %reduce-scatter.63.cloned.1.call-start = ((), (), s32[]{:S(2)}) async-start(), calls=%async_computation.47 | async-start | bytes 2359296
  1034.6 131.8 %reduce-scatter.53.cloned.1.call-start = ((), (), s32[]{:S(2)}) async-start(), calls=%async_computation.42 | async-start | bytes 2359296
  1106.3 71.4 %reduce-scatter.55.cloned.1.call-start = ((), (), s32[]{:S(2)}) async-start(), calls=%async_computation.43 | async-start | bytes 2359296
  1135.9 212.1 %all-reduce.34.cloned.1.call-start = ((), (), s32[]{:S(2)}) async-start(), calls=%async_computation.48 | async-start | bytes 196608
  1197.2 295.2 %reduce-scatter.39.cloned.1.call-start = ((), (), s32[]{:S(2)}) async-start(), calls=%async_computation.27 | async-start | bytes 4325376 | tf_op jit(solution)/shard_map/reduce_scatter | solution.py:393
  1202.4 431.6 %reduce-scatter.37.cloned.1.call-start = ((), (), s32[]{:S(2)}) async-start(), calls=%async_computation.26 | async-start | bytes 4325376 | tf_op jit(solution)/shard_map/reduce_scatter | solution.py:393
  1206.7 588.7 %reduce-scatter.35.cloned.1.call-start = ((), (), s32[]{:S(2)}) async-start(), calls=%async_computation.25 | async-start | bytes 12976128 | tf_op jit(solution)/shard_map/reduce_scatter | solution.py:390
  1216.6 740.3 %reduce-scatter.33.cloned.1.call-start = ((), (), s32[]{:S(2)}) async-start(), calls=%async_computation.24 | async-start | bytes 12976128 | tf_op jit(solution)/shard_map/reduce_scatter | solution.py:390
  1226.4 916.0 %reduce-scatter.47.cloned.1.call-start = ((), (), s32[]{:S(2)}) async-start(), calls=%async_computation.31 | async-start | bytes 17301504 | tf_op jit(solution)/shard_map/reduce_scatter | solution.py:397
  1251.9 1077.1 %reduce-scatter.45.cloned.1.call-start = ((), (), s32[]{:S(2)}) async-start(), calls=%async_computation.30 | async-start | bytes 17301504 | tf_op jit(solution)/shard_map/reduce_scatter | solution.py:397
  1266.8 1248.9 %reduce-scatter.43.cloned.1.call-start = ((), (), s32[]{:S(2)}) async-start(), calls=%async_computation.29 | async-start | bytes 17301504 | tf_op jit(solution)/shard_map/reduce_scatter | solution.py:395
  1279.4 1422.8 %reduce-scatter.41.cloned.1.call-start = ((), (), s32[]{:S(2)}) async-start(), calls=%async_computation.28 | async-start | bytes 17301504 | tf_op jit(solution)/shard_map/reduce_scatter | solution.py:395
  (215 other events, 6941.8 us)
Sparse Core Ops, SparseCore 0:
  11.6 71.9 all-gather.56
  91.5 29.1 all-gather.42
  122.8 29.9 all-gather.40
  156.2 76.5 all-gather.60
  236.3 75.9 all-gather.62
  315.1 55.0 all-gather.58
  373.2 68.2 all-gather.64
  482.3 29.8 all-gather.48
  515.1 55.8 all-gather.66
  572.5 29.4 all-gather.54
  603.4 29.8 all-gather.52
  634.9 29.8 all-gather.46
  666.3 29.8 all-gather.44
  699.1 76.8 all-gather.68
  779.4 76.0 all-gather.70
  857.6 31.1 reduce-scatter.56
  891.0 34.4 reduce-scatter.58
  927.8 34.5 reduce-scatter.48
  964.5 34.3 reduce-scatter.50
  1001.2 34.6 reduce-scatter.60
  1038.2 34.6 reduce-scatter.62
  1106.4 34.5 reduce-scatter.52
  1143.1 34.4 reduce-scatter.54
  1197.3 150.6 all-reduce.33
  1352.3 140.0 reduce-scatter.38
  1494.5 139.5 reduce-scatter.36
  1640.0 155.3 reduce-scatter.34
  1802.5 154.3 reduce-scatter.32
  1959.0 183.2 reduce-scatter.46
  2144.7 184.3 reduce-scatter.44
  2331.3 184.3 reduce-scatter.42
  2517.9 184.3 reduce-scatter.40
  (1 shorter events, 29.0 us)
where the time goes:
time: 2730 us; the launch traced here: 2710 us
  waiting for transfers between devices  1790 us (66%)
  matrix products  377 us (14%)
  local copies, waits for them, and re-layouts  305 us (11%)
  blocking collectives  137 us (5%)
  other arithmetic  83.1 us (3%)
    reduce_scatter x2, waiting for transfers between devices, reduce_end(): lax.psum_scatter(inner_matrix_grad, ('dp', 'ctx'), scatter_dimension=0, t...  371 us
    reduce_scatter x2, waiting for transfers between devices, reduce_end(): lax.psum_scatter(outer_matrix_grad, ('dp', 'ctx'), scatter_dimension=0, t...  370 us
    reduce_scatter x2, waiting for transfers between devices, reduce_end(): lax.psum_scatter(triple_matrix_grad, ('dp', 'ctx'), scatter_dimension=0,...  321 us
    reduce_scatter x2, waiting for transfers between devices, reduce_end(): lax.psum_scatter(proj_matrix_grad, ('dp', 'ctx'), scatter_dimension=0, ti...  270 us
    unnamed x432, local copies, waits for them, and re-layouts  169 us
    unnamed x42, waiting for transfers between devices  101 us
    all_gather x2, waiting for transfers between devices, per_device(): lax.all_gather(outer_weight[which_layer], ('dp', 'ctx'), axis=0, tiled=True)  85 us
    all_gather x2, waiting for transfers between devices, per_device(): lax.all_gather(triple_weight[which_layer], ('dp', 'ctx'), axis=0, tiled=T...  80.1 us
  transfers between devices with their start and end apart: 33, of which 24 were waited for; matrix products, arithmetic and copies ran while one was open for 25% of the time, Pallas kernels for 0%

commit v1 on v0

v1 whole, which is shorter than its diff:
```python
import functools
import math

import jax
import jax.numpy as jnp
from jax import lax
from jax.experimental import pallas as pl
from jax.experimental.pallas import tpu as pltpu
from jax.sharding import Mesh
from jax.sharding import PartitionSpec as P

HD = 64
ROT = 16
EPSILON = 1e-05
NEG_LARGE = -1e30
MESH = pl.DeviceIdType.MESH
BF16 = jnp.bfloat16
F32 = jnp.float32
VMEM_LIMIT = 60 * 1024 * 1024


def dot(a, b, dims):
    return lax.dot_general(a, b, (dims, ((), ())), preferred_element_type=F32)


NN = ((1,), (0,))
NT = ((1,), (1,))
TN = ((0,), (0,))


def rows_of(b, size):
    return pl.ds(pl.multiple_of(b * size, size), size)


def group_barrier(tn):
    t = lax.axis_index("t")
    zc, co = t // 2, lax.rem(t, 2)
    chips = tn // 2
    sem = pltpu.get_barrier_semaphore()
    peers = [zc * 2 + 1 - co] + [lax.rem(zc + k, chips) * 2 + co for k in range(1, chips)]
    for p in peers:
        pl.semaphore_signal(sem, inc=1, device_id={"t": p}, device_id_type=MESH)
    pl.semaphore_wait(sem, len(peers))


class Spread:
    def __init__(self, tn, buf, size, ssem, fsem, rsem):
        self.tn, self.buf, self.size = tn, buf, size
        self.ssem, self.fsem, self.rsem = ssem, fsem, rsem
        self.t = lax.axis_index("t")
        self.zc, self.co = self.t // 2, lax.rem(self.t, 2)
        self.chips = tn // 2

    def copy(self, block, send, to):
        ref = self.buf.at[rows_of(block, self.size)]
        return pltpu.make_async_remote_copy(
            ref, ref, send, self.rsem.at[block], device_id={"t": to}, device_id_type=MESH
        )

    def start(self):
        for k in range(1, self.chips):
            chip = lax.rem(self.zc + k, self.chips)
            self.copy(self.t, self.ssem.at[k], chip * 2 + self.co).start()
        self.copy(self.t, self.ssem.at[0], self.zc * 2 + 1 - self.co).start()

    def peer_core(self):
        b = self.zc * 2 + 1 - self.co
        self.copy(b, self.ssem.at[0], b).wait_recv()
        return b

    def same_core(self, k):
        b = lax.rem(self.zc + self.chips - k, self.chips) * 2 + self.co
        self.copy(b, self.fsem.at[k], b).wait_recv()
        self.copy(b, self.fsem.at[k], self.zc * 2 + 1 - self.co).start()
        return b

    def other_core(self, k):
        b = lax.rem(self.zc + self.chips - k, self.chips) * 2 + 1 - self.co
        self.copy(b, self.fsem.at[k], b).wait_recv()
        return b

    def finish(self):
        for k in range(self.chips):
            self.copy(self.t, self.ssem.at[k], self.t).wait_send()
        for k in range(1, self.chips):
            self.copy(self.t, self.fsem.at[k], self.t).wait_send()


class Gather:
    def __init__(self, tn, tocore, fromcore, toici, fromici, sems):
        self.tn = tn
        self.tocore, self.fromcore, self.toici, self.fromici = tocore, fromcore, toici, fromici
        self.cs, self.cr, self.ls, self.lr = sems
        self.t = lax.axis_index("t")
        self.zc, self.co = self.t // 2, lax.rem(self.t, 2)
        self.chips = tn // 2

    def core_copy(self, chip):
        return pltpu.make_async_remote_copy(
            self.tocore.at[chip],
            self.fromcore.at[chip],
            self.cs.at[chip],
            self.cr.at[chip],
            device_id={"t": self.zc * 2 + 1 - self.co},
            device_id_type=MESH,
        )

    def link_copy(self, chip, slot):
        return pltpu.make_async_remote_copy(
            self.toici.at[chip],
            self.fromici.at[slot],
            self.ls.at[chip],
            self.lr.at[slot],
            device_id={"t": chip * 2 + self.co},
            device_id_type=MESH,
        )

    def send_core(self, chip):
        self.core_copy(chip).start()

    def send_link(self, chip):
        self.core_copy(chip).wait_recv()
        self.toici[chip] = (self.toici[chip].astype(F32) + self.fromcore[chip].astype(F32)).astype(BF16)
        self.link_copy(chip, self.zc).start()

    def total(self):
        self.core_copy(self.zc).wait_recv()
        value = self.fromcore[self.zc].astype(F32)
        for k in range(1, self.chips):
            chip = lax.rem(self.zc + k, self.chips)
            self.link_copy(chip, chip).wait_recv()
            value = value + self.fromici[chip].astype(F32)
        return value

    def finish(self):
        for chip in range(self.chips):
            self.core_copy(chip).wait_send()
        for k in range(1, self.chips):
            chip = lax.rem(self.zc + k, self.chips)
            self.link_copy(chip, self.zc).wait_send()


def norm_stats(x):
    mean = jnp.mean(x, axis=-1, keepdims=True)
    centred = x - mean
    inverse = lax.rsqrt(jnp.mean(centred * centred, axis=-1, keepdims=True) + EPSILON)
    return centred * inverse, inverse


def widen(tab, width):
    return jnp.concatenate([tab] * (width // tab.shape[1]), axis=1)


def turn(x, cos, sa, sb, sign):
    width = x.shape[1]
    cos, sa, sb = widen(cos, width), widen(sa, width), widen(sb, width)
    side = pltpu.roll(x, width - ROT // 2, 1) * sa + pltpu.roll(x, ROT // 2, 1) * sb
    return x * cos + sign * side


def head_masks(width, dtype):
    lane = lax.broadcasted_iota(jnp.int32, (1, width), 1) // HD
    return [(lane == h).astype(F32).astype(dtype) for h in range(width // HD)]


def pair_bias(qb, kb, size, segcol, segrow):
    qpos = lax.broadcasted_iota(jnp.int32, (size, size), 0) + qb * size
    kpos = lax.broadcasted_iota(jnp.int32, (size, size), 1) + kb * size
    same = segcol[rows_of(qb, size), :] == segrow[:, rows_of(kb, size)]
    return jnp.where(same & (kpos <= qpos), 0.0, NEG_LARGE)


TILE = 256


def forward_kernel(
    tn, size,
    x_ref, wt, wi, wo, wp, vec, bt, bi, segcol, segrow, ctab, satab, sbtab,
    xo_ref, n_ref, q_ref, k_ref, v_ref, o_ref, lse_ref, g_ref, gp_ref,
    keep, tocore, fromcore, toici, fromici, ssem, fsem, rsem, cs, cr, ls, lr,
):
    chips = tn // 2
    width = q_ref.shape[1]
    heads = width // HD
    units = g_ref.shape[1]
    group_barrier(tn)
    spread = Spread(tn, n_ref, size, ssem, fsem, rsem)
    gather = Gather(tn, tocore, fromcore, toici, fromici, (cs, cr, ls, lr))
    t, zc, co = spread.t, spread.zc, spread.co
    own_n, _ = norm_stats(x_ref[...])
    n_ref[rows_of(t, size), :] = own_n.astype(BF16)
    spread.start()

    def project(b):
        rows = rows_of(b, size)
        n = n_ref[rows, :].astype(F32)
        h1 = (n * vec[0:1, :] + vec[1:2, :]).astype(BF16)
        h2 = (n * vec[2:3, :] + vec[3:4, :]).astype(BF16)
        cos, sa, sb = ctab[rows, :], satab[rows, :], sbtab[rows, :]
        q = dot(h1, wt[:, 0:width], NN) + bt[:, 0:width]
        q_ref[rows, :] = (turn(q, cos, sa, sb, 1.0).astype(BF16).astype(F32) * (1.0 / math.sqrt(HD))).astype(BF16)
        k = dot(h1, wt[:, width : 2 * width], NN) + bt[:, width : 2 * width]
        k_ref[rows, :] = turn(k, cos, sa, sb, 1.0).astype(BF16)
        v = dot(h1, wt[:, 2 * width : 3 * width], NN) + bt[:, 2 * width : 3 * width]
        v_ref[rows, :] = v.astype(BF16)

        def mix(j, carry):
            cols = rows_of(j, TILE)
            u = dot(h2, wi[:, cols], NN) + bi[:, cols]
            half = 0.5 + 0.5 * lax.erf(u * (1.0 / math.sqrt(2.0)))
            g_ref[rows, cols] = (u * half).astype(BF16)
            bell = jnp.exp(-0.5 * u * u) * (1.0 / math.sqrt(2.0 * math.pi))
            gp_ref[rows, cols] = (half + u * bell).astype(BF16)
            return carry

        lax.fori_loop(0, units // TILE, mix, 0)

    project(t)
    project(spread.peer_core())
    for i in range(1, chips):
        project(spread.same_core(i))
        project(spread.other_core(i))

    masks = head_masks(width, F32)
    lane = lax.broadcasted_iota(jnp.int32, (1, 128), 1)

    def attend(b):
        rows = rows_of(b, size)
        qb = q_ref[rows, :]
        qs = [qb * masks[h].astype(BF16) for h in range(heads)]

        def step(i, carry):
            peaks, sums, acc = carry
            kb = b - i
            keys = k_ref[rows_of(kb, size), :]
            vals = v_ref[rows_of(kb, size), :]
            bias = pair_bias(b, kb, size, segcol, segrow)
            new_peaks, new_sums = [], []
            scale = jnp.zeros((size, width), F32)
            add = jnp.zeros((size, width), F32)
            for h in range(heads):
                s = dot(qs[h], keys, NT) + bias
                peak = jnp.maximum(peaks[h], jnp.max(s, axis=1, keepdims=True))
                p = jnp.exp(s - peak)
                fade = jnp.exp(peaks[h] - peak)
                new_peaks.append(peak)
                new_sums.append(sums[h] * fade + jnp.sum(p, axis=1, keepdims=True))
                scale = scale + fade * masks[h]
                add = add + dot(p.astype(BF16), vals * masks[h].astype(BF16), NN)
            return tuple(new_peaks), tuple(new_sums), acc * scale + add

        start = (
            tuple(jnp.full((size, 1), NEG_LARGE, F32) for _ in range(heads)),
            tuple(jnp.zeros((size, 1), F32) for _ in range(heads)),
            jnp.zeros((size, width), F32),
        )
        peaks, sums, acc = lax.fori_loop(0, b + 1, step, start)
        scale = jnp.zeros((size, width), F32)
        lse = jnp.zeros((size, 128), F32)
        for h in range(heads):
            scale = scale + (1.0 / sums[h]) * masks[h]
            lse = jnp.where(lane == h, peaks[h] + jnp.log(sums[h]), lse)
        lse_ref[rows, :] = lse
        o_ref[rows, :] = acc * scale

    def partial(b, store):
        attend(b)
        rows = rows_of(b, size)

        def part(j, carry):
            cols = rows_of(j, TILE)
            store(cols, dot(g_ref[rows, :], wo[:, cols], NN) + dot(o_ref[rows, :].astype(BF16), wp[:, cols], NN))
            return carry

        lax.fori_loop(0, x_ref.shape[1] // TILE, part, 0)

    def into(ref, chip):
        def store(cols, value):
            ref[chip, :, cols] = value.astype(BF16)

        return store

    def into_keep(cols, value):
        keep[:, cols] = value

    for i in range(1, chips):
        chip = lax.rem(zc + i, chips)
        partial(chip * 2 + 1 - co, into(tocore, chip))
        gather.send_core(chip)
        partial(chip * 2 + co, into(toici, chip))
        gather.send_link(chip)
    partial(zc * 2 + 1 - co, into(tocore, zc))
    gather.send_core(zc)
    partial(t, into_keep)
    xo_ref[...] = x_ref[...] + vec[4:5, :] + keep[...] + gather.total()
    spread.finish()
    gather.finish()


def backward_kernel(
    tn, size,
    dy_ref, x_ref, wt, wi, wo, wp, vec, segcol, segrow, ctab, satab, sbtab,
    n_ref, q_ref, k_ref, v_ref, o_ref, lse_ref, g_ref, gp_ref,
    dx_ref, dwt, dwi, dwo, dwp, dvec, dbt, dbi,
    gb, do, du, dt, dq, dk, dv, dh2, keep,
    tocore, fromcore, toici, fromici, ssem, fsem, rsem, cs, cr, ls, lr,
):
    chips = tn // 2
    width = q_ref.shape[1]
    heads = width // HD
    units = g_ref.shape[1]
    model = x_ref.shape[1]
    group_barrier(tn)
    spread = Spread(tn, gb, size, ssem, fsem, rsem)
    gather = Gather(tn, tocore, fromcore, toici, fromici, (cs, cr, ls, lr))
    t, zc, co = spread.t, spread.zc, spread.co
    own = dy_ref[...].astype(F32).astype(BF16)
    gb[rows_of(t, size), :] = own
    spread.start()
    dvec[...] = jnp.zeros_like(dvec)
    dbt[...] = jnp.zeros_like(dbt)
    dbi[...] = jnp.zeros_like(dbi)
    dvec[4:5, :] = jnp.sum(own.astype(F32), axis=0, keepdims=True)
    dq[...] = jnp.zeros_like(dq)
    dk[...] = jnp.zeros_like(dk)
    dv[...] = jnp.zeros_like(dv)

    def mixer(b):
        rows = rows_of(b, size)
        grad = gb[rows, :]
        do[rows, :] = dot(grad, wp[...], NT).astype(BF16)

        def unit(j, carry):
            cols = rows_of(j, TILE)
            d = (dot(grad, wo[cols, :], NT) * gp_ref[rows, cols].astype(F32)).astype(BF16)
            du[rows, cols] = d
            dbi[0:1, cols] += jnp.sum(d.astype(F32), axis=0, keepdims=True)
            return carry

        lax.fori_loop(0, units // TILE, unit, 0)

        def back(j, carry):
            cols = rows_of(j, TILE)
            d = dot(du[rows, :], wi[cols, :], NT)
            dvec[2:3, cols] += jnp.sum(d * n_ref[rows, cols].astype(F32), axis=0, keepdims=True)
            dvec[3:4, cols] += jnp.sum(d, axis=0, keepdims=True)
            dh2[rows, cols] = d * vec[2:3, cols]
            return carry

        lax.fori_loop(0, model // TILE, back, 0)

    mixer(t)
    mixer(spread.peer_core())
    for i in range(1, chips):
        mixer(spread.same_core(i))
        mixer(spread.other_core(i))

    masks = head_masks(width, BF16)
    lane = lax.broadcasted_iota(jnp.int32, (1, 128), 1)
    up = zc >= (chips + 1) // 2
    tsize = tn

    def pair(qb, kb):
        qrows, krows = rows_of(qb, size), rows_of(kb, size)
        q, keys, vals = q_ref[qrows, :], k_ref[krows, :], v_ref[krows, :]
        grad = do[qrows, :]
        prod = grad.astype(F32) * o_ref[qrows, :]
        lse = lse_ref[qrows, :]
        bias = pair_bias(qb, kb, size, segcol, segrow)
        dq_new = jnp.zeros((size, width), F32)
        dk_new = jnp.zeros((size, width), F32)
        dv_new = jnp.zeros((size, width), F32)
        for h in range(heads):
            qh, gh = q * masks[h], grad * masks[h]
            total = jnp.sum(jnp.where(lane == h, lse, 0.0), axis=1, keepdims=True)
            delta = jnp.sum(prod * masks[h].astype(F32), axis=1, keepdims=True)
            p = jnp.exp(dot(qh, keys, NT) + bias - total)
            ds = (p * (dot(gh, vals, NT) - delta)).astype(BF16)
            dv_new = dv_new + dot(p.astype(BF16), gh, TN)
            dk_new = dk_new + dot(ds, qh, TN)
            dq_new = dq_new + dot(ds, keys * masks[h], NN)
        dq[qrows, :] += dq_new
        dk[krows, :] += dk_new
        dv[krows, :] += dv_new

    def attend_back(stage):
        pivot = jnp.where(up, stage, tsize - 1 - stage)

        def step(j, carry):
            pair(jnp.where(up, pivot + j, pivot), jnp.where(up, pivot, pivot - j))
            return carry

        lax.fori_loop(0, tsize - stage, step, 0)
        rows = rows_of(pivot, size)
        cos, sa, sb = ctab[rows, :], satab[rows, :], sbtab[rows, :]
        dt[rows, 0:width] = turn(dq[rows, :] * (1.0 / math.sqrt(HD)), cos, sa, sb, -1.0).astype(BF16)
        dt[rows, width : 2 * width] = turn(dk[rows, :], cos, sa, sb, -1.0).astype(BF16)
        dt[rows, 2 * width : 3 * width] = dv[rows, :].astype(BF16)
        block = dt[rows, :]
        dbt[...] += jnp.sum(block.astype(F32), axis=0, keepdims=True)

        def back(j, carry):
            cols = rows_of(j, TILE)
            d = dot(block, wt[cols, :], NT)
            dvec[0:1, cols] += jnp.sum(d * n_ref[rows, cols].astype(F32), axis=0, keepdims=True)
            dvec[1:2, cols] += jnp.sum(d, axis=0, keepdims=True)
            dh2[rows, cols] = dh2[rows, cols] + d * vec[0:1, cols]
            return carry

        lax.fori_loop(0, model // TILE, back, 0)
        value = dh2[rows, :]
        chip, core = pivot // 2, lax.rem(pivot, 2)

        @pl.when(core != co)
        def _():
            tocore[chip] = value.astype(BF16)
            gather.send_core(chip)

        @pl.when((core == co) & (chip != zc))
        def _():
            toici[chip] = value.astype(BF16)

        @pl.when(pivot == t)
        def _():
            keep[...] = value

        if stage % 2 == 1:

            @pl.when(chip != zc)
            def _():
                gather.send_link(chip)

    for stage in range(tn):
        attend_back(stage)

    def grad_one(j, carry):
        cols = rows_of(j, TILE)
        h1 = (n_ref[:, cols].astype(F32) * vec[0:1, cols] + vec[1:2, cols]).astype(BF16)
        dwt[cols, :] = dot(h1, dt[...], TN).astype(dwt.dtype)
        return carry

    lax.fori_loop(0, model // TILE, grad_one, 0)

    def grad_two(j, carry):
        cols = rows_of(j, TILE)
        h2 = (n_ref[:, cols].astype(F32) * vec[2:3, cols] + vec[3:4, cols]).astype(BF16)
        dwi[cols, :] = dot(h2, du[...], TN).astype(dwi.dtype)
        return carry

    lax.fori_loop(0, model // TILE, grad_two, 0)

    def grad_three(j, carry):
        cols = rows_of(j, TILE)
        dwo[cols, :] = dot(g_ref[:, cols], gb[...], TN).astype(dwo.dtype)
        return carry

    lax.fori_loop(0, units // TILE, grad_three, 0)
    small = min(TILE, width)

    def grad_four(j, carry):
        cols = rows_of(j, small)
        dwp[cols, :] = dot(o_ref[:, cols].astype(BF16), gb[...], TN).astype(dwp.dtype)
        return carry

    lax.fori_loop(0, width // small, grad_four, 0)

    own_n, inverse = norm_stats(x_ref[...])
    e = keep[...] + gather.total()
    inner = e - jnp.mean(e, axis=-1, keepdims=True) - own_n * jnp.mean(e * own_n, axis=-1, keepdims=True)
    dx_ref[...] = dy_ref[...].astype(F32) + inner * inverse
    spread.finish()
    gather.finish()


VM = pl.BlockSpec(memory_space=pltpu.VMEM)


def shape(dims, dtype):
    return jax.ShapeDtypeStruct(tuple(dims), dtype)


def group_sems(chips, tn):
    dma = pltpu.SemaphoreType.DMA
    return [dma((chips,)), dma((chips,)), dma((tn,)), dma((chips,)), dma((chips,)), dma((chips,)), dma((chips,))]


def group_buffers(chips, size, model):
    return [pltpu.VMEM((chips, size, model), BF16) for _ in range(4)]


def params_of(cid):
    return pltpu.CompilerParams(collective_id=cid, has_side_effects=True, vmem_limit_bytes=VMEM_LIMIT)


def forward_layer(tn, x, weights, vec, bt, bi, tables):
    wt, wi, wo, wp = weights
    size, model = x.shape
    length = size * tn
    width, units, chips = wp.shape[0], wo.shape[0], tn // 2
    outs = (
        shape((size, model), F32),
        shape((length, model), BF16),
        shape((length, width), BF16),
        shape((length, width), BF16),
        shape((length, width), BF16),
        shape((length, width), F32),
        shape((length, 128), F32),
        shape((length, units), BF16),
        shape((length, units), BF16),
    )
    return pl.pallas_call(
        functools.partial(forward_kernel, tn, size),
        out_shape=outs,
        in_specs=[VM] * 13,
        out_specs=[VM] * len(outs),
        scratch_shapes=[pltpu.VMEM((size, model), F32)] + group_buffers(chips, size, model) + group_sems(chips, tn),
        compiler_params=params_of(0),
        name="forward",
    )(x, wt, wi, wo, wp, vec, bt, bi, *tables)


def backward_layer(tn, dy, x, weights, vec, tables, kept):
    wt, wi, wo, wp = weights
    size, model = x.shape
    length = size * tn
    width, units, chips = wp.shape[0], wo.shape[0], tn // 2
    outs = (
        shape((size, model), F32),
        shape(wt.shape, BF16),
        shape(wi.shape, BF16),
        shape(wo.shape, BF16),
        shape(wp.shape, BF16),
        shape((8, model), F32),
        shape((1, 3 * width), F32),
        shape((1, units), F32),
    )
    return pl.pallas_call(
        functools.partial(backward_kernel, tn, size),
        out_shape=outs,
        in_specs=[VM] * 20,
        out_specs=[VM] * len(outs),
        scratch_shapes=[
            pltpu.VMEM((length, model), BF16),
            pltpu.VMEM((length, width), BF16),
            pltpu.VMEM((length, units), BF16),
            pltpu.VMEM((length, 3 * width), BF16),
            pltpu.VMEM((length, width), F32),
            pltpu.VMEM((length, width), F32),
            pltpu.VMEM((length, width), F32),
            pltpu.VMEM((length, model), F32),
            pltpu.VMEM((size, model), F32),
        ]
        + group_buffers(chips, size, model)
        + group_sems(chips, tn),
        compiler_params=params_of(1),
        name="backward",
    )(dy, x, wt, wi, wo, wp, vec, *tables, *kept)


GROUPS = ("dp", "h")
EVERY = ("dp", "h", "t")


def to_group(tn, blocks):
    h, t = lax.axis_index("h"), lax.axis_index("t")
    count = 2 * tn
    parity = lax.rem(t, 2)
    got = []
    for j in range(2):
        moves = [(c, ((c + j) % 2) * tn + c // 2) for c in range(count)]
        piece = jnp.where(lax.rem(parity + j, 2) == 0, blocks[0], blocks[1])
        got.append(lax.ppermute(piece, ("h", "t"), moves))
    low = jnp.where(h == 0, got[0], got[1])
    high = jnp.where(h == 0, got[1], got[0])
    return jnp.concatenate([low, high], axis=0)


def from_group(tn, rows):
    h, t = lax.axis_index("h"), lax.axis_index("t")
    count = 2 * tn
    parity = lax.rem(t, 2)
    size = rows.shape[0] // 2
    got = []
    for j in range(2):
        moves = [(((c + j) % 2) * tn + c // 2, c) for c in range(count)]
        piece = jnp.where(lax.rem(h + j, 2) == 0, rows[:size], rows[size:])
        got.append(lax.ppermute(piece, ("h", "t"), moves))
    first = jnp.where(parity == 0, got[0], got[1])
    second = jnp.where(parity == 0, got[1], got[0])
    return jnp.stack([first, second], axis=0)


def proj_moves(gn, tn):
    return [(r, (r % gn) * tn + r // gn) for r in range(gn * tn)]


def slice_columns(weight, gn, tn):
    rows, cols = weight.shape
    return weight.reshape(rows, gn, tn, cols // (gn * tn)).transpose(2, 0, 1, 3).reshape(tn, rows, cols // tn)


def slice_triple(weight, tn):
    rows, cols = weight.shape
    return weight.reshape(rows, 3, tn, cols // (3 * tn)).transpose(2, 0, 1, 3).reshape(tn, rows, cols // tn)


def gather_weights(gn, tn, triple, proj, inner, outer):
    def spread(parts):
        moved = lax.all_to_all(parts, "t", 0, 0, tiled=True)
        whole = lax.all_gather(moved.reshape(-1, moved.shape[-1]), GROUPS, axis=0, tiled=True)
        return whole

    wt = spread(slice_triple(triple, tn))
    wi = spread(slice_columns(inner, gn, tn))
    wo = lax.all_gather(outer, GROUPS, axis=0, tiled=True)
    wp = lax.all_gather(lax.ppermute(proj, EVERY, proj_moves(gn, tn)), GROUPS, axis=0, tiled=True)
    return wt, wi, wo, wp


def reduce_weights(gn, tn, dwt, dwi, dwo, dwp):
    def back(parts):
        mine = lax.psum_scatter(parts, GROUPS, scatter_dimension=0, tiled=True)
        rows = mine.shape[0] // tn
        return lax.all_to_all(mine.reshape(tn, rows, -1), "t", 0, 0, tiled=True).astype(F32)

    triple = back(dwt)
    rows = triple.shape[1]
    triple = triple.reshape(tn, rows, 3, -1).transpose(1, 2, 0, 3).reshape(rows, -1)
    inner = back(dwi)
    inner = inner.reshape(tn, rows, gn, -1).transpose(1, 2, 0, 3).reshape(rows, -1)
    outer = lax.psum_scatter(dwo, GROUPS, scatter_dimension=0, tiled=True).astype(F32)
    proj = lax.psum_scatter(dwp, GROUPS, scatter_dimension=0, tiled=True)
    proj = lax.ppermute(proj, EVERY, [(b, a) for a, b in proj_moves(gn, tn)]).astype(F32)
    return triple, proj, inner, outer


def per_device(
    gn, tn,
    tokens, segments, cotangent, triple_weight, triple_bias, proj_weight, proj_bias, inner_weight, inner_bias,
    outer_weight, outer_bias, first_gain, first_shift, second_gain, second_shift,
):
    layers = triple_weight.shape[0]
    model = tokens.shape[2]
    span = tokens.shape[1] * 2 * tn
    h, t = lax.axis_index("h"), lax.axis_index("t")
    device = (lax.axis_index("dp") * 2 + h) * tn + t
    shards = gn * tn
    heads_wide = model // tn
    units = outer_weight.shape[1] * gn

    x = to_group(tn, tokens).astype(F32)
    cot = to_group(tn, cotangent).astype(F32)
    segs_all = lax.all_gather(segments, ("h", "t"), axis=1, tiled=True)
    segs = jnp.where(h == 0, segs_all[0], segs_all[1])
    place = jnp.arange(span, dtype=jnp.int32)
    segs = jnp.where(segs == 0, -1 - place, segs)
    freq = 10000.0 ** (-(2.0 * jnp.arange(ROT // 2, dtype=F32)) / ROT)
    angle = place.astype(F32)[:, None] * freq[None, :]
    cosine, sine = jnp.cos(angle), jnp.sin(angle)
    none = jnp.zeros((span, HD - ROT), F32)
    empty = jnp.zeros_like(sine)
    ctab = jnp.concatenate([cosine, cosine, none + 1.0] * (128 // HD), axis=1)
    satab = jnp.concatenate([-sine, empty, none] * (128 // HD), axis=1)
    sbtab = jnp.concatenate([empty, sine, none] * (128 // HD), axis=1)
    tables = (segs[:, None], segs[None, :], ctab, satab, sbtab)

    small = (triple_bias, inner_bias, proj_bias, outer_bias, first_gain, first_shift, second_gain, second_shift)
    packed = jnp.concatenate(small, axis=1)
    packed = lax.all_gather(packed[None], EVERY, axis=0, tiled=True).astype(F32)
    starts = [0]
    for item in small:
        starts.append(starts[-1] + item.shape[1])

    def vector(layer, i):
        return packed[:, layer, starts[i] : starts[i + 1]].reshape(-1)

    weights, vecs, bts, bis = [], [], [], []
    for layer in range(layers):
        weights.append(
            gather_weights(
                gn, tn, triple_weight[layer], proj_weight[layer], inner_weight[layer], outer_weight[layer]
            )
        )
        bt = lax.dynamic_index_in_dim(vector(layer, 0).reshape(3, tn, heads_wide), t, 1, keepdims=False)
        bts.append(bt.reshape(1, -1))
        bi = lax.dynamic_index_in_dim(vector(layer, 1).reshape(gn, tn, -1), t, 1, keepdims=False)
        bis.append(bi.reshape(1, -1))
        zero = jnp.zeros((model,), F32)
        vecs.append(
            jnp.stack(
                [vector(layer, 4), vector(layer, 5), vector(layer, 6), vector(layer, 7)]
                + [vector(layer, 2) + vector(layer, 3), zero, zero, zero]
            )
        )

    inputs, kept = [], []
    for layer in range(layers):
        inputs.append(x)
        x, *saved = forward_layer(tn, x, weights[layer], vecs[layer], bts[layer], bis[layer], tables)
        kept.append(saved)
    output = from_group(tn, x.astype(BF16))
    grad = cot
    mats, flats = [None] * layers, [None] * layers
    for layer in reversed(range(layers)):
        grad, dwt, dwi, dwo, dwp, dvec, dbt, dbi = backward_layer(
            tn, grad, inputs[layer], weights[layer], vecs[layer], tables, kept[layer]
        )
        mats[layer] = reduce_weights(gn, tn, dwt, dwi, dwo, dwp)
        triple = lax.dynamic_update_slice(
            jnp.zeros((3, tn, heads_wide), F32), dbt.reshape(3, 1, heads_wide), (0, t, 0)
        )
        inner = lax.dynamic_update_slice(
            jnp.zeros((gn, tn, units // gn), F32), dbi.reshape(gn, 1, units // gn), (0, t, 0)
        )
        flats[layer] = jnp.concatenate([dvec[:5].reshape(-1), triple.reshape(-1), inner.reshape(-1)])
    tokens_grad = from_group(tn, grad.astype(BF16))
    summed = lax.psum(jnp.stack(flats), EVERY)

    def own(start, length):
        piece = length // shards
        return lax.dynamic_slice_in_dim(summed, start + device * piece, piece, 1)

    base = 5 * model
    bias_sum = own(4 * model, model)
    return (
        output,
        tokens_grad,
        jnp.stack([m[0] for m in mats]),
        own(base, 2 * model),
        own(base + 2 * model, model),
        jnp.stack([m[1] for m in mats]),
        bias_sum,
        jnp.stack([m[2] for m in mats]),
        own(base + 3 * model, units * tn),
        jnp.stack([m[3] for m in mats]),
        bias_sum,
        own(0, model),
        own(model, model),
        own(2 * model, model),
        own(3 * model, model),
    )


def solution(mesh):
    dp, ctx = mesh.shape["dp"], mesh.shape["ctx"]
    tn = ctx // 2
    gn = 2 * dp
    fine = Mesh(mesh.devices.reshape(dp, 2, tn), EVERY)
    seq = P("dp", ("h", "t"), None)
    mat = P(None, EVERY, None)
    row = P(None, EVERY)
    in_specs = (seq, P("dp", ("h", "t")), seq, mat, row, mat, row, mat, row, mat, row, row, row, row, row)
    out_specs = (seq, seq, mat, row, row, mat, row, mat, row, mat, row, row, row, row, row)
    return jax.shard_map(
        functools.partial(per_device, gn, tn), mesh=fine, in_specs=in_specs, out_specs=out_specs, check_vma=False
    )
```

time: 2730 us -> 1200 us (0.44)
  waiting for transfers between devices: 1790 us -> 642 us
  matrix products: 377 us -> 0 us
  local copies, waits for them, and re-layouts: 305 us -> 31 us
  Pallas kernels: 0 us -> 251 us
  other arithmetic: 83.1 us -> 17.8 us
  starting transfers between devices: 2.62 us -> 64.7 us
  blocking collectives: 137 us -> 167 us
    reduce_scatter x8, waiting for transfers between devices: 1330 us -> 451 us  [the longest x4 217 us: back(): mine = lax.psum_scatter(parts, GROUPS, scatter_dimension=0, tiled=True)]
    dot_general x104 -> x0, matrix products: 377 us -> none  [the longest x4 43.8 us: backward_layer(): jnp.einsum('rd,fd->rf', grad_low, outer_matrix, preferred_element_type=jn...]
    all_gather x16 -> x6, waiting for transfers between devices: 354 us -> 69.2 us  [the longest x4 54.8 us: spread(): lax.all_gather(moved.reshape(-1, moved.shape[-1]), GROUPS, axis=0, tiled=...]
    pallas_call x0 -> x4, Pallas kernels: none -> 251 us  [the longest x2 137 us: backward_layer(): pl.pallas_call(functools.partial(backward_kernel, tn, size), out_shape=ou...]
    unnamed x432 -> x65, local copies, waits for them, and re-layouts: 169 us -> 1.58 us
    psum x0 -> x1, waiting for transfers between devices: none -> 106 us  [per_device(): summed = lax.psum(jnp.stack(flats), EVERY)]
    unnamed x42 -> x15, waiting for transfers between devices: 101 us -> 4.8 us
    all_gather x4, blocking collectives: 95.4 us -> 141 us  [the longest x2 85.4 us: gather_weights(): lax.all_gather(lax.ppermute(proj, EVERY, proj_moves(gn, tn)), GROUPS, axi...]
  transfers between devices with their start and end apart: 33 -> 32, of which waited for: 24 -> 13; matrix products, arithmetic and copies ran while one was open for 25% -> 4% of each run, Pallas kernels for 0% -> 11%
where the time goes in v1:
time: 1200 us; the launch traced here: 1190 us
  waiting for transfers between devices  642 us (54%)
  Pallas kernels  251 us (21%)
  blocking collectives  167 us (14%)
  starting transfers between devices  64.7 us (5%)
  local copies, waits for them, and re-layouts  31 us (3%)
  other arithmetic  17.8 us (1%)
  between operations  15.2 us (1%)
    reduce_scatter x4, waiting for transfers between devices, back(): mine = lax.psum_scatter(parts, GROUPS, scatter_dimension=0, tiled=True)  217 us
    reduce_scatter x2, waiting for transfers between devices, reduce_weights(): lax.psum_scatter(dwo, GROUPS, scatter_dimension=0, tiled=True).astype(F32)  174 us
    pallas_call x2, Pallas kernels, backward_layer(): pl.pallas_call(functools.partial(backward_kernel, tn, size), out_shape=ou...  137 us
    pallas_call x2, Pallas kernels, forward_layer(): pl.pallas_call(functools.partial(forward_kernel, tn, size), out_shape=out...  114 us
    psum x1, waiting for transfers between devices, per_device(): summed = lax.psum(jnp.stack(flats), EVERY)  106 us
    all_gather x2, blocking collectives, gather_weights(): lax.all_gather(lax.ppermute(proj, EVERY, proj_moves(gn, tn)), GROUPS, axi...  85.4 us
    reduce_scatter x2, waiting for transfers between devices, reduce_weights(): proj = lax.psum_scatter(dwp, GROUPS, scatter_dimension=0, tiled=True)  59.2 us
    all_gather x4, waiting for transfers between devices, spread(): lax.all_gather(moved.reshape(-1, moved.shape[-1]), GROUPS, axis=0, tiled=...  54.8 us
  transfers between devices with their start and end apart: 32, of which 13 were waited for; matrix products, arithmetic and copies ran while one was open for 4% of the time, Pallas kernels for 11%

profile of v1, /device:TPU:5, one launch (start us, length us, event | category | flops | bytes accessed | tf_op | source)
XLA Modules:
  0.0 1187.8 jit_solution(10645264080671349062)
XLA Ops:
  8.8 8.3 all_to_all.40
  18.5 8.8 all_to_all.41
  27.9 8.8 all_to_all.42
  38.5 4.3 all-to-all-start.3
  42.8 5.2 all-to-all-done.3
  49.4 5.0 collective-permute-start
  58.3 6.3 collective-permute-start.3
  67.6 46.6 %all-gather.3 = bf16[32,2,416]{2,1,0:T(2,128)(2,1)S(1)} all-gather(bf16[1,2,416]{2,1,0:T(2,128)(2,1)S(1)} %bitcast.137), channel_id=3, replica_groups=mesh['dp'=4,'h'=2,'t'=4] {'dp','h','t'}, dimensions={0}, use_global_device_ids=true | all-gather | bytes 54912 | tf_op jit(solution)/shard_map/all_gather | solution.py:669
  120.1 8.8 all_gather.35
  143.2 54.7 %all_gather.33.wp = bf16[256,1024]{1,0:T(8,128)(2,1)} all-gather(bf16[32,1024]{1,0:T(8,128)(2,1)} %collective-permute-done.2), channel_id=1, replica_groups=mesh['dp'=4,'h'=2,'t'=4] {'dp','h'}, dimensions={0}, use_global_device_ids=true | all-gather | bytes 589824 | tf_op jit(solution)/shard_map/all_gather | solution.py:616
  197.8 30.8 %all_gather.39.wp = bf16[256,1024]{1,0:T(8,128)(2,1)} all-gather(bf16[32,1024]{1,0:T(8,128)(2,1)S(1)} %collective-permute-done.3), channel_id=1, replica_groups=mesh['dp'=4,'h'=2,'t'=4] {'dp','h'}, dimensions={0}, use_global_device_ids=true | all-gather | bytes 589824 | tf_op jit(solution)/shard_map/all_gather | solution.py:616
  232.8 66.1 %forward.2 = (f32[256,1024]{1,0:T(8,128)}, bf16[1024,1024]{1,0:T(8,128)(2,1)}, bf16[1024,256]{1,0:T(8,128)(2,1)}, bf16[1024,256]{1,0:T(8,128)(2,1)}, bf16[1024,2...) custom-call(f32[256,1024]{1,0:T(8,128)} %maximum_convert_fusion.x_re, ...), custom_call_target="tpu_custom_call" | custom-call | tf_op jit(solution)/shard_map/forward/pallas_call | solution.py:511
  299.0 14.3 %all-gather.21.cloned.1.call-done = bf16[1,1024,1024]{2,1,0:T(8,128)(2,1)} async-done(((bf16[1,128,1024]{2,1,0:T(8,128)(2,1)}), bf16[1,1024,1024]{2,1,0:T(8,128)(2,1)}) %all-gather.21.cloned.1.call-update) | async-done | bytes 2097168 | tf_op jit(solution)/shard_map/all_gather | solution.py:615
  313.3 54.8 %all-gather.17.cloned.1.call-done.wi = bf16[1024,1024]{1,0:T(8,128)(2,1)} async-done(((bf16[128,1024]{1,0:T(8,128)(2,1)}), bf16[1024,1024]{1,0:T(8,128)(2,1)}) %all-gather.17.cloned.1.call-update) | async-done | bytes 2097168 | tf_op jit(solution)/shard_map/all_gather | solution.py:610
  368.1 47.9 %forward.3 = (f32[256,1024]{1,0:T(8,128)}, bf16[1024,1024]{1,0:T(8,128)(2,1)}, bf16[1024,256]{1,0:T(8,128)(2,1)}, bf16[1024,256]{1,0:T(8,128)(2,1)}, bf16[1024,2...) custom-call(f32[256,1024]{1,0:T(8,128)} %get-tuple-element.49.x_ref,, ...), custom_call_target="tpu_custom_call" | custom-call | tf_op jit(solution)/shard_map/forward/pallas_call | solution.py:511
  416.0 67.5 %backward.2 = (f32[256,1024]{1,0:T(8,128)}, bf16[1024,768]{1,0:T(8,128)(2,1)}, bf16[1024,1024]{1,0:T(8,128)(2,1)}, bf16[1024,1024]{1,0:T(8,128)(2,1)}, bf16[256,...) custom-call(f32[256,1024]{1,0:T(8,128)} %maximum_convert_fusion.1.dy_ref, ...), custom_call_target="tpu_custom_call" | custom-call | tf_op jit(solution)/shard_map/backward/pallas_call | solution.py:537
  485.1 69.1 %backward.3 = (f32[256,1024]{1,0:T(8,128)}, bf16[1024,768]{1,0:T(8,128)(2,1)}, bf16[1024,1024]{1,0:T(8,128)(2,1)}, bf16[1024,1024]{1,0:T(8,128)(2,1)}, bf16[256,...) custom-call(f32[256,1024]{1,0:T(8,128)} %get-tuple-element.59.dy_ref, ...), custom_call_target="tpu_custom_call" | custom-call | tf_op jit(solution)/shard_map/backward/pallas_call | solution.py:537
  562.1 4.6 collective-permute-start.4
  568.6 3.4 all-to-all-start.5
  575.4 106.1 %all-reduce.2.cloned.1.call-done = f32[2,12288]{1,0:T(2,128)} async-done(((f32[2,12288]{1,0:T(2,128)}), f32[2,12288]{1,0:T(2,128)}) %all-reduce.2.cloned.1.call-update) | async-done | bytes 98320 | tf_op jit(solution)/shard_map/psum | solution.py:717
  684.2 53.2 %reduce-scatter.9.cloned.1.call-done = bf16[128,768]{1,0:T(8,128)(2,1)} async-done(((bf16[1024,768]{1,0:T(8,128)(2,1)}), bf16[128,768]{1,0:T(8,128)(2,1)}) %reduce-scatter.9.cloned.1.call-update) | async-done | bytes 196624 | tf_op jit(solution)/shard_map/reduce_scatter | solution.py:622
  737.4 4.2 all-to-all-start.4
  746.1 81.3 %reduce-scatter.19.cloned.1.call-done = bf16[128,1024]{1,0:T(8,128)(2,1)} async-done(((bf16[1024,1024]{1,0:T(8,128)(2,1)}), bf16[128,1024]{1,0:T(8,128)(2,1)}) %reduce-scatter.19.cloned.1.call-update) | async-done | bytes 262160 | tf_op jit(solution)/shard_map/reduce_scatter | solution.py:622
  827.4 4.2 all-to-all-start.7
  832.5 28.4 %reduce-scatter.15.cloned.1.call-done = bf16[32,1024]{1,0:T(8,128)(2,1)} async-done(((bf16[256,1024]{1,0:T(8,128)(2,1)}), bf16[32,1024]{1,0:T(8,128)(2,1)}) %reduce-scatter.15.cloned.1.call-update) | async-done | bytes 65552 | tf_op jit(solution)/shard_map/reduce_scatter | solution.py:632
  861.0 9.1 collective-permute-start.11
  870.1 30.8 %reduce-scatter.13.cloned.1.call-done = bf16[32,1024]{1,0:T(8,128)(2,1)} async-done(((bf16[256,1024]{1,0:T(8,128)(2,1)}), bf16[32,1024]{1,0:T(8,128)(2,1)}) %reduce-scatter.13.cloned.1.call-update) | async-done | bytes 65552 | tf_op jit(solution)/shard_map/reduce_scatter | solution.py:632
  900.9 8.4 collective-permute-start.10
  914.0 82.8 %reduce-scatter.17.cloned.1.call-done = bf16[128,1024]{1,0:T(8,128)(2,1)} async-done(((bf16[1024,1024]{1,0:T(8,128)(2,1)}), bf16[128,1024]{1,0:T(8,128)(2,1)}) %reduce-scatter.17.cloned.1.call-update) | async-done | bytes 262160 | tf_op jit(solution)/shard_map/reduce_scatter | solution.py:622
  996.9 4.2 all-to-all-start.6
  1002.0 84.5 %reduce-scatter.23.cloned.1.call-done = bf16[128,1024]{1,0:T(8,128)(2,1)} async-done(((bf16[1024,1024]{1,0:T(8,128)(2,1)}), bf16[128,1024]{1,0:T(8,128)(2,1)}) %reduce-scatter.23.cloned.1.call-update) | async-done | bytes 262160 | tf_op jit(solution)/shard_map/reduce_scatter | solution.py:631
  1086.5 89.7 %reduce-scatter.21.cloned.1.call-done = bf16[128,1024]{1,0:T(8,128)(2,1)} async-done(((bf16[1024,1024]{1,0:T(8,128)(2,1)}), bf16[128,1024]{1,0:T(8,128)(2,1)}) %reduce-scatter.21.cloned.1.call-update) | async-done | bytes 262160 | tf_op jit(solution)/shard_map/reduce_scatter | solution.py:631
  (220 shorter events, 70.4 us)
Async XLA Ops:
  7.2 225.6 %all-gather.11.cloned.1.call-start = ((), (), s32[]{:S(2)}) async-start(), calls=%async_computation.16 | async-start | bytes 1769472 | tf_op jit(solution)/shard_map/all_gather | solution.py:610
  17.2 215.6 %all-gather.19.cloned.1.call-start = ((), (), s32[]{:S(2)}) async-start(), calls=%async_computation.29 | async-start | bytes 2359296 | tf_op jit(solution)/shard_map/all_gather | solution.py:615
  18.1 214.7 %all-gather.13.cloned.1.call-start = ((), (), s32[]{:S(2)}) async-start(), calls=%async_computation.17 | async-start | bytes 2359296 | tf_op jit(solution)/shard_map/all_gather | solution.py:610
  27.4 271.5 %all-gather.15.cloned.1.call-start = ((), (), s32[]{:S(2)}) async-start(), calls=%async_computation.18 | async-start | bytes 1769472 | tf_op jit(solution)/shard_map/all_gather | solution.py:610
  36.8 276.5 %all-gather.21.cloned.1.call-start = ((), (), s32[]{:S(2)}) async-start(), calls=%async_computation.30 | async-start | bytes 2359296 | tf_op jit(solution)/shard_map/all_gather | solution.py:615
  38.5 9.4 all-to-all-start.3
  42.8 325.3 %all-gather.17.cloned.1.call-start = ((), (), s32[]{:S(2)}) async-start(), calls=%async_computation.19 | async-start | bytes 2359296 | tf_op jit(solution)/shard_map/all_gather | solution.py:610
  48.6 520.0 %reduce-scatter.11.cloned.1.call-start = ((), (), s32[]{:S(2)}) async-start(), calls=%async_computation.21 | async-start | bytes 1769472 | tf_op jit(solution)/shard_map/reduce_scatter | solution.py:622
  49.4 179.1 %collective-permute-start = (bf16[128,1024]{1,0:T(8,128)(2,1)}, bf16[128,1024]{1,0:T(8,128)(2,1)}, u32[]{:S(2)}, u32[]{:S(2)}) collective-permute-start(bf16[128,1024]{1,0:T(8,128)(2,1)} %get-tuple-element.113), channel_id=1, source_target_pairs={{0,0},{1,4},{2,1},{3,5},{4,2},{5,6},{6,3},{7,7},{8,8},{9,12},{10,9... | collective-permute-start | bytes 786440 | tf_op jit(solution)/shard_map/ppermute | solution.py:572
  54.4 174.2 %collective-permute-start.1 = (bf16[128,1024]{1,0:T(8,128)(2,1)S(1)}, bf16[128,1024]{1,0:T(8,128)(2,1)}, u32[]{:S(2)}, u32[]{:S(2)}) collective-permute-start(bf16[128,1024]{1,0:T(8,128)(2,1)S(1)} %get-tuple-element.114), channel_id=1, source_target_pairs={{0,4},{1,0},{2,5},{3,1},{4,6},{5,2},{6,7},{7,3},{8,12},{9,8},{10,1... | collective-permute-start | bytes 786440 | tf_op jit(solution)/shard_map/ppermute | solution.py:572
  55.2 87.8 %collective-permute-start.2 = (bf16[32,1024]{1,0:T(8,128)(2,1)}, bf16[32,1024]{1,0:T(8,128)(2,1)}, u32[]{:S(2)}, u32[]{:S(2)}) collective-permute-start(bf16[32,1024]{1,0:T(8,128)(2,1)} %get-tuple-element.118), channel_id=1, source_target_pairs={{0,0},{1,4},{2,8},{3,12},{4,16},{5,20},{6,24},{7,28},{8,1},{9,5},{... | collective-permute-start | bytes 196616 | tf_op jit(solution)/shard_map/ppermute | solution.py:616
  58.3 139.5 %collective-permute-start.3 = (bf16[32,1024]{1,0:T(8,128)(2,1)}, bf16[32,1024]{1,0:T(8,128)(2,1)S(1)}, u32[]{:S(2)}, u32[]{:S(2)}) collective-permute-start(bf16[32,1024]{1,0:T(8,128)(2,1)} %get-tuple-element.117), channel_id=1, source_target_pairs={{0,0},{1,4},{2,8},{3,12},{4,16},{5,20},{6,24},{7,28},{8,1},{9,5},{... | collective-permute-start | bytes 196616 | tf_op jit(solution)/shard_map/ppermute | solution.py:616
  65.5 165.3 %collective-permute-start.6 = (bf16[128,1024]{1,0:T(8,128)(2,1)}, bf16[128,1024]{1,0:T(8,128)(2,1)}, u32[]{:S(2)}, u32[]{:S(2)}) collective-permute-start(bf16[128,1024]{1,0:T(8,128)(2,1)} %get-tuple-element.101), channel_id=1, source_target_pairs={{0,0},{1,4},{2,1},{3,5},{4,2},{5,6},{6,3},{7,7},{8,8},{9,12},{10,9... | collective-permute-start | bytes 786440 | tf_op jit(solution)/shard_map/ppermute | solution.py:572
  143.0 87.8 %collective-permute-start.7 = (bf16[128,1024]{1,0:T(8,128)(2,1)S(1)}, bf16[128,1024]{1,0:T(8,128)(2,1)S(1)}, u32[]{:S(2)}, u32[]{:S(2)}) collective-permute-start(bf16[128,1024]{1,0:T(8,128)(2,1)S(1)} %copy-done.7), channel_id=1, source_target_pairs={{0,4},{1,0},{2,5},{3,1},{4,6},{5,2},{6,7},{7,3},{8,12},{9,8},{10,1... | collective-permute-start | bytes 786440 | tf_op jit(solution)/shard_map/ppermute | solution.py:572
  483.5 198.1 %all-reduce.2.cloned.1.call-start = ((), (), s32[]{:S(2)}) async-start(), calls=%async_computation.22 | async-start | bytes 196608 | tf_op jit(solution)/shard_map/psum | solution.py:717
  557.3 180.1 %reduce-scatter.9.cloned.1.call-start = ((), (), s32[]{:S(2)}) async-start(), calls=%async_computation.20 | async-start | bytes 1769472 | tf_op jit(solution)/shard_map/reduce_scatter | solution.py:622
  558.0 269.4 %reduce-scatter.19.cloned.1.call-start = ((), (), s32[]{:S(2)}) async-start(), calls=%async_computation.26 | async-start | bytes 2359296 | tf_op jit(solution)/shard_map/reduce_scatter | solution.py:622
  558.6 302.4 %reduce-scatter.15.cloned.1.call-start = ((), (), s32[]{:S(2)}) async-start(), calls=%async_computation.24 | async-start | bytes 589824 | tf_op jit(solution)/shard_map/reduce_scatter | solution.py:632
  559.3 341.5 %reduce-scatter.13.cloned.1.call-start = ((), (), s32[]{:S(2)}) async-start(), calls=%async_computation.23 | async-start | bytes 589824 | tf_op jit(solution)/shard_map/reduce_scatter | solution.py:632
  559.9 437.0 %reduce-scatter.17.cloned.1.call-start = ((), (), s32[]{:S(2)}) async-start(), calls=%async_computation.25 | async-start | bytes 2359296 | tf_op jit(solution)/shard_map/reduce_scatter | solution.py:622
  560.7 525.9 %reduce-scatter.23.cloned.1.call-start = ((), (), s32[]{:S(2)}) async-start(), calls=%async_computation.28 | async-start | bytes 2359296 | tf_op jit(solution)/shard_map/reduce_scatter | solution.py:631
  561.2 615.0 %reduce-scatter.21.cloned.1.call-start = ((), (), s32[]{:S(2)}) async-start(), calls=%async_computation.27 | async-start | bytes 2359296 | tf_op jit(solution)/shard_map/reduce_scatter | solution.py:631
  562.1 180.7 %collective-permute-start.4 = (bf16[128,1024]{1,0:T(8,128)(2,1)S(1)}, bf16[128,1024]{1,0:T(8,128)(2,1)S(1)}, u32[]{:S(2)}, u32[]{:S(2)}) collective-permute-start(bf16[128,1024]{1,0:T(8,128)(2,1)S(1)} %get-tuple-element.105), channel_id=1, source_target_pairs={{0,0},{4,1},{1,2},{5,3},{2,4},{6,5},{3,6},{7,7},{8,8},{12,9},{9,10... | collective-permute-start | bytes 786440 | tf_op jit(solution)/shard_map/ppermute | solution.py:587
  566.6 176.2 %collective-permute-start.5 = (bf16[128,1024]{1,0:T(8,128)(2,1)S(1)}, bf16[128,1024]{1,0:T(8,128)(2,1)S(1)}, u32[]{:S(2)}, u32[]{:S(2)}) collective-permute-start(bf16[128,1024]{1,0:T(8,128)(2,1)S(1)} %get-tuple-element.106), channel_id=1, source_target_pairs={{4,0},{0,1},{5,2},{1,3},{6,4},{2,5},{7,6},{3,7},{12,8},{8,9},{13,1... | collective-permute-start | bytes 786440 | tf_op jit(solution)/shard_map/ppermute | solution.py:587
  568.6 168.8 %all-to-all-start.5 = ((bf16[4,32,768]{2,1,0:T(8,128)(2,1)}), bf16[4,32,768]{2,1,0:T(8,128)(2,1)S(1)}, u32[]{:S(2)}, u32[]{:S(2)}) async-start(bf16[4,32,768]{2,1,0:T(8,128)(2,1)} %bitcast.119), calls=%async_computation.7 | async-start | bytes 393216 | tf_op jit(solution)/shard_map/all_to_all | solution.py:624
  572.0 259.6 %collective-permute-start.8 = (bf16[128,1024]{1,0:T(8,128)(2,1)S(1)}, bf16[128,1024]{1,0:T(8,128)(2,1)S(1)}, u32[]{:S(2)}, u32[]{:S(2)}) collective-permute-start(bf16[128,1024]{1,0:T(8,128)(2,1)S(1)} %get-tuple-element.97), channel_id=1, source_target_pairs={{0,0},{4,1},{1,2},{5,3},{2,4},{6,5},{3,6},{7,7},{8,8},{12,9},{9,10... | collective-permute-start | bytes 786440 | tf_op jit(solution)/shard_map/ppermute | solution.py:587
  575.4 256.3 %collective-permute-start.9 = (bf16[128,1024]{1,0:T(8,128)(2,1)S(1)}, bf16[128,1024]{1,0:T(8,128)(2,1)S(1)}, u32[]{:S(2)}, u32[]{:S(2)}) collective-permute-start(bf16[128,1024]{1,0:T(8,128)(2,1)S(1)} %get-tuple-element.98), channel_id=1, source_target_pairs={{4,0},{0,1},{5,2},{1,3},{6,4},{2,5},{7,6},{3,7},{12,8},{8,9},{13,1... | collective-permute-start | bytes 786440 | tf_op jit(solution)/shard_map/ppermute | solution.py:587
  737.4 8.7 all-to-all-start.4
  827.4 169.5 %all-to-all-start.7 = ((bf16[4,32,1024]{2,1,0:T(8,128)(2,1)}), bf16[4,32,1024]{2,1,0:T(8,128)(2,1)S(1)}, u32[]{:S(2)}, u32[]{:S(2)}) async-start(bf16[4,32,1024]{2,1,0:T(8,128)(2,1)} %bitcast.115), calls=%async_computation.13 | async-start | bytes 524288 | tf_op jit(solution)/shard_map/all_to_all | solution.py:624
  861.0 49.2 %collective-permute-start.11 = (bf16[32,1024]{1,0:T(8,128)(2,1)}, bf16[32,1024]{1,0:T(8,128)(2,1)S(1)}, u32[]{:S(2)}, u32[]{:S(2)}) collective-permute-start(bf16[32,1024]{1,0:T(8,128)(2,1)} %reduce-scatter.15.cloned.1.call-done), channel_id=1, source_target_pairs={{0,0},{4,1},{8,2},{12,3},{16,4},{20,5},{24,6},{28,7},{1,8},{5,9},{... | collective-permute-start | bytes 196616 | tf_op jit(solution)/shard_map/ppermute | solution.py:633
  900.9 11.6 collective-permute-start.10
  996.9 181.9 %all-to-all-start.6 = ((bf16[4,32,1024]{2,1,0:T(8,128)(2,1)}), bf16[4,32,1024]{2,1,0:T(8,128)(2,1)S(1)}, u32[]{:S(2)}, u32[]{:S(2)}) async-start(bf16[4,32,1024]{2,1,0:T(8,128)(2,1)} %bitcast.116), calls=%async_computation.11 | async-start | bytes 524288 | tf_op jit(solution)/shard_map/all_to_all | solution.py:624
  (30 other events, 1018.8 us)
Sparse Core Ops, SparseCore 0:
  17.3 61.5 all-gather.10
  81.1 54.0 all-gather.18
  137.4 71.0 all-gather.12
  210.5 47.7 all-gather.14
  260.4 52.8 all-gather.20
  315.4 52.6 all-gather.16
  483.6 52.0 reduce-scatter.10
  557.4 124.1 all-reduce.1
  685.3 52.0 reduce-scatter.8
  739.6 87.7 reduce-scatter.18
  829.7 31.2 reduce-scatter.14
  863.2 37.6 reduce-scatter.12
  903.2 93.6 reduce-scatter.16
  999.0 87.4 reduce-scatter.22
  1088.7 87.5 reduce-scatter.20

commit v2 on v1

--- a/solution.py
+++ b/solution.py
@@ -557,6 +557,636 @@
     )(dy, x, wt, wi, wo, wp, vec, *tables, *kept)
 
 
+class Place:
+    def __init__(self, gn, tn):
+        self.gn, self.tn = gn, tn
+        self.h, self.t = lax.axis_index("h"), lax.axis_index("t")
+        self.g = lax.axis_index("dp") * 2 + self.h
+        self.c = self.h * tn + self.t
+        self.bits = [1 << i for i in range(gn.bit_length() - 1)]
+
+    def group(self, g):
+        return {"dp": g // 2, "h": lax.rem(g, 2)}
+
+    def line(self, c):
+        return {"h": c // self.tn, "t": lax.rem(c, self.tn)}
+
+    def other(self, k):
+        return lax.rem(self.t + k, self.tn)
+
+
+def flip(value, bit):
+    return value + bit * (1 - 2 * lax.rem(value // bit, 2))
+
+
+def remote(src, dst, send, recv, device):
+    return pltpu.make_async_remote_copy(src, dst, send, recv, device_id=device, device_id_type=MESH)
+
+
+def runs_by_step(place, bits):
+    runs, steps = [(place.g, 1)], []
+    for bit in bits:
+        steps.append((bit, runs))
+        if len(runs) == 1 and runs[0][1] == bit:
+            runs = [(runs[0][0] // (2 * bit) * (2 * bit), 2 * bit)]
+        else:
+            runs = runs + [(flip(start, bit), count) for start, count in runs]
+    return steps
+
+
+def bit_orders(place):
+    bits = place.bits
+    return [bits, bits[:1] + bits[:0:-1]]
+
+
+class Doubling:
+    def __init__(self, place, ref, block, cols, order, sems, slot):
+        self.place, self.ref, self.block, self.cols = place, ref, block, cols
+        self.steps = runs_by_step(place, order)
+        self.send, self.recv, self.slot = sems[0], sems[1], slot
+        self.plan = []
+        index = 0
+        for bit, runs in self.steps:
+            entry = []
+            for start, count in runs:
+                entry.append((bit, start, count, index))
+                index += 1
+            self.plan.append(entry)
+
+    def copy(self, bit, start, count, index):
+        rows = pl.ds(pl.multiple_of(start * self.block, self.block), count * self.block)
+        ref = self.ref.at[rows, self.cols]
+        return remote(
+            ref,
+            ref,
+            self.send.at[self.slot, index],
+            self.recv.at[self.slot, index],
+            self.place.group(flip(self.place.g, bit)),
+        )
+
+    def begin(self, step):
+        for bit, start, count, index in self.plan[step]:
+            self.copy(bit, start, count, index).start()
+
+    def arrive(self, step):
+        for bit, start, count, index in self.plan[step]:
+            self.copy(bit, flip(start, bit), count, index).wait_recv()
+
+    def advance(self, step):
+        if step > 0:
+            self.arrive(step - 1)
+        if step < len(self.plan):
+            self.begin(step)
+
+    def finish(self):
+        for entry in self.plan:
+            for item in entry:
+                self.copy(*item).wait_send()
+
+
+def doubling_slots(place):
+    return sum(1 << i for i in range(len(place.bits)))
+
+
+def halves(cols):
+    return [pl.ds(0, cols // 2), pl.ds(cols // 2, cols // 2)]
+
+
+def line_barrier(place, extra):
+    sem = pltpu.get_barrier_semaphore()
+    span = 2 * place.tn
+    for k in range(1, span):
+        pl.semaphore_signal(sem, inc=1, device_id=place.line(lax.rem(place.c + k, span)), device_id_type=MESH)
+    for bit in place.bits[1:]:
+        pl.semaphore_signal(sem, inc=1, device_id=place.group(flip(place.g, bit)), device_id_type=MESH)
+    peers = span - 1 + len(place.bits) - 1
+    source, moved = extra
+
+    @pl.when(moved)
+    def _():
+        pl.semaphore_signal(sem, inc=1, device_id=source, device_id_type=MESH)
+        pl.semaphore_wait(sem, peers + 1)
+
+    @pl.when(jnp.logical_not(moved))
+    def _():
+        pl.semaphore_wait(sem, peers)
+
+
+def proj_places(place):
+    gn, tn = place.gn, place.tn
+    r = place.g * tn + place.t
+    target = place.group(lax.rem(r, gn)) | {"t": r // gn}
+    q = place.t * gn + place.g
+    source = place.group(q // tn) | {"t": lax.rem(q, tn)}
+    return target, source, r, q
+
+
+def open_kernel(
+    gn, tn, layers,
+    tok, cot, seg, vec, ti, outer, proj,
+    tok_o, cot_o, seg_o, vec_o, *rest,
+):
+    wts, wis, wos, wps = (rest[i * layers : (i + 1) * layers] for i in range(4))
+    (ssem, rsem, lsem, asend, arecv, psend, precv, msend, mrecv, gsend, grecv) = rest[4 * layers :]
+    place = Place(gn, tn)
+    g, t, c = place.g, place.t, place.c
+    span = 2 * tn
+    target, source, r, q = proj_places(place)
+    moved = q != r
+    line_barrier(place, (source, moved))
+    local, sends = [], []
+
+    def near(src, dst):
+        cp = pltpu.make_async_copy(src, dst, lsem.at[len(local)])
+        cp.start()
+        local.append(cp)
+
+    half = tok.shape[1]
+
+    def move(src, dst, slot):
+        for i in range(2):
+            to = i * tn + c // 2
+            rows = pl.ds(pl.multiple_of(lax.rem(c, 2) * half, half), half)
+
+            @pl.when(to == c)
+            def _():
+                pltpu.make_async_copy(src.at[i], dst.at[rows], msend.at[slot, i]).start()
+
+            @pl.when(to != c)
+            def _():
+                remote(
+                    src.at[i], dst.at[rows], msend.at[slot, i], mrecv.at[slot, lax.rem(c, 2)], place.line(to)
+                ).start()
+
+    def moved_in(src, dst, slot):
+        for i in range(2):
+            to = i * tn + c // 2
+            rows = pl.ds(pl.multiple_of(lax.rem(c, 2) * half, half), half)
+
+            @pl.when(to == c)
+            def _():
+                pltpu.make_async_copy(src.at[i], dst.at[rows], msend.at[slot, i]).wait()
+
+            @pl.when(to != c)
+            def _():
+                remote(
+                    src.at[i], dst.at[rows], msend.at[slot, i], mrecv.at[slot, lax.rem(c, 2)], place.line(to)
+                ).wait_send()
+
+        for s in range(2):
+
+            @pl.when(2 * t + s != c)
+            def _():
+                rows = pl.ds(s * half, half)
+                remote(
+                    src.at[0], dst.at[rows], msend.at[slot, 0], mrecv.at[slot, s], place.line(c)
+                ).wait_recv()
+
+    move(tok, tok_o, 0)
+
+    def slot_rows(index, size):
+        return pl.ds(pl.multiple_of(index * size, size), size)
+
+    def share(src_of, dst, slot):
+        size = src_of(0).shape[0]
+        rows = slot_rows(g * tn + t, size)
+        near(src_of(t), dst.at[rows])
+        for k in range(1, tn):
+            to = place.other(k)
+            cp = remote(
+                src_of(to), dst.at[rows], asend.at[slot, k], arecv.at[slot, t], {"t": to}
+            )
+            cp.start()
+            sends.append(cp)
+
+    def shared(dst, slot, size):
+        for k in range(1, tn):
+            frm = place.other(k)
+            ref = dst.at[slot_rows(g * tn + frm, size)]
+            remote(ref, ref, asend.at[slot, k], arecv.at[slot, frm], {"t": frm}).wait_recv()
+
+    depth = ti[0].shape[2]
+    triple_cols, inner_cols = wts[0].shape[1], wis[0].shape[1]
+    vec_rows = vec.shape[0]
+    shares = [(lambda to: vec, vec_o, vec_rows)]
+    for layer in range(layers):
+        lay = layer
+        shares.append((lambda to, lay=lay: ti[0].at[lay, to], wts[layer], depth))
+        shares.append((lambda to, lay=lay: ti[1].at[lay, to], wis[layer], depth))
+    for slot, (src_of, dst, size) in enumerate(shares):
+        share(src_of, dst, slot)
+    prows = proj.shape[1]
+    orows = outer.shape[1]
+    for layer in range(layers):
+        near(outer.at[layer], wos[layer].at[slot_rows(g, orows)])
+        src = proj.at[layer]
+
+        @pl.when(moved)
+        def _():
+            dst = wps[layer].at[slot_rows(lax.rem(r, gn), prows)]
+            remote(src, dst, psend.at[layer], precv.at[layer], target).start()
+
+        @pl.when(jnp.logical_not(moved))
+        def _():
+            pltpu.make_async_copy(src, wps[layer].at[slot_rows(g, prows)], psend.at[layer]).start()
+
+    near(seg, seg_o.at[slot_rows(c, 8)])
+    for k in range(1, span):
+        to = lax.rem(c + k, span)
+        cp = remote(seg, seg_o.at[slot_rows(c, 8)], gsend.at[k], grecv.at[c], place.line(to))
+        cp.start()
+        sends.append(cp)
+    move(cot, cot_o, 1)
+
+    sems = (ssem, rsem)
+    orders = bit_orders(place)
+    chunks, slot = [], 0
+    waits = []
+
+    def add(ref, block, ready):
+        nonlocal slot
+        parts = []
+        cols = ref.shape[1]
+        pieces = halves(cols) if cols >= 256 else [pl.ds(0, cols)]
+        for i, piece in enumerate(pieces):
+            parts.append(Doubling(place, ref, block, piece, orders[i], sems, slot))
+            slot += 1
+        chunks.append(parts)
+        waits.append(ready)
+
+    for cp in local:
+        cp.wait()
+    add(vec_o, tn * vec_rows, lambda: shared(vec_o, 0, vec_rows))
+    for layer in range(layers):
+        base = 1 + 2 * layer
+
+        def proj_ready(layer=layer):
+            ref = wps[layer].at[slot_rows(g, prows)]
+
+            @pl.when(moved)
+            def _():
+                cp = remote(ref, ref, psend.at[layer], precv.at[layer], target)
+                cp.wait_recv()
+                cp.wait_send()
+
+            @pl.when(jnp.logical_not(moved))
+            def _():
+                pltpu.make_async_copy(proj.at[layer], ref, psend.at[layer]).wait()
+
+        add(wts[layer], tn * depth, lambda base=base, layer=layer: shared(wts[layer], base, depth))
+        add(wis[layer], tn * depth, lambda base=base, layer=layer: shared(wis[layer], base + 1, depth))
+        add(wos[layer], orows, lambda: None)
+        add(wps[layer], prows, proj_ready)
+    steps = len(place.bits) + 1
+    for turn in range(len(chunks) + steps - 1):
+        for step in range(steps):
+            i = turn - step
+            if 0 <= i < len(chunks):
+                if step == 0:
+                    waits[i]()
+                for part in chunks[i]:
+                    part.advance(step)
+    for parts in chunks:
+        for part in parts:
+            part.finish()
+    for cp in sends:
+        cp.wait_send()
+    for k in range(1, span):
+        frm = lax.rem(c + k, span)
+        ref = seg_o.at[slot_rows(frm, 8)]
+        remote(ref, ref, gsend.at[k], grecv.at[frm], place.line(frm)).wait_recv()
+    moved_in(tok, tok_o, 0)
+    moved_in(cot, cot_o, 1)
+
+
+ANY = pl.BlockSpec(memory_space=pl.ANY)
+
+
+def open_call(gn, tn, tokens, cotangent, segments, vec, tri, inn, outer, proj):
+    layers = outer.shape[0]
+    _, half, model = tokens.shape
+    rows = tn * tri.shape[2]
+    dma = pltpu.SemaphoreType.DMA
+
+    def body(tok, cot, seg, vec, tri, inn, *rest):
+        open_kernel(gn, tn, layers, tok, cot, seg, vec, (tri, inn), *rest)
+
+    outs = (
+        [shape((2 * half, model), BF16)] * 2
+        + [shape((2 * tn * 8, 128), jnp.int32), shape((gn * tn * vec.shape[0], 128), BF16)]
+        + [shape((gn * rows, tri.shape[3]), BF16)] * layers
+        + [shape((gn * rows, inn.shape[3]), BF16)] * layers
+        + [shape((gn * outer.shape[1], model), BF16)] * layers
+        + [shape((gn * proj.shape[1], model), BF16)] * layers
+    )
+    slots = 1 + 8 * layers
+    return pl.pallas_call(
+        body,
+        out_shape=tuple(outs),
+        in_specs=[ANY] * 8,
+        out_specs=tuple([ANY] * len(outs)),
+        scratch_shapes=[
+            dma((slots, gn)), dma((slots, gn)), dma((2 + 3 * layers,)),
+            dma((1 + 2 * layers, tn)), dma((1 + 2 * layers, tn)),
+            dma((layers,)), dma((layers,)), dma((2, 2)), dma((2, 2)),
+            dma((2 * tn,)), dma((2 * tn,)),
+        ],
+        compiler_params=params_of(2),
+        name="opening",
+    )(tokens, cotangent, segments, vec, tri, inn, outer, proj)
+
+
+class Halving:
+    def __init__(self, place, acc, inbox, block, cols, order, sems, slot):
+        self.place, self.acc, self.inbox, self.block, self.cols = place, acc, inbox, block, cols
+        self.send, self.recv, self.slot = sems[0], sems[1], slot
+        self.plan, index, base = [], 0, 0
+        for bit, runs in reversed(runs_by_step(place, order)):
+            entry = []
+            for start, count in runs:
+                entry.append((bit, start, count, index, base))
+                index += 1
+                base += count
+            self.plan.append(entry)
+
+    def copy(self, bit, start, count, index, base):
+        rows = pl.ds(pl.multiple_of(flip(start, bit) * self.block, self.block), count * self.block)
+        return remote(
+            self.acc.at[rows, self.cols],
+            self.inbox.at[pl.ds(base * self.block, count * self.block), self.cols],
+            self.send.at[self.slot, index],
+            self.recv.at[self.slot, index],
+            self.place.group(flip(self.place.g, bit)),
+        )
+
+    def advance(self, step):
+        if step > 0:
+            for item in self.plan[step - 1]:
+                self.copy(*item).wait_recv()
+                _, start, count, _, base = item
+
+                def add(i, carry):
+                    rows = pl.ds(pl.multiple_of((start + i) * self.block, self.block), self.block)
+                    came = pl.ds(pl.multiple_of((base + i) * self.block, self.block), self.block)
+                    value = self.acc[rows, self.cols].astype(F32) + self.inbox[came, self.cols].astype(F32)
+                    self.acc[rows, self.cols] = value.astype(BF16)
+                    return carry
+
+                lax.fori_loop(0, count, add, 0)
+        if step < len(self.plan):
+            for item in self.plan[step]:
+                self.copy(*item).start()
+
+    def finish(self):
+        for entry in self.plan:
+            for item in entry:
+                self.copy(*item).wait_send()
+
+
+def close_kernel(
+    gn, tn, layers,
+    out_in, grad_in, flat, dwts, dwis, dwos, dwps,
+    out_o, grad_o, flat_o, triple_o, proj_o, inner_o, outer_o,
+    accs, boxes, cross, projbox, flatbox,
+    lsem, hs, hr, cs, cr, ps, pr, ms, mr, fs, fr,
+):
+    place = Place(gn, tn)
+    g, t, c = place.g, place.t, place.c
+    target, source, r, q = proj_places(place)
+    moved = q != r
+    loads = []
+    for i, src in enumerate(dwts + dwis + dwos + dwps):
+        cp = pltpu.make_async_copy(src, accs[i], lsem.at[i])
+        cp.start()
+        loads.append(cp)
+    line_barrier(place, (target, moved))
+    half = out_o.shape[1]
+
+    def move(src, dst, slot):
+        for s in range(2):
+            to = 2 * t + s
+
+            @pl.when(to == c)
+            def _():
+                pltpu.make_async_copy(src.at[pl.ds(s * half, half)], dst.at[place.h], ms.at[slot, s]).start()
+
+            @pl.when(to != c)
+            def _():
+                remote(
+                    src.at[pl.ds(s * half, half)], dst.at[place.h], ms.at[slot, s], mr.at[slot, place.h], place.line(to)
+                ).start()
+
+    def moved_in(src, dst, slot):
+        for s in range(2):
+            to = 2 * t + s
+
+            @pl.when(to == c)
+            def _():
+                pltpu.make_async_copy(src.at[pl.ds(s * half, half)], dst.at[place.h], ms.at[slot, s]).wait()
+
+            @pl.when(to != c)
+            def _():
+                remote(
+                    src.at[pl.ds(s * half, half)], dst.at[place.h], ms.at[slot, s], mr.at[slot, place.h], place.line(to)
+                ).wait_send()
+
+        for i in range(2):
+
+            @pl.when(i * tn + c // 2 != c)
+            def _():
+                remote(
+                    src.at[pl.ds(0, half)], dst.at[i], ms.at[slot, 0], mr.at[slot, i], place.line(c)
+                ).wait_recv()
+
+    move(grad_in, grad_o, 0)
+    move(out_in, out_o, 1)
+    orders = bit_orders(place)
+    chunks, slot = [], 0
+    plans = []
+    for layer in reversed(range(layers)):
+        for kind in range(4):
+            plans.append((kind, layer))
+    for kind, layer in plans:
+        i = kind * layers + layer
+        acc = accs[i]
+        block = acc.shape[0] // gn
+        parts = []
+        for k, cols in enumerate(halves(acc.shape[1])):
+            parts.append(Halving(place, acc, boxes[kind].at[layer], block, cols, orders[k], (hs, hr), slot))
+            slot += 1
+        chunks.append(parts)
+
+    tbits = [1 << i for i in range(tn.bit_length() - 1)]
+    exchanges = [("g", bit) for bit in place.bits] + [("t", bit) for bit in tbits]
+    flat_o[...] = flat[...]
+
+    def exchange(k):
+        kind, bit = exchanges[k]
+        to = place.group(flip(g, bit)) if kind == "g" else {"t": flip(t, bit)}
+        return remote(flatbox.at[0, k], flatbox.at[1, k], fs.at[k], fr.at[k], to)
+
+    def flat_turn(k):
+        if k > 0 and k <= len(exchanges):
+            exchange(k - 1).wait_recv()
+            flat_o[...] += flatbox[1, k - 1]
+        if k < len(exchanges):
+            flatbox[0, k] = flat_o[...]
+            exchange(k).start()
+
+    steps = len(place.bits) + 1
+
+    def cross_copy(kind, layer, to, slot_of):
+        acc = accs[kind * layers + layer]
+        rows = acc.shape[0] // (gn * tn)
+        src = acc.at[pl.ds(pl.multiple_of((g * tn + to) * rows, rows), rows)]
+        return remote(
+            src, cross[kind].at[layer, t], cs.at[kind, layer, slot_of], cr.at[kind, layer, t], {"t": to}
+        )
+
+    def proj_copy(layer):
+        acc = accs[3 * layers + layer]
+        rows = acc.shape[0] // gn
+        src = acc.at[pl.ds(pl.multiple_of(g * rows, rows), rows)]
+        return src, remote(src, projbox.at[layer], ps.at[layer], pr.at[layer], source)
+
+    def owned(kind, layer):
+        acc = accs[kind * layers + layer]
+        if kind < 2:
+            rows = acc.shape[0] // (gn * tn)
+            for k in range(1, tn):
+                cross_copy(kind, layer, place.other(k), k).start()
+            cross[kind][layer, t] = acc[pl.ds(pl.multiple_of((g * tn + t) * rows, rows), rows), :]
+        elif kind == 2:
+            rows = acc.shape[0] // gn
+            outer_o[layer] = acc[pl.ds(pl.multiple_of(g * rows, rows), rows), :].astype(F32)
+        else:
+
+            @pl.when(moved)
+            def _():
+                proj_copy(layer)[1].start()
+
+            @pl.when(jnp.logical_not(moved))
+            def _():
+                rows = acc.shape[0] // gn
+                projbox[layer] = acc[pl.ds(pl.multiple_of(g * rows, rows), rows), :]
+
+    def settle(kind, layer):
+        if kind < 2:
+            for k in range(1, tn):
+                frm = place.other(k)
+                remote(
+                    cross[kind].at[layer, frm], cross[kind].at[layer, frm], cs.at[kind, layer, k],
+                    cr.at[kind, layer, frm], {"t": frm},
+                ).wait_recv()
+            groups = 3 if kind == 0 else gn
+            out = triple_o if kind == 0 else inner_o
+            wide = cross[kind].shape[3] // groups
+            for s in range(tn):
+                for i in range(groups):
+                    at = (i * tn + s) * wide
+                    out[layer, :, at : at + wide] = cross[kind][layer, s, :, i * wide : (i + 1) * wide].astype(F32)
+        elif kind == 3:
+
+            @pl.when(moved)
+            def _():
+                proj_copy(layer)[1].wait_recv()
+
+            proj_o[layer] = projbox[layer].astype(F32)
+
+    total = len(chunks) + steps + 1
+    for turn in range(max(total, len(exchanges) + 1)):
+        if turn <= len(exchanges):
+            flat_turn(turn)
+        for step in range(steps + 2):
+            i = turn - step
+            if 0 <= i < len(chunks):
+                kind, layer = plans[i]
+                if step == 0:
+                    loads[kind * layers + layer].wait()
+                if step < steps:
+                    for part in chunks[i]:
+                        part.advance(step)
+                if step == steps - 1:
+                    owned(kind, layer)
+                if step == steps + 1:
+                    settle(kind, layer)
+    for k in range(len(exchanges)):
+        exchange(k).wait_send()
+    for (kind, layer), parts in zip(plans, chunks):
+        for part in parts:
+            part.finish()
+        if kind < 2:
+            for k in range(1, tn):
+                cross_copy(kind, layer, place.other(k), k).wait_send()
+        elif kind == 3:
+
+            @pl.when(moved)
+            def _():
+                proj_copy(layer)[1].wait_send()
+
+    moved_in(grad_in, grad_o, 0)
+    moved_in(out_in, out_o, 1)
+
+
+def close_call(gn, tn, output, grad, flat, mats):
+    layers = len(mats)
+    size, model = output.shape
+    dwts, dwis, dwos, dwps = ([m[k] for m in mats] for k in range(4))
+    dma = pltpu.SemaphoreType.DMA
+    width3, units = dwts[0].shape[1], dwis[0].shape[1]
+    shard = dwts[0].shape[0] // (gn * tn)
+    prows, orows = dwps[0].shape[0] // gn, dwos[0].shape[0] // gn
+    every = dwts + dwis + dwos + dwps
+    boxes = [
+        pltpu.VMEM((layers, (gn - 1) * m.shape[0] // gn, m.shape[1]), BF16)
+        for m in (dwts[0], dwis[0], dwos[0], dwps[0])
+    ]
+    exchanges = (gn * tn).bit_length() - 1
+
+    def body(out_in, grad_in, flat_in, *rest):
+        refs = list(rest)
+        groups = [refs[i * layers : (i + 1) * layers] for i in range(4)]
+        outs = refs[4 * layers : 4 * layers + 7]
+        rest = refs[4 * layers + 7 :]
+        accs, rest = rest[: 4 * layers], rest[4 * layers :]
+        box, rest = rest[:4], rest[4:]
+        cross, rest = rest[:2], rest[2:]
+        close_kernel(gn, tn, layers, out_in, grad_in, flat_in, *groups, *outs, accs, box, cross, *rest)
+
+    outs = (
+        shape((2, size // 2, model), BF16),
+        shape((2, size // 2, model), BF16),
+        shape(flat.shape, F32),
+        shape((layers, shard, width3 * tn), F32),
+        shape((layers, prows, model), F32),
+        shape((layers, shard, units * tn), F32),
+        shape((layers, orows, model), F32),
+    )
+    slots = 8 * layers
+    return pl.pallas_call(
+        body,
+        out_shape=outs,
+        in_specs=[ANY, ANY, VM] + [ANY] * (4 * layers),
+        out_specs=(ANY, ANY, VM, VM, VM, VM, VM),
+        scratch_shapes=[pltpu.VMEM(m.shape, BF16) for m in every]
+        + boxes
+        + [
+            pltpu.VMEM((layers, tn, shard, width3), BF16),
+            pltpu.VMEM((layers, tn, shard, units), BF16),
+            pltpu.VMEM((layers, prows, model), BF16),
+            pltpu.VMEM((2, exchanges) + flat.shape, F32),
+            dma((4 * layers,)),
+            dma((slots, gn)), dma((slots, gn)),
+            dma((2, layers, tn)), dma((2, layers, tn)),
+            dma((layers,)), dma((layers,)),
+            dma((2, 2)), dma((2, 2)),
+            dma((exchanges,)), dma((exchanges,)),
+        ],
+        compiler_params=params_of(3),
+        name="closing",
+    )(output, grad, flat, *dwts, *dwis, *dwos, *dwps)
+
+
 GROUPS = ("dp", "h")
 EVERY = ("dp", "h", "t")
 
@@ -648,9 +1278,37 @@
     heads_wide = model // tn
     units = outer_weight.shape[1] * gn
 
-    x = to_group(tn, tokens).astype(F32)
-    cot = to_group(tn, cotangent).astype(F32)
-    segs_all = lax.all_gather(segments, ("h", "t"), axis=1, tiled=True)
+    small = (triple_bias, inner_bias, proj_bias, outer_bias, first_gain, first_shift, second_gain, second_shift)
+    starts = [0]
+    for item in small:
+        starts.append(starts[-1] + item.shape[1])
+    packed = jnp.concatenate(small, axis=1)
+    rows = triple_weight.shape[1]
+    direct = rows % 16 == 0
+    if direct:
+        count = -(-packed.size // 2048) * 2048
+        vec = jnp.pad(packed.reshape(-1), (0, count - packed.size)).reshape(-1, 128)
+        opened = open_call(
+            gn, tn, tokens, cotangent, jnp.pad(segments, ((0, 6), (0, 0))), vec,
+            triple_weight.reshape(layers, rows, 3, tn, -1).transpose(0, 3, 1, 2, 4).reshape(layers, tn, rows, -1),
+            inner_weight.reshape(layers, rows, gn, tn, -1).transpose(0, 3, 1, 2, 4).reshape(layers, tn, rows, -1),
+            outer_weight, proj_weight,
+        )
+        x, cot, segs_all, vec_all = opened[0].astype(F32), opened[1].astype(F32), opened[2], opened[3]
+        weights = [tuple(opened[4 + k * layers + layer] for k in (0, 1, 2, 3)) for layer in range(layers)]
+        segs_all = segs_all.reshape(2 * tn, 8, -1)[:, :2].transpose(1, 0, 2).reshape(2, span)
+        everything = vec_all.reshape(shards, -1)[:, : packed.size].reshape((shards,) + packed.shape).astype(F32)
+    else:
+        x = to_group(tn, tokens).astype(F32)
+        cot = to_group(tn, cotangent).astype(F32)
+        segs_all = lax.all_gather(segments, ("h", "t"), axis=1, tiled=True)
+        everything = lax.all_gather(packed[None], EVERY, axis=0, tiled=True).astype(F32)
+        weights = [
+            gather_weights(
+                gn, tn, triple_weight[layer], proj_weight[layer], inner_weight[layer], outer_weight[layer]
+            )
+            for layer in range(layers)
+        ]
     segs = jnp.where(h == 0, segs_all[0], segs_all[1])
     place = jnp.arange(span, dtype=jnp.int32)
     segs = jnp.where(segs == 0, -1 - place, segs)
@@ -664,23 +1322,11 @@
     sbtab = jnp.concatenate([empty, sine, none] * (128 // HD), axis=1)
     tables = (segs[:, None], segs[None, :], ctab, satab, sbtab)
 
-    small = (triple_bias, inner_bias, proj_bias, outer_bias, first_gain, first_shift, second_gain, second_shift)
-    packed = jnp.concatenate(small, axis=1)
-    packed = lax.all_gather(packed[None], EVERY, axis=0, tiled=True).astype(F32)
-    starts = [0]
-    for item in small:
-        starts.append(starts[-1] + item.shape[1])
-
     def vector(layer, i):
-        return packed[:, layer, starts[i] : starts[i + 1]].reshape(-1)
-
-    weights, vecs, bts, bis = [], [], [], []
+        return everything[:, layer, starts[i] : starts[i + 1]].reshape(-1)
+
+    vecs, bts, bis = [], [], []
     for layer in range(layers):
-        weights.append(
-            gather_weights(
-                gn, tn, triple_weight[layer], proj_weight[layer], inner_weight[layer], outer_weight[layer]
-            )
-        )
         bt = lax.dynamic_index_in_dim(vector(layer, 0).reshape(3, tn, heads_wide), t, 1, keepdims=False)
         bts.append(bt.reshape(1, -1))
         bi = lax.dynamic_index_in_dim(vector(layer, 1).reshape(gn, tn, -1), t, 1, keepdims=False)
@@ -698,14 +1344,14 @@
         inputs.append(x)
         x, *saved = forward_layer(tn, x, weights[layer], vecs[layer], bts[layer], bis[layer], tables)
         kept.append(saved)
-    output = from_group(tn, x.astype(BF16))
+    output = x.astype(BF16)
     grad = cot
     mats, flats = [None] * layers, [None] * layers
     for layer in reversed(range(layers)):
         grad, dwt, dwi, dwo, dwp, dvec, dbt, dbi = backward_layer(
             tn, grad, inputs[layer], weights[layer], vecs[layer], tables, kept[layer]
         )
-        mats[layer] = reduce_weights(gn, tn, dwt, dwi, dwo, dwp)
+        mats[layer] = (dwt, dwi, dwo, dwp)
         triple = lax.dynamic_update_slice(
             jnp.zeros((3, tn, heads_wide), F32), dbt.reshape(3, 1, heads_wide), (0, t, 0)
         )
@@ -713,8 +1359,18 @@
             jnp.zeros((gn, tn, units // gn), F32), dbi.reshape(gn, 1, units // gn), (0, t, 0)
         )
         flats[layer] = jnp.concatenate([dvec[:5].reshape(-1), triple.reshape(-1), inner.reshape(-1)])
-    tokens_grad = from_group(tn, grad.astype(BF16))
-    summed = lax.psum(jnp.stack(flats), EVERY)
+    tokens_grad = grad.astype(BF16)
+    flat = jnp.stack(flats)
+    if direct:
+        output, tokens_grad, summed, triple, proj, inner, outer = close_call(
+            gn, tn, output, tokens_grad, flat.reshape(-1, 1024), mats
+        )
+        summed = summed.reshape(flat.shape)
+    else:
+        output, tokens_grad = from_group(tn, output), from_group(tn, tokens_grad)
+        done = [reduce_weights(gn, tn, *m) for m in mats]
+        triple, proj, inner, outer = (jnp.stack([m[k] for m in done]) for k in range(4))
+        summed = lax.psum(flat, EVERY)
 
     def own(start, length):
         piece = length // shards
@@ -725,14 +1381,14 @@
     return (
         output,
         tokens_grad,
-        jnp.stack([m[0] for m in mats]),
+        triple,
         own(base, 2 * model),
         own(base + 2 * model, model),
-        jnp.stack([m[1] for m in mats]),
+        proj,
         bias_sum,
-        jnp.stack([m[2] for m in mats]),
+        inner,
         own(base + 3 * model, units * tn),
-        jnp.stack([m[3] for m in mats]),
+        outer,
         bias_sum,
         own(0, model),
         own(model, model),

time: 1200 us -> 607 us (0.51)
  waiting for transfers between devices: 642 us -> 0 us
  Pallas kernels: 251 us -> 559 us
  blocking collectives: 167 us -> 0 us
  starting transfers between devices: 64.7 us -> 0 us
  between operations: 15.2 us -> 1.21 us
    reduce_scatter x8 -> x0, waiting for transfers between devices: 451 us -> none  [the longest x4 217 us: back(): mine = lax.psum_scatter(parts, GROUPS, scatter_dimension=0, tiled=True)]
    pallas_call x0 -> x2, Pallas kernels: none -> 315 us  [the longest x1 159 us: open_call(): pl.pallas_call(body, out_shape=tuple(outs), in_specs=[ANY] * 8, out_specs...]
    all_gather x4 -> x0, blocking collectives: 141 us -> none  [the longest x2 85.4 us: gather_weights(): lax.all_gather(lax.ppermute(proj, EVERY, proj_moves(gn, tn)), GROUPS, axi...]
    psum x1 -> x0, waiting for transfers between devices: 106 us -> none  [per_device(): summed = lax.psum(jnp.stack(flats), EVERY)]
    all_gather x6 -> x0, waiting for transfers between devices: 69.2 us -> none  [the longest x4 54.8 us: spread(): lax.all_gather(moved.reshape(-1, moved.shape[-1]), GROUPS, axis=0, tiled=...]
    ppermute x12 -> x0, starting transfers between devices: 43.9 us -> none  [the longest x2 17.5 us: reduce_weights(): lax.ppermute(proj, EVERY, [(b, a) for a, b in proj_moves(gn, tn)])]
    all_to_all x3 -> x0, blocking collectives: 26 us -> none  [spread(): moved = lax.all_to_all(parts, 't', 0, 0, tiled=True)]
    all_to_all x5 -> x0, starting transfers between devices: 20.3 us -> none  [the longest x4 16 us: back(): lax.all_to_all(mine.reshape(tn, rows, -1), 't', 0, 0, tiled=True)]
  transfers between devices with their start and end apart: 32 -> 0, of which waited for: 13 -> 0; matrix products, arithmetic and copies ran while one was open for 4% -> 0% of each run, Pallas kernels for 11% -> 0%
where the time goes in v2:
time: 607 us; the launch traced here: 603 us
  Pallas kernels  559 us (92%)
  local copies, waits for them, and re-layouts  32.1 us (5%)
  other arithmetic  11.4 us (2%)
    pallas_call x1, Pallas kernels, open_call(): pl.pallas_call(body, out_shape=tuple(outs), in_specs=[ANY] * 8, out_specs...  159 us
    pallas_call x1, Pallas kernels, close_call(): pl.pallas_call(body, out_shape=outs, in_specs=[ANY, ANY, VM] + [ANY] * (4...  156 us
    pallas_call x2, Pallas kernels, backward_layer(): pl.pallas_call(functools.partial(backward_kernel, tn, size), out_shape=ou...  132 us
    pallas_call x2, Pallas kernels, forward_layer(): pl.pallas_call(functools.partial(forward_kernel, tn, size), out_shape=out...  111 us

profile of v2, /device:TPU:5, one launch (start us, length us, event | category | flops | bytes accessed | tf_op | source)
XLA Modules:
  0.0 603.4 jit_solution(2960860315204196735)
XLA Ops:
  0.7 1.3 pad.8.seg
  2.0 0.9 concatenate.18
  3.5 1.3 reshape.227
  5.0 1.2 reshape.228.tri
  6.7 1.0 reshape.230.inn
  7.7 159.4 %opening.1 = (bf16[256,1024]{1,0:T(8,128)(2,1)}, bf16[256,1024]{1,0:T(8,128)(2,1)}, s32[64,128]{1,0:T(8,128)}, bf16[512,128]{1,0:T(8,128)(2,1)}, bf16[1024,768]{...) custom-call(bf16[2,128,1024]{2,1,0:T(8,128)(2,1)} %tok.1, ...), custom_call_target="tpu_custom_call" | custom-call | tf_op jit(solution)/shard_map/opening/pallas_call | solution.py:883
  167.1 2.1 convert_element_type.41.x_ref
  169.2 1.0 reshape.231
  173.6 0.8 slice.99
  174.6 0.9 compare_select_fusion.segcol
  176.1 1.9 multiply_sine_fusion
  178.0 1.7 concatenate.19.ctab
  179.9 1.7 concatenate.20.satab
  181.6 1.7 concatenate.21.sbtab
  183.4 48.3 %forward.2 = (f32[256,1024]{1,0:T(8,128)}, bf16[1024,1024]{1,0:T(8,128)(2,1)}, bf16[1024,256]{1,0:T(8,128)(2,1)}, bf16[1024,256]{1,0:T(8,128)(2,1)}, bf16[1024,2...) custom-call(f32[256,1024]{1,0:T(8,128)} %convert_element_type.41.x_r, ...), custom_call_target="tpu_custom_call" | custom-call | tf_op jit(solution)/shard_map/forward/pallas_call | solution.py:511
  232.7 63.1 %forward.3 = (f32[256,1024]{1,0:T(8,128)}, bf16[1024,1024]{1,0:T(8,128)(2,1)}, bf16[1024,256]{1,0:T(8,128)(2,1)}, bf16[1024,256]{1,0:T(8,128)(2,1)}, bf16[1024,2...) custom-call(f32[256,1024]{1,0:T(8,128)} %get-tuple-element.75.x_ref,, ...), custom_call_target="tpu_custom_call" | custom-call | tf_op jit(solution)/shard_map/forward/pallas_call | solution.py:511
  295.8 2.1 convert_element_type.45.out_in
  297.9 1.1 convert_element_type.46.dy_ref
  299.0 67.2 %backward.2 = (f32[256,1024]{1,0:T(8,128)}, bf16[1024,768]{1,0:T(8,128)(2,1)}, bf16[1024,1024]{1,0:T(8,128)(2,1)}, bf16[1024,1024]{1,0:T(8,128)(2,1)}, bf16[256,...) custom-call(f32[256,1024]{1,0:T(8,128)} %convert_element_type.46.dy_ref, ...), custom_call_target="tpu_custom_call" | custom-call | tf_op jit(solution)/shard_map/backward/pallas_call | solution.py:537
  366.3 64.6 %backward.3 = (f32[256,1024]{1,0:T(8,128)}, bf16[1024,768]{1,0:T(8,128)(2,1)}, bf16[1024,1024]{1,0:T(8,128)(2,1)}, bf16[1024,1024]{1,0:T(8,128)(2,1)}, bf16[256,...) custom-call(f32[256,1024]{1,0:T(8,128)} %get-tuple-element.90.dy_ref, ...), custom_call_target="tpu_custom_call" | custom-call | tf_op jit(solution)/shard_map/backward/pallas_call | solution.py:537
  430.9 2.1 convert_element_type.47.grad_in
  433.2 0.7 dynamic_update_slice.13
  433.9 0.7 dynamic_update_slice.12
  434.6 0.8 reshape.237
  435.5 0.7 reshape.247.flat_in
  436.2 156.1 %closing.1 = (bf16[2,128,1024]{2,1,0:T(8,128)(2,1)}, bf16[2,128,1024]{2,1,0:T(8,128)(2,1)}, f32[24,1024]{1,0:T(8,128)}, f32[2,32,3072]{2,1,0:T(8,128)}, f32[2,32...) custom-call(bf16[256,1024]{1,0:T(8,128)(2,1)} %convert_element_type.45.out_in, ...), custom_call_target="tpu_custom_call" | custom-call | tf_op jit(solution)/shard_map/closing/pallas_call | solution.py:1166
  592.3 1.1 reshape.248
  595.8 2.0 copy.89
  597.8 1.9 copy.90
  599.6 0.9 copy.91
  601.2 1.0 copy.93
  602.2 1.0 copy.94
  (74 shorter events, 10.1 us)
Async XLA Ops:
  0.6 5.6 copy-start.4
  232.7 65.2 %copy-start.3 = (bf16[256,1024]{1,0:T(8,128)(2,1)S(1)}, bf16[256,1024]{1,0:T(8,128)(2,1)}, u32[]{:S(2)}) copy-start(bf16[256,1024]{1,0:T(8,128)(2,1)} %get-tuple-element.81) | copy-start | bytes 1572868
  366.2 66.7 %copy-start.7 = (f32[1,1024]{1,0:T(1,128)S(1)}, f32[1,1024]{1,0:T(1,128)}, u32[]{:S(2)}) copy-start(f32[1,1024]{1,0:T(1,128)} %get-tuple-element.105) | copy-start | bytes 12292
  366.2 66.8 %copy-start.9 = (f32[1,768]{1,0:T(1,128)S(1)}, f32[1,768]{1,0:T(1,128)}, u32[]{:S(2)}) copy-start(f32[1,768]{1,0:T(1,128)} %get-tuple-element.104) | copy-start | bytes 9220
  366.2 66.9 %copy-start.6 = (f32[8,1024]{1,0:T(8,128)S(1)}, f32[8,1024]{1,0:T(8,128)}, u32[]{:S(2)}) copy-start(f32[8,1024]{1,0:T(8,128)} %get-tuple-element.103) | copy-start | bytes 98308
  592.3 7.3 %copy-start.2 = (f32[2,32,3072]{2,1,0:T(8,128)S(1)}, f32[2,32,3072]{2,1,0:T(8,128)}, u32[]{:S(2)}) copy-start(f32[2,32,3072]{2,1,0:T(8,128)} %get-tuple-element.195) | copy-start | bytes 2359300
  592.3 8.2 %copy-start.5 = (f32[2,32,1024]{2,1,0:T(8,128)S(1)}, f32[2,32,1024]{2,1,0:T(8,128)}, u32[]{:S(2)}) copy-start(f32[2,32,1024]{2,1,0:T(8,128)} %get-tuple-element.198) | copy-start | bytes 786436
  594.7 6.5 %copy-start.8 = (f32[2,32]{1,0:T(2,128)}, f32[2,32]{1,0:T(2,128)S(1)}, u32[]{:S(2)}) copy-start(f32[2,32]{1,0:T(2,128)S(1)} %get-tuple-element.199) | copy-start | bytes 772
  595.8 5.4 copy-start.1
  599.6 2.6 copy-start

commit v3 on v2

--- a/solution.py
+++ b/solution.py
@@ -3,6 +3,7 @@
 
 import jax
 import jax.numpy as jnp
+import numpy as np
 from jax import lax
 from jax.experimental import pallas as pl
 from jax.experimental.pallas import tpu as pltpu
@@ -171,70 +172,67 @@
 
 
 TILE = 256
-
-
-def forward_kernel(
-    tn, size,
-    x_ref, wt, wi, wo, wp, vec, bt, bi, segcol, segrow, ctab, satab, sbtab,
-    xo_ref, n_ref, q_ref, k_ref, v_ref, o_ref, lse_ref, g_ref, gp_ref,
-    keep, tocore, fromcore, toici, fromici, ssem, fsem, rsem, cs, cr, ls, lr,
-):
-    chips = tn // 2
-    width = q_ref.shape[1]
-    heads = width // HD
-    units = g_ref.shape[1]
-    group_barrier(tn)
-    spread = Spread(tn, n_ref, size, ssem, fsem, rsem)
-    gather = Gather(tn, tocore, fromcore, toici, fromici, (cs, cr, ls, lr))
-    t, zc, co = spread.t, spread.zc, spread.co
-    own_n, _ = norm_stats(x_ref[...])
-    n_ref[rows_of(t, size), :] = own_n.astype(BF16)
-    spread.start()
-
-    def project(b):
-        rows = rows_of(b, size)
-        n = n_ref[rows, :].astype(F32)
-        h1 = (n * vec[0:1, :] + vec[1:2, :]).astype(BF16)
-        h2 = (n * vec[2:3, :] + vec[3:4, :]).astype(BF16)
-        cos, sa, sb = ctab[rows, :], satab[rows, :], sbtab[rows, :]
-        q = dot(h1, wt[:, 0:width], NN) + bt[:, 0:width]
-        q_ref[rows, :] = (turn(q, cos, sa, sb, 1.0).astype(BF16).astype(F32) * (1.0 / math.sqrt(HD))).astype(BF16)
-        k = dot(h1, wt[:, width : 2 * width], NN) + bt[:, width : 2 * width]
-        k_ref[rows, :] = turn(k, cos, sa, sb, 1.0).astype(BF16)
-        v = dot(h1, wt[:, 2 * width : 3 * width], NN) + bt[:, 2 * width : 3 * width]
-        v_ref[rows, :] = v.astype(BF16)
+SKEW = 1
+
+
+class Forward:
+    def __init__(self, tn, size, x, w, vecs, segs, tables, kept, keep):
+        self.tn, self.size, self.chips = tn, size, tn // 2
+        self.x, self.keep = x, keep
+        self.wt, self.wi, self.wo, self.wp = w
+        self.vec, self.bt, self.bi = vecs
+        self.segcol, self.segrow = segs
+        self.tables = tables
+        self.n, self.q, self.k, self.v, self.o, self.lse, self.g, self.gp = kept
+        self.width, self.units = self.q.shape[1], self.g.shape[1]
+        self.heads = self.width // HD
+
+    def norm(self, t):
+        own, _ = norm_stats(self.x[...])
+        self.n[rows_of(t, self.size), :] = own.astype(BF16)
+
+    def heads_in(self, b):
+        width, vec, bt = self.width, self.vec, self.bt
+        rows = rows_of(b, self.size)
+        h1 = (self.n[rows, :].astype(F32) * vec[0:1, :] + vec[1:2, :]).astype(BF16)
+        cos, sa, sb = (tab[rows, :] for tab in self.tables)
+        q = dot(h1, self.wt[:, 0:width], NN) + bt[:, 0:width]
+        low = turn(q, cos, sa, sb, 1.0).astype(BF16).astype(F32)
+        self.q[rows, :] = (low * (1.0 / math.sqrt(HD))).astype(BF16)
+        k = dot(h1, self.wt[:, width : 2 * width], NN) + bt[:, width : 2 * width]
+        self.k[rows, :] = turn(k, cos, sa, sb, 1.0).astype(BF16)
+        v = dot(h1, self.wt[:, 2 * width : 3 * width], NN) + bt[:, 2 * width : 3 * width]
+        self.v[rows, :] = v.astype(BF16)
+
+    def mixer_in(self, b):
+        rows = rows_of(b, self.size)
+        h2 = (self.n[rows, :].astype(F32) * self.vec[2:3, :] + self.vec[3:4, :]).astype(BF16)
 
         def mix(j, carry):
             cols = rows_of(j, TILE)
-            u = dot(h2, wi[:, cols], NN) + bi[:, cols]
+            u = dot(h2, self.wi[:, cols], NN) + self.bi[:, cols]
             half = 0.5 + 0.5 * lax.erf(u * (1.0 / math.sqrt(2.0)))
-            g_ref[rows, cols] = (u * half).astype(BF16)
+            self.g[rows, cols] = (u * half).astype(BF16)
             bell = jnp.exp(-0.5 * u * u) * (1.0 / math.sqrt(2.0 * math.pi))
-            gp_ref[rows, cols] = (half + u * bell).astype(BF16)
+            self.gp[rows, cols] = (half + u * bell).astype(BF16)
             return carry
 
-        lax.fori_loop(0, units // TILE, mix, 0)
-
-    project(t)
-    project(spread.peer_core())
-    for i in range(1, chips):
-        project(spread.same_core(i))
-        project(spread.other_core(i))
-
-    masks = head_masks(width, F32)
-    lane = lax.broadcasted_iota(jnp.int32, (1, 128), 1)
-
-    def attend(b):
+        lax.fori_loop(0, self.units // TILE, mix, 0)
+
+    def attend(self, b):
+        size, width, heads = self.size, self.width, self.heads
+        masks = head_masks(width, F32)
+        lane = lax.broadcasted_iota(jnp.int32, (1, 128), 1)
         rows = rows_of(b, size)
-        qb = q_ref[rows, :]
+        qb = self.q[rows, :]
         qs = [qb * masks[h].astype(BF16) for h in range(heads)]
 
         def step(i, carry):
             peaks, sums, acc = carry
             kb = b - i
-            keys = k_ref[rows_of(kb, size), :]
-            vals = v_ref[rows_of(kb, size), :]
-            bias = pair_bias(b, kb, size, segcol, segrow)
+            keys = self.k[rows_of(kb, size), :]
+            vals = self.v[rows_of(kb, size), :]
+            bias = pair_bias(b, kb, size, self.segcol, self.segrow)
             new_peaks, new_sums = [], []
             scale = jnp.zeros((size, width), F32)
             add = jnp.zeros((size, width), F32)
@@ -260,38 +258,81 @@
         for h in range(heads):
             scale = scale + (1.0 / sums[h]) * masks[h]
             lse = jnp.where(lane == h, peaks[h] + jnp.log(sums[h]), lse)
-        lse_ref[rows, :] = lse
-        o_ref[rows, :] = acc * scale
-
-    def partial(b, store):
-        attend(b)
-        rows = rows_of(b, size)
+        self.lse[rows, :] = lse
+        self.o[rows, :] = acc * scale
+
+    def branches(self, b, store):
+        rows = rows_of(b, self.size)
 
         def part(j, carry):
             cols = rows_of(j, TILE)
-            store(cols, dot(g_ref[rows, :], wo[:, cols], NN) + dot(o_ref[rows, :].astype(BF16), wp[:, cols], NN))
+            value = dot(self.g[rows, :], self.wo[:, cols], NN)
+            store(cols, value + dot(self.o[rows, :].astype(BF16), self.wp[:, cols], NN))
             return carry
 
-        lax.fori_loop(0, x_ref.shape[1] // TILE, part, 0)
-
-    def into(ref, chip):
+        lax.fori_loop(0, self.x.shape[1] // TILE, part, 0)
+
+    def into(self, ref, chip):
         def store(cols, value):
             ref[chip, :, cols] = value.astype(BF16)
 
         return store
 
-    def into_keep(cols, value):
-        keep[:, cols] = value
-
-    for i in range(1, chips):
-        chip = lax.rem(zc + i, chips)
-        partial(chip * 2 + 1 - co, into(tocore, chip))
+    def into_keep(self, cols, value):
+        self.keep[:, cols] = value
+
+
+def arrivals(spread):
+    yield spread.t
+    yield spread.peer_core()
+    for i in range(1, spread.chips):
+        yield spread.same_core(i)
+        yield spread.other_core(i)
+
+
+def far_first(spread):
+    out = []
+    for i in range(1, spread.chips):
+        chip = lax.rem(spread.zc + i, spread.chips)
+        out += [chip * 2 + 1 - spread.co, chip * 2 + spread.co]
+    return out + [spread.zc * 2 + 1 - spread.co, spread.t]
+
+
+def branch_sums(layer, spread, gather, tick=lambda: None):
+    for i in range(1, spread.chips):
+        chip = lax.rem(spread.zc + i, spread.chips)
+        layer.branches(chip * 2 + 1 - spread.co, layer.into(gather.tocore, chip))
         gather.send_core(chip)
-        partial(chip * 2 + co, into(toici, chip))
+        layer.branches(chip * 2 + spread.co, layer.into(gather.toici, chip))
         gather.send_link(chip)
-    partial(zc * 2 + 1 - co, into(tocore, zc))
-    gather.send_core(zc)
-    partial(t, into_keep)
+        tick()
+    layer.branches(spread.zc * 2 + 1 - spread.co, layer.into(gather.tocore, spread.zc))
+    gather.send_core(spread.zc)
+    layer.branches(spread.t, layer.into_keep)
+    tick()
+
+
+def forward_kernel(
+    tn, size,
+    x_ref, wt, wi, wo, wp, vec, bt, bi, segcol, segrow, ctab, satab, sbtab,
+    xo_ref, n_ref, q_ref, k_ref, v_ref, o_ref, lse_ref, g_ref, gp_ref,
+    keep, tocore, fromcore, toici, fromici, ssem, fsem, rsem, cs, cr, ls, lr,
+):
+    group_barrier(tn)
+    spread = Spread(tn, n_ref, size, ssem, fsem, rsem)
+    gather = Gather(tn, tocore, fromcore, toici, fromici, (cs, cr, ls, lr))
+    layer = Forward(
+        tn, size, x_ref, (wt, wi, wo, wp), (vec, bt, bi), (segcol, segrow), (ctab, satab, sbtab),
+        (n_ref, q_ref, k_ref, v_ref, o_ref, lse_ref, g_ref, gp_ref), keep,
+    )
+    layer.norm(spread.t)
+    spread.start()
+    for b in arrivals(spread):
+        layer.heads_in(b)
+        layer.mixer_in(b)
+    for b in far_first(spread):
+        layer.attend(b)
+    branch_sums(layer, spread, gather)
     xo_ref[...] = x_ref[...] + vec[4:5, :] + keep[...] + gather.total()
     spread.finish()
     gather.finish()
@@ -601,21 +642,25 @@
 
 class Doubling:
     def __init__(self, place, ref, block, cols, order, sems, slot):
-        self.place, self.ref, self.block, self.cols = place, ref, block, cols
-        self.steps = runs_by_step(place, order)
+        self.place, self.ref, self.block, self.cols, self.order = place, ref, block, cols, order
         self.send, self.recv, self.slot = sems[0], sems[1], slot
-        self.plan = []
-        index = 0
-        for bit, runs in self.steps:
-            entry = []
-            for start, count in runs:
-                entry.append((bit, start, count, index))
-                index += 1
-            self.plan.append(entry)
-
-    def copy(self, bit, start, count, index):
-        rows = pl.ds(pl.multiple_of(start * self.block, self.block), count * self.block)
+        self.levels = [[] for _ in order]
+        for i, bit in enumerate(order):
+            for bits in range(1 << i):
+                held = [order[j] for j in range(i) if bits >> j & 1]
+                self.levels[len(held)].append((bit, held))
+
+    def at(self, held):
+        g = self.place.g
+        for bit in held:
+            g = flip(g, bit)
+        return g
+
+    def copy(self, bit, held):
+        start = self.at(held)
+        rows = pl.ds(pl.multiple_of(start * self.block, self.block), self.block)
         ref = self.ref.at[rows, self.cols]
+        index = sum(held) + bit
         return remote(
             ref,
             ref,
@@ -624,28 +669,33 @@
             self.place.group(flip(self.place.g, bit)),
         )
 
-    def begin(self, step):
-        for bit, start, count, index in self.plan[step]:
-            self.copy(bit, start, count, index).start()
-
-    def arrive(self, step):
-        for bit, start, count, index in self.plan[step]:
-            self.copy(bit, flip(start, bit), count, index).wait_recv()
-
-    def advance(self, step):
-        if step > 0:
-            self.arrive(step - 1)
-        if step < len(self.plan):
-            self.begin(step)
+    def arrive(self, held):
+        start = self.at(held)
+        rows = pl.ds(pl.multiple_of(start * self.block, self.block), self.block)
+        ref = self.ref.at[rows, self.cols]
+        index = sum(held)
+        peer = self.place.group(flip(self.place.g, held[-1]))
+        remote(ref, ref, self.send.at[self.slot, index], self.recv.at[self.slot, index], peer).wait_recv()
+
+    def advance(self, level):
+        seen = set()
+        for bit, held in self.levels[level]:
+            if held and tuple(held) not in seen:
+                seen.add(tuple(held))
+                self.arrive(held)
+            self.copy(bit, held).start()
+
+    def whole(self):
+        last = self.order[-1]
+        for level in self.levels:
+            for bit, held in level:
+                if bit == last:
+                    self.arrive(held + [bit])
 
     def finish(self):
-        for entry in self.plan:
-            for item in entry:
+        for level in self.levels:
+            for item in level:
                 self.copy(*item).wait_send()
-
-
-def doubling_slots(place):
-    return sum(1 << i for i in range(len(place.bits)))
 
 
 def halves(cols):
@@ -681,219 +731,447 @@
     return target, source, r, q
 
 
-def open_kernel(
-    gn, tn, layers,
-    tok, cot, seg, vec, ti, outer, proj,
-    tok_o, cot_o, seg_o, vec_o, *rest,
+def slot_rows(index, size):
+    return pl.ds(pl.multiple_of(index * size, size), size)
+
+
+class Opening:
+    def __init__(self, place, layers, tok, cot, seg, vec, tri, inn, outer, proj, tok_o, cot_o, seg_o, vec_o, w, sems):
+        self.place, self.layers = place, layers
+        self.tok, self.cot, self.seg, self.vec = tok, cot, seg, vec
+        self.tri, self.inn, self.outer, self.proj = tri, inn, outer, proj
+        self.tok_o, self.cot_o, self.seg_o, self.vec_o = tok_o, cot_o, seg_o, vec_o
+        self.wts, self.wis, self.wos, self.wps = w
+        (
+            self.ssem, self.rsem, self.lsem, self.asend, self.arecv, self.psend, self.precv,
+            self.msend, self.mrecv, self.gsend, self.grecv,
+        ) = sems
+        self.half = tok.shape[1]
+        self.target, self.source, self.r, self.q = proj_places(place)
+        self.moved = self.q != self.r
+        self.local, self.sends, self.shared_with = [], [], {}
+        self.locals_of = {}
+
+    def barrier(self):
+        line_barrier(self.place, (self.source, self.moved))
+
+    def near(self, src, dst, key):
+        cp = pltpu.make_async_copy(src, dst, self.lsem.at[len(self.local)])
+        cp.start()
+        self.local.append(cp)
+        self.locals_of[key] = cp
+
+    def hop(self, src, dst, slot, i):
+        c, tn = self.place.c, self.place.tn
+        to = i * tn + c // 2
+        rows = slot_rows(lax.rem(c, 2), self.half)
+        near = pltpu.make_async_copy(src.at[i], dst.at[rows], self.msend.at[slot, i])
+        far = remote(
+            src.at[i], dst.at[rows], self.msend.at[slot, i], self.mrecv.at[slot, lax.rem(c, 2)],
+            self.place.line(to),
+        )
+        return to == c, near, far
+
+    def move(self, src, dst, slot):
+        for i in range(2):
+            stays, near, far = self.hop(src, dst, slot, i)
+            pl.when(stays)(near.start)
+            pl.when(jnp.logical_not(stays))(far.start)
+
+    def moved_in(self, src, dst, slot):
+        for i in range(2):
+            stays, near, far = self.hop(src, dst, slot, i)
+            pl.when(stays)(near.wait)
+            pl.when(jnp.logical_not(stays))(far.wait_send)
+        for s in range(2):
+            cp = remote(
+                src.at[0], dst.at[pl.ds(s * self.half, self.half)], self.msend.at[slot, 0],
+                self.mrecv.at[slot, s], self.place.line(self.place.c),
+            )
+            pl.when(2 * self.place.t + s != self.place.c)(cp.wait_recv)
+
+    def share(self, key, src_of, dst, size, slot):
+        g, t, tn = self.place.g, self.place.t, self.place.tn
+        rows = slot_rows(g * tn + t, size)
+        self.near(src_of(t), dst.at[rows], key)
+        for k in range(1, tn):
+            to = self.place.other(k)
+            cp = remote(src_of(to), dst.at[rows], self.asend.at[slot, k], self.arecv.at[slot, t], {"t": to})
+            cp.start()
+            self.sends.append(cp)
+        self.shared_with[key] = (dst, size, slot)
+
+    def shared(self, key):
+        dst, size, slot = self.shared_with[key]
+        self.locals_of[key].wait()
+        for k in range(1, self.place.tn):
+            frm = self.place.other(k)
+            ref = dst.at[slot_rows(self.place.g * self.place.tn + frm, size)]
+            remote(ref, ref, self.asend.at[slot, k], self.arecv.at[slot, frm], {"t": frm}).wait_recv()
+
+    def share_layer(self, layer):
+        depth = self.tri.shape[2]
+        base = 1 + 2 * layer
+        self.share(("t", layer), lambda to: self.tri.at[layer, to], self.wts[layer], depth, base)
+        self.share(("i", layer), lambda to: self.inn.at[layer, to], self.wis[layer], depth, base + 1)
+        g = self.place.g
+        self.near(self.outer.at[layer], self.wos[layer].at[slot_rows(g, self.outer.shape[1])], ("o", layer))
+        here, far = self.proj_copies(layer)
+        pl.when(self.moved)(far.start)
+        pl.when(jnp.logical_not(self.moved))(here.start)
+
+    def proj_copies(self, layer):
+        prows = self.proj.shape[1]
+        src = self.proj.at[layer]
+        here = pltpu.make_async_copy(src, self.wps[layer].at[slot_rows(self.place.g, prows)], self.psend.at[layer])
+        dst = self.wps[layer].at[slot_rows(lax.rem(self.r, self.place.gn), prows)]
+        return here, remote(src, dst, self.psend.at[layer], self.precv.at[layer], self.target)
+
+    def proj_ready(self, layer):
+        here, far = self.proj_copies(layer)
+
+        @pl.when(self.moved)
+        def _():
+            far.wait_recv()
+            far.wait_send()
+
+        pl.when(jnp.logical_not(self.moved))(here.wait)
+
+    def start(self):
+        place, span = self.place, 2 * self.place.tn
+        self.move(self.tok, self.tok_o, 0)
+        vec_rows = self.vec.shape[0]
+        self.share("v", lambda to: self.vec, self.vec_o, vec_rows, 0)
+        self.near(self.seg, self.seg_o.at[slot_rows(place.c, 8)], "s")
+        for k in range(1, span):
+            to = lax.rem(place.c + k, span)
+            dst = self.seg_o.at[slot_rows(place.c, 8)]
+            cp = remote(self.seg, dst, self.gsend.at[k], self.grecv.at[place.c], place.line(to))
+            cp.start()
+            self.sends.append(cp)
+        for layer in range(self.layers):
+            self.share_layer(layer)
+        orders = bit_orders(place)
+        self.chunks, slot = [], 0
+        tn, depth = place.tn, self.tri.shape[2]
+        todo = []
+        for layer in range(self.layers):
+            todo += [
+                [(("t", layer), self.wts[layer], tn * depth)],
+                [(("i", layer), self.wis[layer], tn * depth)],
+                [
+                    (("o", layer), self.wos[layer], self.outer.shape[1]),
+                    (("p", layer), self.wps[layer], self.proj.shape[1]),
+                ],
+            ]
+        todo[0].insert(0, ("v", self.vec_o, tn * vec_rows))
+        self.keys = [[key for key, _, _ in chunk] for chunk in todo]
+        for chunk in todo:
+            parts = []
+            for _, ref, block in chunk:
+                pieces = halves(ref.shape[1]) if ref.shape[1] >= 256 else [pl.ds(0, ref.shape[1])]
+                for i, piece in enumerate(pieces):
+                    parts.append(Doubling(place, ref, block, piece, orders[i], (self.ssem, self.rsem), slot))
+                    slot += 1
+            self.chunks.append(parts)
+        self.steps = len(place.bits)
+        self.turn, self.turns = 0, len(self.chunks) + SKEW * (self.steps - 1)
+        self.complete = set()
+
+    def ready(self, i):
+        for key in self.keys[i]:
+            if key == "v" or key[0] in ("t", "i"):
+                self.shared(key)
+            elif key[0] == "o":
+                self.locals_of[key].wait()
+            else:
+                self.proj_ready(key[1])
+
+    def tick(self, until=None):
+        while self.turn < self.turns and (until is None or self.turn <= until):
+            for step in reversed(range(self.steps)):
+                i = self.turn - SKEW * step
+                if 0 <= i < len(self.chunks):
+                    if step == 0:
+                        self.ready(i)
+                    for part in self.chunks[i]:
+                        part.advance(step)
+            self.turn += 1
+            if until is None:
+                break
+
+    def have(self, key):
+        i = [key in keys for keys in self.keys].index(True)
+        if i not in self.complete:
+            self.complete.add(i)
+            self.tick(i + SKEW * (self.steps - 1))
+            for part in self.chunks[i]:
+                part.whole()
+
+    def segments_in(self):
+        place, span = self.place, 2 * self.place.tn
+        self.locals_of["s"].wait()
+        for k in range(1, span):
+            frm = lax.rem(place.c + k, span)
+            ref = self.seg_o.at[slot_rows(frm, 8)]
+            remote(ref, ref, self.gsend.at[k], self.grecv.at[frm], place.line(frm)).wait_recv()
+
+    def finish(self):
+        self.tick(self.turns)
+        for parts in self.chunks:
+            for part in parts:
+                part.finish()
+        for cp in self.sends:
+            cp.wait_send()
+
+
+def ascend_kernel(
+    gn, tn, layers, size,
+    tok, cot, seg, vec, tri, inn, outer, proj, ctab, satab, sbtab, e32, m32, e96, m96,
+    cot_o, out_o, segcol, segrow, vecs_o, bts_o, bis_o, xs_o, w_o, kept_o,
+    w, kept, xs, x_low, out_low, keep, seg_in, vec_in, vec_wide, bt_wide,
+    bufs, group, opening_sems, save_sem, tok_sem,
 ):
-    wts, wis, wos, wps = (rest[i * layers : (i + 1) * layers] for i in range(4))
-    (ssem, rsem, lsem, asend, arecv, psend, precv, msend, mrecv, gsend, grecv) = rest[4 * layers :]
     place = Place(gn, tn)
-    g, t, c = place.g, place.t, place.c
-    span = 2 * tn
-    target, source, r, q = proj_places(place)
-    moved = q != r
-    line_barrier(place, (source, moved))
-    local, sends = [], []
-
-    def near(src, dst):
-        cp = pltpu.make_async_copy(src, dst, lsem.at[len(local)])
+    opening = Opening(
+        place, layers, tok, cot, seg, vec, tri, inn, outer, proj, x_low, cot_o, seg_in, vec_in, w, opening_sems
+    )
+    opening.barrier()
+    opening.start()
+    saves = []
+
+    def save(src, dst):
+        cp = pltpu.make_async_copy(src, dst, save_sem.at[len(saves)])
         cp.start()
-        local.append(cp)
-
-    half = tok.shape[1]
-
-    def move(src, dst, slot):
-        for i in range(2):
-            to = i * tn + c // 2
-            rows = pl.ds(pl.multiple_of(lax.rem(c, 2) * half, half), half)
-
-            @pl.when(to == c)
-            def _():
-                pltpu.make_async_copy(src.at[i], dst.at[rows], msend.at[slot, i]).start()
-
-            @pl.when(to != c)
-            def _():
-                remote(
-                    src.at[i], dst.at[rows], msend.at[slot, i], mrecv.at[slot, lax.rem(c, 2)], place.line(to)
-                ).start()
-
-    def moved_in(src, dst, slot):
-        for i in range(2):
-            to = i * tn + c // 2
-            rows = pl.ds(pl.multiple_of(lax.rem(c, 2) * half, half), half)
-
-            @pl.when(to == c)
-            def _():
-                pltpu.make_async_copy(src.at[i], dst.at[rows], msend.at[slot, i]).wait()
-
-            @pl.when(to != c)
-            def _():
-                remote(
-                    src.at[i], dst.at[rows], msend.at[slot, i], mrecv.at[slot, lax.rem(c, 2)], place.line(to)
-                ).wait_send()
-
-        for s in range(2):
-
-            @pl.when(2 * t + s != c)
-            def _():
-                rows = pl.ds(s * half, half)
-                remote(
-                    src.at[0], dst.at[rows], msend.at[slot, 0], mrecv.at[slot, s], place.line(c)
-                ).wait_recv()
-
-    move(tok, tok_o, 0)
-
-    def slot_rows(index, size):
-        return pl.ds(pl.multiple_of(index * size, size), size)
-
-    def share(src_of, dst, slot):
-        size = src_of(0).shape[0]
-        rows = slot_rows(g * tn + t, size)
-        near(src_of(t), dst.at[rows])
-        for k in range(1, tn):
-            to = place.other(k)
-            cp = remote(
-                src_of(to), dst.at[rows], asend.at[slot, k], arecv.at[slot, t], {"t": to}
+        saves.append(cp)
+
+    opening.tick(1)
+    opening.moved_in(tok, x_low, 0)
+    xs[0][...] = x_low[...].astype(F32)
+    spreads, gathers, stages = [], [], []
+    for layer in range(layers):
+        ssem, fsem, rsem, cs, cr, ls, lr = group[layer]
+        spreads.append(Spread(tn, kept[layer][0], size, ssem, fsem, rsem))
+        gathers.append(Gather(tn, *bufs, (cs, cr, ls, lr)))
+        stages.append(
+            Forward(
+                tn, size, xs[layer], tuple(w[k][layer] for k in range(4)),
+                (vecs_o.at[layer], bts_o.at[layer], bis_o.at[layer]), (segcol, segrow), (ctab, satab, sbtab),
+                kept[layer], keep,
             )
-            cp.start()
-            sends.append(cp)
-
-    def shared(dst, slot, size):
-        for k in range(1, tn):
-            frm = place.other(k)
-            ref = dst.at[slot_rows(g * tn + frm, size)]
-            remote(ref, ref, asend.at[slot, k], arecv.at[slot, frm], {"t": frm}).wait_recv()
-
-    depth = ti[0].shape[2]
-    triple_cols, inner_cols = wts[0].shape[1], wis[0].shape[1]
+        )
+    stages[0].norm(place.t)
+    spreads[0].start()
+    opening.segments_in()
+    block = segcol.shape[0] // (2 * tn)
+    eye = lax.broadcasted_iota(jnp.int32, (block, block), 0) == lax.broadcasted_iota(jnp.int32, (block, block), 1)
+    for i in range(2 * tn):
+        row = jnp.where(place.h == 0, seg_in[8 * i : 8 * i + 1, :], seg_in[8 * i + 1 : 8 * i + 2, :])
+        spot = lax.broadcasted_iota(jnp.int32, (1, block), 1) + i * block
+        row = jnp.where(row == 0, -1 - spot, row).astype(F32)
+        segrow[:, i * block : (i + 1) * block] = row
+        segcol[i * block : (i + 1) * block, :] = jnp.sum(jnp.where(eye, row, 0.0), axis=1, keepdims=True)
+    opening.have("v")
+    shards = gn * tn
     vec_rows = vec.shape[0]
-    shares = [(lambda to: vec, vec_o, vec_rows)]
+    vec_wide[...] = vec_in[...].astype(F32)
+    lane = lax.broadcasted_iota(jnp.int32, (1, 128), 1)
     for layer in range(layers):
-        lay = layer
-        shares.append((lambda to, lay=lay: ti[0].at[lay, to], wts[layer], depth))
-        shares.append((lambda to, lay=lay: ti[1].at[lay, to], wis[layer], depth))
-    for slot, (src_of, dst, size) in enumerate(shares):
-        share(src_of, dst, slot)
-    prows = proj.shape[1]
-    orows = outer.shape[1]
+
+        def line(k):
+            return vec_wide[pl.ds(4 * layer + k, shards, stride=vec_rows), :]
+
+        def spread_out(value, place_of, mask):
+            return jnp.sum(dot(value.astype(BF16), place_of, NN) * mask, axis=0, keepdims=True)
+
+        thick = line(2)
+        parts = [jnp.where(lane // 32 == i, thick, 0.0) for i in range(4)]
+        thin = line(3)
+        gains = [jnp.where(lane // 32 == i, thin, 0.0) for i in range(2)]
+        rows = [spread_out(p, e32[...], m32[...]) for p in parts + gains]
+        vecs_o[layer] = jnp.concatenate(
+            [rows[2], rows[3], rows[4], rows[5], rows[0] + rows[1]] + [jnp.zeros_like(rows[0])] * 3, axis=0
+        )
+        bt_wide[...] = spread_out(line(1), e96[...], m96[...])
+        wide = bts_o.shape[2] // 3
+        for i in range(3):
+            start = pl.multiple_of(i * wide * tn + place.t * wide, 128)
+            bts_o[layer, :, i * wide : (i + 1) * wide] = bt_wide[:, pl.ds(start, wide)]
+        for i in range(gn):
+            bis_o[layer, :, i * 128 : (i + 1) * 128] = vec_wide[
+                pl.ds((i * tn + place.t) * vec_rows + 4 * layer, 1), :
+            ]
+
     for layer in range(layers):
-        near(outer.at[layer], wos[layer].at[slot_rows(g, orows)])
-        src = proj.at[layer]
-
-        @pl.when(moved)
-        def _():
-            dst = wps[layer].at[slot_rows(lax.rem(r, gn), prows)]
-            remote(src, dst, psend.at[layer], precv.at[layer], target).start()
-
-        @pl.when(jnp.logical_not(moved))
-        def _():
-            pltpu.make_async_copy(src, wps[layer].at[slot_rows(g, prows)], psend.at[layer]).start()
-
-    near(seg, seg_o.at[slot_rows(c, 8)])
-    for k in range(1, span):
-        to = lax.rem(c + k, span)
-        cp = remote(seg, seg_o.at[slot_rows(c, 8)], gsend.at[k], grecv.at[c], place.line(to))
-        cp.start()
-        sends.append(cp)
-    move(cot, cot_o, 1)
-
-    sems = (ssem, rsem)
-    orders = bit_orders(place)
-    chunks, slot = [], 0
-    waits = []
-
-    def add(ref, block, ready):
-        nonlocal slot
-        parts = []
-        cols = ref.shape[1]
-        pieces = halves(cols) if cols >= 256 else [pl.ds(0, cols)]
-        for i, piece in enumerate(pieces):
-            parts.append(Doubling(place, ref, block, piece, orders[i], sems, slot))
-            slot += 1
-        chunks.append(parts)
-        waits.append(ready)
-
-    for cp in local:
+        stage, spread, gather = stages[layer], spreads[layer], gathers[layer]
+        if layer > 0:
+            stage.norm(place.t)
+            spread.start()
+        opening.have(("t", layer))
+        for i, b in enumerate(arrivals(spread)):
+            stage.heads_in(b)
+            if i == 1:
+                opening.tick()
+        if layer == 0:
+            opening.move(cot, cot_o, 1)
+        for i, b in enumerate(far_first(spread)):
+            stage.attend(b)
+            if i == 1:
+                opening.tick()
+        opening.have(("i", layer))
+        save(kept[layer][0], kept_o[layer][0])
+        for i in range(1, 6):
+            save(kept[layer][i], kept_o[layer][i])
+        for i, b in enumerate(far_first(spread)):
+            stage.mixer_in(b)
+            if i == 1:
+                opening.tick()
+        save(kept[layer][6], kept_o[layer][6])
+        save(kept[layer][7], kept_o[layer][7])
+        opening.have(("o", layer))
+        for k in range(4):
+            save(w[k][layer], w_o[k][layer])
+        branch_sums(stage, spread, gather, opening.tick)
+        total = xs[layer][...] + vecs_o[layer, 4:5, :] + keep[...] + gather.total()
+        if layer + 1 < layers:
+            xs[layer + 1][...] = total
+        else:
+            out_low[...] = total.astype(BF16)
+            save(out_low, out_o)
+        save(xs[layer], xs_o[layer])
+        spread.finish()
+        gather.finish()
+    opening.finish()
+    opening.moved_in(cot, cot_o, 1)
+    for cp in saves:
         cp.wait()
-    add(vec_o, tn * vec_rows, lambda: shared(vec_o, 0, vec_rows))
-    for layer in range(layers):
-        base = 1 + 2 * layer
-
-        def proj_ready(layer=layer):
-            ref = wps[layer].at[slot_rows(g, prows)]
-
-            @pl.when(moved)
-            def _():
-                cp = remote(ref, ref, psend.at[layer], precv.at[layer], target)
-                cp.wait_recv()
-                cp.wait_send()
-
-            @pl.when(jnp.logical_not(moved))
-            def _():
-                pltpu.make_async_copy(proj.at[layer], ref, psend.at[layer]).wait()
-
-        add(wts[layer], tn * depth, lambda base=base, layer=layer: shared(wts[layer], base, depth))
-        add(wis[layer], tn * depth, lambda base=base, layer=layer: shared(wis[layer], base + 1, depth))
-        add(wos[layer], orows, lambda: None)
-        add(wps[layer], prows, proj_ready)
-    steps = len(place.bits) + 1
-    for turn in range(len(chunks) + steps - 1):
-        for step in range(steps):
-            i = turn - step
-            if 0 <= i < len(chunks):
-                if step == 0:
-                    waits[i]()
-                for part in chunks[i]:
-                    part.advance(step)
-    for parts in chunks:
-        for part in parts:
-            part.finish()
-    for cp in sends:
-        cp.wait_send()
-    for k in range(1, span):
-        frm = lax.rem(c + k, span)
-        ref = seg_o.at[slot_rows(frm, 8)]
-        remote(ref, ref, gsend.at[k], grecv.at[frm], place.line(frm)).wait_recv()
-    moved_in(tok, tok_o, 0)
-    moved_in(cot, cot_o, 1)
 
 
 ANY = pl.BlockSpec(memory_space=pl.ANY)
 
 
-def open_call(gn, tn, tokens, cotangent, segments, vec, tri, inn, outer, proj):
+def constant_tables(span, shards, model):
+    angle = np.arange(span, dtype=np.float32)[:, None] * (
+        np.float32(10000.0) ** (-(2.0 * np.arange(ROT // 2, dtype=np.float32)) / np.float32(ROT))
+    )
+    cosine, sine = np.cos(angle).astype(np.float32), np.sin(angle).astype(np.float32)
+    none, empty = np.zeros((span, HD - ROT), np.float32), np.zeros_like(sine)
+    reps = 128 // HD
+    ctab = np.concatenate([cosine, cosine, none + 1.0] * reps, axis=1)
+    satab = np.concatenate([-sine, empty, none] * reps, axis=1)
+    sbtab = np.concatenate([empty, sine, none] * reps, axis=1)
+    return tuple(jnp.asarray(tab, F32) for tab in (ctab, satab, sbtab))
+
+
+def placement(piece, shards):
+    j, col = np.arange(128)[:, None], np.arange(piece * shards)[None, :]
+    put = (j % piece == col % piece) if 128 % piece == 0 else (j == col % piece)
+    mask = np.arange(shards)[:, None] == col // piece
+    return jnp.asarray(put, BF16), jnp.asarray(mask, F32)
+
+
+def kept_shapes(length, model, width, units):
+    return [
+        ((length, model), BF16),
+        ((length, width), BF16),
+        ((length, width), BF16),
+        ((length, width), BF16),
+        ((length, width), F32),
+        ((length, 128), F32),
+        ((length, units), BF16),
+        ((length, units), BF16),
+    ]
+
+
+def ascend_call(gn, tn, tokens, cotangent, segments, vec, tri, inn, outer, proj, tables, placing):
     layers = outer.shape[0]
     _, half, model = tokens.shape
-    rows = tn * tri.shape[2]
+    size = 2 * half
+    length = size * tn
+    depth = tri.shape[2]
+    wshapes = [
+        (gn * tn * depth, tri.shape[3]), (gn * tn * depth, inn.shape[3]),
+        (gn * outer.shape[1], model), (gn * proj.shape[1], model),
+    ]
+    width, units, chips = wshapes[3][0], wshapes[2][0], tn // 2
+    kept = kept_shapes(length, model, width, units)
     dma = pltpu.SemaphoreType.DMA
-
-    def body(tok, cot, seg, vec, tri, inn, *rest):
-        open_kernel(gn, tn, layers, tok, cot, seg, vec, (tri, inn), *rest)
-
-    outs = (
-        [shape((2 * half, model), BF16)] * 2
-        + [shape((2 * tn * 8, 128), jnp.int32), shape((gn * tn * vec.shape[0], 128), BF16)]
-        + [shape((gn * rows, tri.shape[3]), BF16)] * layers
-        + [shape((gn * rows, inn.shape[3]), BF16)] * layers
-        + [shape((gn * outer.shape[1], model), BF16)] * layers
-        + [shape((gn * proj.shape[1], model), BF16)] * layers
-    )
+    outs = [
+        (shape((size, model), BF16), ANY),
+        (shape((size, model), BF16), ANY),
+        (shape((length, 1), F32), VM),
+        (shape((1, length), F32), VM),
+        (shape((layers, 8, model), F32), VM),
+        (shape((layers, 1, 3 * width), F32), VM),
+        (shape((layers, 1, units), F32), VM),
+    ]
+    outs += [(shape((size, model), F32), ANY)] * layers
+    for dims in wshapes:
+        outs += [(shape(dims, BF16), ANY)] * layers
+    for _ in range(layers):
+        outs += [(shape(*item), ANY) for item in kept]
+    scratch = []
+    for dims in wshapes:
+        scratch += [pltpu.VMEM(dims, BF16)] * layers
+    for _ in range(layers):
+        scratch += [pltpu.VMEM(*item) for item in kept]
+    scratch += [pltpu.VMEM((size, model), F32)] * layers
+    scratch += [
+        pltpu.VMEM((size, model), BF16),
+        pltpu.VMEM((size, model), BF16),
+        pltpu.VMEM((size, model), F32),
+        pltpu.VMEM((2 * tn * 8, 128), jnp.int32),
+        pltpu.VMEM((gn * tn * vec.shape[0], 128), BF16),
+        pltpu.VMEM((gn * tn * vec.shape[0], 128), F32),
+        pltpu.VMEM((1, 3 * model), F32),
+    ]
+    scratch += group_buffers(chips, size, model)
+    for _ in range(layers):
+        scratch += group_sems(chips, tn)
     slots = 1 + 8 * layers
+    scratch += [
+        dma((slots, gn)), dma((slots, gn)), dma((2 + 3 * layers,)),
+        dma((1 + 2 * layers, tn)), dma((1 + 2 * layers, tn)),
+        dma((layers,)), dma((layers,)), dma((2, 2)), dma((2, 2)),
+        dma((2 * tn,)), dma((2 * tn,)),
+    ]
+    scratch += [dma((14 * layers,)), dma((1,))]
+
+    def body(*refs):
+        refs = list(refs)
+
+        def take(count):
+            out, refs[:] = refs[:count], refs[count:]
+            return out
+
+        ins = take(15)
+        cot_o, out_o, segcol, segrow, vecs_o, bts_o, bis_o = take(7)
+        xs_o = take(layers)
+        w_o = [take(layers) for _ in range(4)]
+        kept_o = [take(8) for _ in range(layers)]
+        w = [take(layers) for _ in range(4)]
+        kept_s = [take(8) for _ in range(layers)]
+        xs = take(layers)
+        x_low, out_low, keep, seg_in, vec_in, vec_wide, bt_wide = take(7)
+        bufs = take(4)
+        group = [take(7) for _ in range(layers)]
+        sems = take(11)
+        save_sem, tok_sem = take(2)
+        ascend_kernel(
+            gn, tn, layers, size, *ins, cot_o, out_o, segcol, segrow, vecs_o, bts_o, bis_o, xs_o, w_o, kept_o,
+            w, kept_s, xs, x_low, out_low, keep, seg_in, vec_in, vec_wide, bt_wide, bufs, group, sems,
+            save_sem, tok_sem,
+        )
+
     return pl.pallas_call(
         body,
-        out_shape=tuple(outs),
-        in_specs=[ANY] * 8,
-        out_specs=tuple([ANY] * len(outs)),
-        scratch_shapes=[
-            dma((slots, gn)), dma((slots, gn)), dma((2 + 3 * layers,)),
-            dma((1 + 2 * layers, tn)), dma((1 + 2 * layers, tn)),
-            dma((layers,)), dma((layers,)), dma((2, 2)), dma((2, 2)),
-            dma((2 * tn,)), dma((2 * tn,)),
-        ],
+        out_shape=tuple(o for o, _ in outs),
+        in_specs=[ANY] * 8 + [VM] * 7,
+        out_specs=tuple(spec for _, spec in outs),
+        scratch_shapes=scratch,
         compiler_params=params_of(2),
-        name="opening",
-    )(tokens, cotangent, segments, vec, tri, inn, outer, proj)
+        name="ascend",
+    )(tokens, cotangent, segments, vec, tri, inn, outer, proj, *tables, *placing)
 
 
 class Halving:
@@ -1093,12 +1371,12 @@
 
             proj_o[layer] = projbox[layer].astype(F32)
 
-    total = len(chunks) + steps + 1
-    for turn in range(max(total, len(exchanges) + 1)):
+    turns = len(chunks) + SKEW * (steps + 1)
+    for turn in range(max(turns, len(exchanges) + 1)):
         if turn <= len(exchanges):
             flat_turn(turn)
-        for step in range(steps + 2):
-            i = turn - step
+        for step in reversed(range(steps + 2)):
+            i = turn - SKEW * step
             if 0 <= i < len(chunks):
                 kind, layer = plans[i]
                 if step == 0:
@@ -1278,27 +1556,41 @@
     heads_wide = model // tn
     units = outer_weight.shape[1] * gn
 
-    small = (triple_bias, inner_bias, proj_bias, outer_bias, first_gain, first_shift, second_gain, second_shift)
-    starts = [0]
-    for item in small:
-        starts.append(starts[-1] + item.shape[1])
-    packed = jnp.concatenate(small, axis=1)
     rows = triple_weight.shape[1]
-    direct = rows % 16 == 0
+    block = tokens.shape[1]
+    tables = constant_tables(span, shards, model)
+    direct = rows % 16 == 0 and block == 128 and layers * 4 <= 16
     if direct:
-        count = -(-packed.size // 2048) * 2048
-        vec = jnp.pad(packed.reshape(-1), (0, count - packed.size)).reshape(-1, 128)
-        opened = open_call(
-            gn, tn, tokens, cotangent, jnp.pad(segments, ((0, 6), (0, 0))), vec,
+        head = jnp.stack(
+            [
+                inner_bias,
+                jnp.pad(triple_bias, ((0, 0), (0, 128 - triple_bias.shape[1]))),
+                jnp.concatenate([proj_bias, outer_bias, first_gain, first_shift], axis=1),
+                jnp.pad(jnp.concatenate([second_gain, second_shift], axis=1), ((0, 0), (0, 64))),
+            ],
+            axis=1,
+        ).reshape(4 * layers, 128)
+        opened = ascend_call(
+            gn, tn, tokens, cotangent, jnp.pad(segments, ((0, 6), (0, 0))),
+            jnp.pad(head, ((0, 16 - 4 * layers), (0, 0))),
             triple_weight.reshape(layers, rows, 3, tn, -1).transpose(0, 3, 1, 2, 4).reshape(layers, tn, rows, -1),
             inner_weight.reshape(layers, rows, gn, tn, -1).transpose(0, 3, 1, 2, 4).reshape(layers, tn, rows, -1),
-            outer_weight, proj_weight,
+            outer_weight, proj_weight, tables,
+            placement(model // shards, shards) + placement(3 * model // shards, shards),
         )
-        x, cot, segs_all, vec_all = opened[0].astype(F32), opened[1].astype(F32), opened[2], opened[3]
-        weights = [tuple(opened[4 + k * layers + layer] for k in (0, 1, 2, 3)) for layer in range(layers)]
-        segs_all = segs_all.reshape(2 * tn, 8, -1)[:, :2].transpose(1, 0, 2).reshape(2, span)
-        everything = vec_all.reshape(shards, -1)[:, : packed.size].reshape((shards,) + packed.shape).astype(F32)
+        opened = list(opened)
+        cot, output, segcol, segrow, vecs, _, _ = opened[:7]
+        inputs = opened[7 : 7 + layers]
+        weights = [tuple(opened[7 + layers + k * layers + layer] for k in range(4)) for layer in range(layers)]
+        kept = [opened[7 + 5 * layers + 8 * i : 7 + 5 * layers + 8 * (i + 1)] for i in range(layers)]
+        cot = cot.astype(F32)
+        tables = (segcol, segrow) + tables
     else:
+        small = (triple_bias, inner_bias, proj_bias, outer_bias, first_gain, first_shift, second_gain, second_shift)
+        starts = [0]
+        for item in small:
+            starts.append(starts[-1] + item.shape[1])
+        packed = jnp.concatenate(small, axis=1)
         x = to_group(tn, tokens).astype(F32)
         cot = to_group(tn, cotangent).astype(F32)
         segs_all = lax.all_gather(segments, ("h", "t"), axis=1, tiled=True)
@@ -1309,42 +1601,30 @@
             )
             for layer in range(layers)
         ]
-    segs = jnp.where(h == 0, segs_all[0], segs_all[1])
-    place = jnp.arange(span, dtype=jnp.int32)
-    segs = jnp.where(segs == 0, -1 - place, segs)
-    freq = 10000.0 ** (-(2.0 * jnp.arange(ROT // 2, dtype=F32)) / ROT)
-    angle = place.astype(F32)[:, None] * freq[None, :]
-    cosine, sine = jnp.cos(angle), jnp.sin(angle)
-    none = jnp.zeros((span, HD - ROT), F32)
-    empty = jnp.zeros_like(sine)
-    ctab = jnp.concatenate([cosine, cosine, none + 1.0] * (128 // HD), axis=1)
-    satab = jnp.concatenate([-sine, empty, none] * (128 // HD), axis=1)
-    sbtab = jnp.concatenate([empty, sine, none] * (128 // HD), axis=1)
-    tables = (segs[:, None], segs[None, :], ctab, satab, sbtab)
-
-    def vector(layer, i):
-        return everything[:, layer, starts[i] : starts[i + 1]].reshape(-1)
-
-    vecs, bts, bis = [], [], []
-    for layer in range(layers):
-        bt = lax.dynamic_index_in_dim(vector(layer, 0).reshape(3, tn, heads_wide), t, 1, keepdims=False)
-        bts.append(bt.reshape(1, -1))
-        bi = lax.dynamic_index_in_dim(vector(layer, 1).reshape(gn, tn, -1), t, 1, keepdims=False)
-        bis.append(bi.reshape(1, -1))
-        zero = jnp.zeros((model,), F32)
-        vecs.append(
-            jnp.stack(
-                [vector(layer, 4), vector(layer, 5), vector(layer, 6), vector(layer, 7)]
-                + [vector(layer, 2) + vector(layer, 3), zero, zero, zero]
+        segs = jnp.where(h == 0, segs_all[0], segs_all[1])
+        segs = jnp.where(segs == 0, -1 - jnp.arange(span, dtype=jnp.int32), segs).astype(F32)
+        tables = (segs[:, None], segs[None, :]) + tables
+
+        def vector(layer, i):
+            return everything[:, layer, starts[i] : starts[i + 1]].reshape(-1)
+
+        vecs, inputs, kept = [], [], []
+        for layer in range(layers):
+            bt = lax.dynamic_index_in_dim(vector(layer, 0).reshape(3, tn, heads_wide), t, 1, keepdims=False)
+            bi = lax.dynamic_index_in_dim(vector(layer, 1).reshape(gn, tn, -1), t, 1, keepdims=False)
+            zero = jnp.zeros((model,), F32)
+            vecs.append(
+                jnp.stack(
+                    [vector(layer, 4), vector(layer, 5), vector(layer, 6), vector(layer, 7)]
+                    + [vector(layer, 2) + vector(layer, 3), zero, zero, zero]
+                )
             )
-        )
-
-    inputs, kept = [], []
-    for layer in range(layers):
-        inputs.append(x)
-        x, *saved = forward_layer(tn, x, weights[layer], vecs[layer], bts[layer], bis[layer], tables)
-        kept.append(saved)
-    output = x.astype(BF16)
+            inputs.append(x)
+            x, *saved = forward_layer(
+                tn, x, weights[layer], vecs[layer], bt.reshape(1, -1), bi.reshape(1, -1), tables
+            )
+            kept.append(saved)
+        output = x.astype(BF16)
     grad = cot
     mats, flats = [None] * layers, [None] * layers
     for layer in reversed(range(layers)):

time: 607 us -> 512 us (0.84)
  Pallas kernels: 559 us -> 477 us
  local copies, waits for them, and re-layouts: 32.1 us -> 20.7 us
    pallas_call x3 -> x1, Pallas kernels: 271 us -> 192 us  [ascend_call(): pl.pallas_call(body, out_shape=tuple((o for o, _ in outs)), in_specs=[ANY...]
    concatenate x4 -> x0, local copies, waits for them, and re-layouts: 6.1 us -> none  [the longest x1 1.75 us: per_device(): ctab = jnp.concatenate([cosine, cosine, none + 1.0] * (128 // HD), axis=1)]
where the time goes in v3:
time: 512 us; the launch traced here: 505 us
  Pallas kernels  477 us (93%)
  local copies, waits for them, and re-layouts  20.7 us (4%)
  other arithmetic  6.59 us (1%)
    pallas_call x1, Pallas kernels, ascend_call(): pl.pallas_call(body, out_shape=tuple((o for o, _ in outs)), in_specs=[ANY...  192 us
    pallas_call x1, Pallas kernels, close_call(): pl.pallas_call(body, out_shape=outs, in_specs=[ANY, ANY, VM] + [ANY] * (4...  154 us
    pallas_call x2, Pallas kernels, backward_layer(): pl.pallas_call(functools.partial(backward_kernel, tn, size), out_shape=ou...  131 us

profile of v3, /device:TPU:5, one launch (start us, length us, event | category | flops | bytes accessed | tf_op | source)
XLA Modules:
  0.0 505.3 jit_solution(11944012228610752807)
XLA Ops:
  0.7 0.8 maximum_bitcast_fusion
  1.5 0.7 fusion.3
  2.3 0.7 pad_maximum_fusion.3
  2.9 0.6 pad.19.refs_3_
  3.5 1.4 reshape.84
  5.0 1.0 reshape.85.refs_5_
  6.0 0.3 reshape.82
  6.3 0.2 copy.52
  6.5 1.2 reshape.83.refs_4_
  7.7 0.6 pad.16.refs_2_
  8.3 191.9 %ascend.1 = (bf16[256,1024]{1,0:T(8,128)(2,1)}, bf16[256,1024]{1,0:T(8,128)(2,1)}, f32[1024,1]{1,0:T(8,128)}, f32[1,1024]{1,0:T(1,128)}, f32[2,8,1024]{2,1,0:T(8...) custom-call(bf16[2,128,1024]{2,1,0:T(8,128)(2,1)} %refs_0_.1, ...), custom_call_target="tpu_custom_call" | custom-call | tf_op jit(solution)/shard_map/ascend/pallas_call | solution.py:1166
  200.2 1.4 slice_bitcast_fusion
  201.6 2.1 convert_element_type.12.dy_ref
  203.7 64.1 %backward.2 = (f32[256,1024]{1,0:T(8,128)}, bf16[1024,768]{1,0:T(8,128)(2,1)}, bf16[1024,1024]{1,0:T(8,128)(2,1)}, bf16[1024,1024]{1,0:T(8,128)(2,1)}, bf16[256,...) custom-call(f32[256,1024]{1,0:T(8,128)} %convert_element_type.12.dy_ref, ...), custom_call_target="tpu_custom_call" | custom-call | tf_op jit(solution)/shard_map/backward/pallas_call | solution.py:578
  267.9 67.3 %backward.3 = (f32[256,1024]{1,0:T(8,128)}, bf16[1024,768]{1,0:T(8,128)(2,1)}, bf16[1024,1024]{1,0:T(8,128)(2,1)}, bf16[1024,1024]{1,0:T(8,128)(2,1)}, bf16[256,...) custom-call(f32[256,1024]{1,0:T(8,128)} %get-tuple-element.87.dy_ref, ...), custom_call_target="tpu_custom_call" | custom-call | tf_op jit(solution)/shard_map/backward/pallas_call | solution.py:578
  335.2 0.7 dynamic_update_slice.12
  336.0 0.7 dynamic_update_slice.13
  336.7 0.8 reshape.86
  337.8 0.7 reshape.96.flat_in
  338.5 2.1 convert_element_type.13.grad_in
  340.6 153.7 %closing.1 = (bf16[2,128,1024]{2,1,0:T(8,128)(2,1)}, bf16[2,128,1024]{2,1,0:T(8,128)(2,1)}, f32[24,1024]{1,0:T(8,128)}, f32[2,32,3072]{2,1,0:T(8,128)}, f32[2,32...) custom-call(bf16[256,1024]{1,0:T(8,128)(2,1)} %get-tuple-element.69.out_in, ...), custom_call_target="tpu_custom_call" | custom-call | tf_op jit(solution)/shard_map/closing/pallas_call | solution.py:1444
  494.3 1.1 reshape.97
  495.3 0.7 constant_dynamic-slice_fusion
  496.0 0.6 constant_dynamic-slice_fusion.4
  496.6 0.6 constant_dynamic-slice_fusion.7
  497.2 0.6 copy.64
  497.8 2.0 copy.65
  499.7 1.9 copy.66
  501.6 0.9 copy.67
  502.5 0.7 copy.68
  503.2 1.0 copy.69
  504.2 1.0 copy.70
  (34 shorter events, 0.4 us)
Async XLA Ops:
  0.6 5.4 %copy-start.3 = (bf16[2,32,3072]{2,1,0:T(8,128)(2,1)S(1)}, bf16[2,32,3072]{2,1,0:T(8,128)(2,1)}, u32[]{:S(2)}) copy-start(bf16[2,32,3072]{2,1,0:T(8,128)(2,1)} %param.25) | copy-start | bytes 1179652
  5.0 2.7 copy-start.9
  267.8 69.6 %copy-start.8 = (f32[1,768]{1,0:T(1,128)S(1)}, f32[1,768]{1,0:T(1,128)}, u32[]{:S(2)}) copy-start(f32[1,768]{1,0:T(1,128)} %get-tuple-element.106) | copy-start | bytes 9220
  267.9 69.7 %copy-start.6 = (f32[1,1024]{1,0:T(1,128)S(1)}, f32[1,1024]{1,0:T(1,128)}, u32[]{:S(2)}) copy-start(f32[1,1024]{1,0:T(1,128)} %get-tuple-element.107) | copy-start | bytes 12292
  267.9 69.8 %copy-start.5 = (f32[8,1024]{1,0:T(8,128)S(1)}, f32[8,1024]{1,0:T(8,128)}, u32[]{:S(2)}) copy-start(f32[8,1024]{1,0:T(8,128)} %get-tuple-element.105) | copy-start | bytes 98308
  494.2 7.4 %copy-start.2 = (f32[2,32,3072]{2,1,0:T(8,128)S(1)}, f32[2,32,3072]{2,1,0:T(8,128)}, u32[]{:S(2)}) copy-start(f32[2,32,3072]{2,1,0:T(8,128)} %get-tuple-element.180) | copy-start | bytes 2359300
  494.2 8.2 %copy-start.4 = (f32[2,32,1024]{2,1,0:T(8,128)S(1)}, f32[2,32,1024]{2,1,0:T(8,128)}, u32[]{:S(2)}) copy-start(f32[2,32,1024]{2,1,0:T(8,128)} %get-tuple-element.183) | copy-start | bytes 786436
  496.0 7.2 %copy-start.7 = (f32[2,32]{1,0:T(2,128)}, f32[2,32]{1,0:T(2,128)S(1)}, u32[]{:S(2)}) copy-start(f32[2,32]{1,0:T(2,128)S(1)} %get-tuple-element.184) | copy-start | bytes 772
  497.8 5.4 %copy-start.1 = (f32[2,32,4096]{2,1,0:T(8,128)S(1)}, f32[2,32,4096]{2,1,0:T(8,128)}, u32[]{:S(2)}) copy-start(f32[2,32,4096]{2,1,0:T(8,128)} %get-tuple-element.185) | copy-start | bytes 3145732
  501.6 2.6 copy-start

commit v4 on v3

--- a/solution.py
+++ b/solution.py
@@ -152,11 +152,12 @@
     return jnp.concatenate([tab] * (width // tab.shape[1]), axis=1)
 
 
-def turn(x, cos, sa, sb, sign):
+def turn(x, cos, sine, sign):
     width = x.shape[1]
-    cos, sa, sb = widen(cos, width), widen(sa, width), widen(sb, width)
-    side = pltpu.roll(x, width - ROT // 2, 1) * sa + pltpu.roll(x, ROT // 2, 1) * sb
-    return x * cos + sign * side
+    cos, sine = widen(cos, width), widen(sine, width)
+    front = lax.rem(lax.broadcasted_iota(jnp.int32, (1, width), 1), HD) < ROT // 2
+    partner = jnp.where(front, pltpu.roll(x, width - ROT // 2, 1), pltpu.roll(x, ROT // 2, 1))
+    return x * cos + sign * (partner * sine)
 
 
 def head_masks(width, dtype):
@@ -195,12 +196,12 @@
         width, vec, bt = self.width, self.vec, self.bt
         rows = rows_of(b, self.size)
         h1 = (self.n[rows, :].astype(F32) * vec[0:1, :] + vec[1:2, :]).astype(BF16)
-        cos, sa, sb = (tab[rows, :] for tab in self.tables)
+        cos, sine = (tab[rows, :] for tab in self.tables)
         q = dot(h1, self.wt[:, 0:width], NN) + bt[:, 0:width]
-        low = turn(q, cos, sa, sb, 1.0).astype(BF16).astype(F32)
+        low = turn(q, cos, sine, 1.0).astype(BF16).astype(F32)
         self.q[rows, :] = (low * (1.0 / math.sqrt(HD))).astype(BF16)
         k = dot(h1, self.wt[:, width : 2 * width], NN) + bt[:, width : 2 * width]
-        self.k[rows, :] = turn(k, cos, sa, sb, 1.0).astype(BF16)
+        self.k[rows, :] = turn(k, cos, sine, 1.0).astype(BF16)
         v = dot(h1, self.wt[:, 2 * width : 3 * width], NN) + bt[:, 2 * width : 3 * width]
         self.v[rows, :] = v.astype(BF16)
 
@@ -314,7 +315,7 @@
 
 def forward_kernel(
     tn, size,
-    x_ref, wt, wi, wo, wp, vec, bt, bi, segcol, segrow, ctab, satab, sbtab,
+    x_ref, wt, wi, wo, wp, vec, bt, bi, segcol, segrow, ctab, stab,
     xo_ref, n_ref, q_ref, k_ref, v_ref, o_ref, lse_ref, g_ref, gp_ref,
     keep, tocore, fromcore, toici, fromici, ssem, fsem, rsem, cs, cr, ls, lr,
 ):
@@ -322,7 +323,7 @@
     spread = Spread(tn, n_ref, size, ssem, fsem, rsem)
     gather = Gather(tn, tocore, fromcore, toici, fromici, (cs, cr, ls, lr))
     layer = Forward(
-        tn, size, x_ref, (wt, wi, wo, wp), (vec, bt, bi), (segcol, segrow), (ctab, satab, sbtab),
+        tn, size, x_ref, (wt, wi, wo, wp), (vec, bt, bi), (segcol, segrow), (ctab, stab),
         (n_ref, q_ref, k_ref, v_ref, o_ref, lse_ref, g_ref, gp_ref), keep,
     )
     layer.norm(spread.t)
@@ -340,7 +341,7 @@
 
 def backward_kernel(
     tn, size,
-    dy_ref, x_ref, wt, wi, wo, wp, vec, segcol, segrow, ctab, satab, sbtab,
+    dy_ref, x_ref, wt, wi, wo, wp, vec, segcol, segrow, ctab, stab,
     n_ref, q_ref, k_ref, v_ref, o_ref, lse_ref, g_ref, gp_ref,
     dx_ref, dwt, dwi, dwo, dwp, dvec, dbt, dbi,
     gb, do, du, dt, dq, dk, dv, dh2, keep,
@@ -433,9 +434,9 @@
 
         lax.fori_loop(0, tsize - stage, step, 0)
         rows = rows_of(pivot, size)
-        cos, sa, sb = ctab[rows, :], satab[rows, :], sbtab[rows, :]
-        dt[rows, 0:width] = turn(dq[rows, :] * (1.0 / math.sqrt(HD)), cos, sa, sb, -1.0).astype(BF16)
-        dt[rows, width : 2 * width] = turn(dk[rows, :], cos, sa, sb, -1.0).astype(BF16)
+        cos, sine = ctab[rows, :], stab[rows, :]
+        dt[rows, 0:width] = turn(dq[rows, :] * (1.0 / math.sqrt(HD)), cos, sine, -1.0).astype(BF16)
+        dt[rows, width : 2 * width] = turn(dk[rows, :], cos, sine, -1.0).astype(BF16)
         dt[rows, 2 * width : 3 * width] = dv[rows, :].astype(BF16)
         block = dt[rows, :]
         dbt[...] += jnp.sum(block.astype(F32), axis=0, keepdims=True)
@@ -552,7 +553,7 @@
     return pl.pallas_call(
         functools.partial(forward_kernel, tn, size),
         out_shape=outs,
-        in_specs=[VM] * 13,
+        in_specs=[VM] * 12,
         out_specs=[VM] * len(outs),
         scratch_shapes=[pltpu.VMEM((size, model), F32)] + group_buffers(chips, size, model) + group_sems(chips, tn),
         compiler_params=params_of(0),
@@ -578,7 +579,7 @@
     return pl.pallas_call(
         functools.partial(backward_kernel, tn, size),
         out_shape=outs,
-        in_specs=[VM] * 20,
+        in_specs=[VM] * 19,
         out_specs=[VM] * len(outs),
         scratch_shapes=[
             pltpu.VMEM((length, model), BF16),
@@ -927,7 +928,7 @@
 
 def ascend_kernel(
     gn, tn, layers, size,
-    tok, cot, seg, vec, tri, inn, outer, proj, ctab, satab, sbtab, e32, m32, e96, m96,
+    tok, cot, seg, vec, tri, inn, outer, proj, ctab, stab, e32, m32, e96, m96,
     cot_o, out_o, segcol, segrow, vecs_o, bts_o, bis_o, xs_o, w_o, kept_o,
     w, kept, xs, x_low, out_low, keep, seg_in, vec_in, vec_wide, bt_wide,
     bufs, group, opening_sems, save_sem, tok_sem,
@@ -956,7 +957,7 @@
         stages.append(
             Forward(
                 tn, size, xs[layer], tuple(w[k][layer] for k in range(4)),
-                (vecs_o.at[layer], bts_o.at[layer], bis_o.at[layer]), (segcol, segrow), (ctab, satab, sbtab),
+                (vecs_o.at[layer], bts_o.at[layer], bis_o.at[layer]), (segcol, segrow), (ctab, stab),
                 kept[layer], keep,
             )
         )
@@ -1055,12 +1056,11 @@
         np.float32(10000.0) ** (-(2.0 * np.arange(ROT // 2, dtype=np.float32)) / np.float32(ROT))
     )
     cosine, sine = np.cos(angle).astype(np.float32), np.sin(angle).astype(np.float32)
-    none, empty = np.zeros((span, HD - ROT), np.float32), np.zeros_like(sine)
+    none = np.zeros((span, HD - ROT), np.float32)
     reps = 128 // HD
     ctab = np.concatenate([cosine, cosine, none + 1.0] * reps, axis=1)
-    satab = np.concatenate([-sine, empty, none] * reps, axis=1)
-    sbtab = np.concatenate([empty, sine, none] * reps, axis=1)
-    return tuple(jnp.asarray(tab, F32) for tab in (ctab, satab, sbtab))
+    stab = np.concatenate([-sine, sine, none] * reps, axis=1)
+    return tuple(jnp.asarray(tab, F32) for tab in (ctab, stab))
 
 
 def placement(piece, shards):
@@ -1144,7 +1144,7 @@
             out, refs[:] = refs[:count], refs[count:]
             return out
 
-        ins = take(15)
+        ins = take(14)
         cot_o, out_o, segcol, segrow, vecs_o, bts_o, bis_o = take(7)
         xs_o = take(layers)
         w_o = [take(layers) for _ in range(4)]
@@ -1166,7 +1166,7 @@
     return pl.pallas_call(
         body,
         out_shape=tuple(o for o, _ in outs),
-        in_specs=[ANY] * 8 + [VM] * 7,
+        in_specs=[ANY] * 8 + [VM] * 6,
         out_specs=tuple(spec for _, spec in outs),
         scratch_shapes=scratch,
         compiler_params=params_of(2),
@@ -1220,249 +1220,500 @@
             for item in entry:
                 self.copy(*item).wait_send()
 
-
-def close_kernel(
-    gn, tn, layers,
-    out_in, grad_in, flat, dwts, dwis, dwos, dwps,
-    out_o, grad_o, flat_o, triple_o, proj_o, inner_o, outer_o,
-    accs, boxes, cross, projbox, flatbox,
-    lsem, hs, hr, cs, cr, ps, pr, ms, mr, fs, fr,
+class Reducing:
+    def __init__(self, place, layers, accs, boxes, outs, sems):
+        self.place, self.layers = place, layers
+        self.accs, self.boxes = accs, boxes
+        self.cross, self.proj_o, self.outer_o = outs[:2], outs[2], outs[3]
+        self.hs, self.hr, self.cs, self.cr, self.ps, self.pr, self.os = sems
+        self.target, self.source, self.r, self.q = proj_places(place)
+        self.moved = self.q != self.r
+        orders = bit_orders(place)
+        self.parts, slot = {}, 0
+        for layer in range(layers):
+            for kind in range(4):
+                acc = accs[kind][layer]
+                parts = []
+                for k, cols in enumerate(halves(acc.shape[1])):
+                    box = boxes[kind].at[layer]
+                    block = acc.shape[0] // place.gn
+                    parts.append(Halving(place, acc, box, block, cols, orders[k], (self.hs, self.hr), slot))
+                    slot += 1
+                self.parts[kind, layer] = parts
+        self.steps = len(place.bits) + 1
+        self.taken = {key: 0 for key in self.parts}
+
+    def advance(self, kind, layer):
+        step = self.taken[kind, layer]
+        self.taken[kind, layer] = step + 1
+        for part in self.parts[kind, layer]:
+            part.advance(step)
+        if step == self.steps - 1:
+            self.owned(kind, layer)
+
+    def own_rows(self, kind, layer, index, pieces):
+        acc = self.accs[kind][layer]
+        rows = acc.shape[0] // pieces
+        return acc.at[slot_rows(index, rows)]
+
+    def cross_copy(self, kind, layer, k):
+        place = self.place
+        to = place.other(k)
+        src = self.own_rows(kind, layer, place.g * place.tn + to, place.gn * place.tn)
+        dst = self.cross[kind].at[layer, place.t]
+        return remote(src, dst, self.cs.at[kind, layer, k], self.cr.at[kind, layer, place.t], {"t": to})
+
+    def proj_copies(self, layer):
+        src = self.own_rows(3, layer, self.place.g, self.place.gn)
+        here = pltpu.make_async_copy(src, self.proj_o.at[layer], self.ps.at[layer])
+        return here, remote(src, self.proj_o.at[layer], self.ps.at[layer], self.pr.at[layer], self.source)
+
+    def own_copy(self, kind, layer):
+        place = self.place
+        if kind == 2:
+            src, dst = self.own_rows(2, layer, place.g, place.gn), self.outer_o.at[layer]
+        else:
+            src = self.own_rows(kind, layer, place.g * place.tn + place.t, place.gn * place.tn)
+            dst = self.cross[kind].at[layer, place.t]
+        return pltpu.make_async_copy(src, dst, self.os.at[kind, layer])
+
+    def owned(self, kind, layer):
+        if kind < 3:
+            self.own_copy(kind, layer).start()
+        if kind < 2:
+            for k in range(1, self.place.tn):
+                self.cross_copy(kind, layer, k).start()
+        if kind == 3:
+            here, far = self.proj_copies(layer)
+            pl.when(self.moved)(far.start)
+            pl.when(jnp.logical_not(self.moved))(here.start)
+
+    def finish(self):
+        for (kind, layer), parts in self.parts.items():
+            for part in parts:
+                part.finish()
+            if kind < 3:
+                self.own_copy(kind, layer).wait()
+            if kind < 2:
+                for k in range(1, self.place.tn):
+                    frm = self.place.other(k)
+                    ref = self.cross[kind].at[layer, frm]
+                    remote(
+                        ref, ref, self.cs.at[kind, layer, k], self.cr.at[kind, layer, frm], {"t": frm}
+                    ).wait_recv()
+                    self.cross_copy(kind, layer, k).wait_send()
+            if kind == 3:
+                here, far = self.proj_copies(layer)
+                pl.when(self.moved)(far.wait)
+                pl.when(jnp.logical_not(self.moved))(here.wait)
+
+
+def descend_kernel(
+    gn, tn, layers, size,
+    cot, out_in, segcol, segrow, vecs, ctab, stab, xs, ws, kepts,
+    out_o, grad_o, flat_o, triple_o, inner_o, proj_o, outer_o,
+    w, kept, dy, x, gb, do, dt, dk, dv, keep, dbt, dbi, bufs, accs, boxes, flatbox,
+    group, reduce_sems, load_sem, ms, mr, fs, fr,
 ):
     place = Place(gn, tn)
     g, t, c = place.g, place.t, place.c
-    target, source, r, q = proj_places(place)
-    moved = q != r
-    loads = []
-    for i, src in enumerate(dwts + dwis + dwos + dwps):
-        cp = pltpu.make_async_copy(src, accs[i], lsem.at[i])
-        cp.start()
-        loads.append(cp)
-    line_barrier(place, (target, moved))
+    wt, wi, wo, wp = w
+    n, q, k, v, o, lse, gact, gp = kept
+    chips = tn // 2
+    width, units, model = q.shape[1], gact.shape[1], dy.shape[1]
+    heads = width // HD
+    dq, dh, du = o, gact, gp
+    loads = {}
+
+    def load(layer, names):
+        for name in names:
+            if name == "x":
+                src, dst = xs[layer], x
+            elif name == "cot":
+                src, dst = cot, gb.at[rows_of(t, size)]
+            elif name[0] == "w":
+                i = int(name[1])
+                src, dst = ws[i][layer], w[i]
+            else:
+                i = int(name[1])
+                src, dst = kepts[layer][i], kept[i]
+            cp = pltpu.make_async_copy(src, dst, load_sem.at[len(loads)])
+            cp.start()
+            loads[layer, name] = cp
+
+    waited = set()
+
+    def need(layer, names):
+        for name in names:
+            if (layer, name) not in waited:
+                waited.add((layer, name))
+                loads[layer, name].wait()
+
+    last = layers - 1
+    load(last, ["cot", "w3", "k4", "w2", "k7", "k6", "k0", "w1", "k1", "k2", "k3", "k5", "w0", "x"])
+    reducing = Reducing(place, layers, accs, boxes, (triple_o, inner_o, proj_o, outer_o), reduce_sems)
+    line_barrier(place, (reducing.target, reducing.moved))
     half = out_o.shape[1]
+
+    def hop(src, dst, slot, s):
+        to = 2 * t + s
+        part = src.at[pl.ds(s * half, half)]
+        near = pltpu.make_async_copy(part, dst.at[place.h], ms.at[slot, s])
+        far = remote(part, dst.at[place.h], ms.at[slot, s], mr.at[slot, place.h], place.line(to))
+        return to == c, near, far
 
     def move(src, dst, slot):
         for s in range(2):
-            to = 2 * t + s
-
-            @pl.when(to == c)
-            def _():
-                pltpu.make_async_copy(src.at[pl.ds(s * half, half)], dst.at[place.h], ms.at[slot, s]).start()
-
-            @pl.when(to != c)
-            def _():
-                remote(
-                    src.at[pl.ds(s * half, half)], dst.at[place.h], ms.at[slot, s], mr.at[slot, place.h], place.line(to)
-                ).start()
+            stays, near, far = hop(src, dst, slot, s)
+            pl.when(stays)(near.start)
+            pl.when(jnp.logical_not(stays))(far.start)
 
     def moved_in(src, dst, slot):
         for s in range(2):
-            to = 2 * t + s
-
-            @pl.when(to == c)
+            stays, near, far = hop(src, dst, slot, s)
+            pl.when(stays)(near.wait)
+            pl.when(jnp.logical_not(stays))(far.wait_send)
+        for i in range(2):
+            cp = remote(
+                src.at[pl.ds(0, half)], dst.at[i], ms.at[slot, 0], mr.at[slot, i], place.line(c)
+            )
+            pl.when(i * tn + c // 2 != c)(cp.wait_recv)
+
+    exchanges = [("g", bit) for bit in place.bits] + [("t", 1 << i) for i in range(tn.bit_length() - 1)]
+
+    def exchange(layer, i):
+        kind, bit = exchanges[i]
+        to = place.group(flip(g, bit)) if kind == "g" else {"t": flip(t, bit)}
+        return remote(flat_o.at[layer], flatbox.at[layer, i], fs.at[layer, i], fr.at[layer, i], to)
+
+    def flat_turn(layer, i):
+        if i > 0:
+            exchange(layer, i - 1).wait()
+            flat_o[layer] += flatbox[layer, i - 1]
+        if i < len(exchanges):
+            exchange(layer, i).start()
+
+    masks = head_masks(width, BF16)
+    lane = lax.broadcasted_iota(jnp.int32, (1, 128), 1)
+    up = place.t // 2 >= (chips + 1) // 2
+
+    def pair(qb, kb):
+        qrows, krows = rows_of(qb, size), rows_of(kb, size)
+        queries, keys, vals = q[qrows, :], k[krows, :], v[krows, :]
+        grad = do[qrows, :]
+        side = lse[qrows, :]
+        bias = pair_bias(qb, kb, size, segcol, segrow)
+        dq_new = jnp.zeros((size, width), F32)
+        dk_new = jnp.zeros((size, width), F32)
+        dv_new = jnp.zeros((size, width), F32)
+        for h in range(heads):
+            qh, gh = queries * masks[h], grad * masks[h]
+            total = jnp.sum(jnp.where(lane == h, side, 0.0), axis=1, keepdims=True)
+            delta = jnp.sum(jnp.where(lane == 64 + h, side, 0.0), axis=1, keepdims=True)
+            p = jnp.exp(dot(qh, keys, NT) + bias - total)
+            ds = (p * (dot(gh, vals, NT) - delta)).astype(BF16)
+            dv_new = dv_new + dot(p.astype(BF16), gh, TN)
+            dk_new = dk_new + dot(ds, qh, TN)
+            dq_new = dq_new + dot(ds, keys * masks[h], NN)
+        dq[qrows, :] += dq_new
+        dk[krows, :] += dk_new
+        dv[krows, :] += dv_new
+
+    def columns(count, tile, body):
+        def step(j, carry):
+            body(rows_of(j, tile))
+            return carry
+
+        lax.fori_loop(0, count // tile, step, 0)
+
+    need(last, ["cot"])
+    dy[...] = gb[rows_of(t, size), :].astype(F32)
+    flat_o[...] = jnp.zeros_like(flat_o)
+
+    for layer in reversed(range(layers)):
+        flat = flat_o.at[layer]
+        vec = vecs.at[layer]
+        dwt, dwi, dwo, dwp = (accs[i][layer] for i in range(4))
+        ssem, fsem, rsem, cs, cr, ls, lr = group[layer]
+        spread = Spread(tn, gb, size, ssem, fsem, rsem)
+        gather = Gather(tn, *bufs, (cs, cr, ls, lr))
+        zc, co = spread.zc, spread.co
+
+        def tick(kind, late, layer=layer):
+            if layer + late < layers and reducing.taken[kind, layer + late] < reducing.steps:
+                reducing.advance(kind, layer + late)
+
+        own = dy[...].astype(BF16)
+        gb[rows_of(t, size), :] = own
+        spread.start()
+        if layer == last:
+            move(out_in, out_o, 0)
+        flat[4:5, :] = jnp.sum(own.astype(F32), axis=0, keepdims=True)
+        dbt[...] = jnp.zeros_like(dbt)
+        dbi[...] = jnp.zeros_like(dbi)
+        dk[...] = jnp.zeros_like(dk)
+        dv[...] = jnp.zeros_like(dv)
+        tick(2, 1)
+        tick(3, 1)
+        if layer < last:
+            flat_turn(layer + 1, 0)
+        for count, b in enumerate(arrivals(spread)):
+            need(layer, ["w3", "k4", "w2", "k7", "k5"])
+            rows = rows_of(b, size)
+            grad = gb[rows, :]
+            heads_grad = dot(grad, wp[...], NT).astype(BF16)
+            do[rows, :] = heads_grad
+            prod = heads_grad.astype(F32) * o[rows, :]
+            side = lse[rows, :]
+            for h in range(heads):
+                delta = jnp.sum(prod * masks[h].astype(F32), axis=1, keepdims=True)
+                side = jnp.where(lane == 64 + h, delta, side)
+            lse[rows, :] = side
+
+            def unit(cols):
+                d = (dot(grad, wo[cols, :], NT) * gp[rows, cols].astype(F32)).astype(BF16)
+                du[rows, cols] = d
+                dbi[0:1, cols] += jnp.sum(d.astype(F32), axis=0, keepdims=True)
+
+            columns(units, TILE, unit)
+            if layer < last:
+                flat_turn(layer + 1, count + 1)
+            if count == 1:
+                tick(1, 1)
+        need(layer, ["k6"])
+        spread.finish()
+
+        def grad_outer(cols):
+            dwo[cols, :] = dot(gact[:, cols], gb[...], TN).astype(BF16)
+
+        columns(units, TILE, grad_outer)
+
+        def grad_proj(cols):
+            dwp[cols, :] = dot(o[:, cols].astype(BF16), gb[...], TN).astype(BF16)
+
+        columns(width, TILE, grad_proj)
+        tick(2, 1)
+        tick(3, 1)
+        tick(2, 0)
+        tick(3, 0)
+        if layer < last:
+            flat_turn(layer + 1, len(exchanges))
+        need(layer, ["w1", "k0"])
+        if layer > 0:
+            load(layer - 1, ["w2", "w3"])
+        dq[...] = jnp.zeros_like(dq)
+        for b in range(tn):
+            rows = pl.ds(b * size, size)
+
+            def back(cols):
+                d = dot(du[rows, :], wi[cols, :], NT)
+                flat[2:3, cols] += jnp.sum(d * n[rows, cols].astype(F32), axis=0, keepdims=True)
+                flat[3:4, cols] += jnp.sum(d, axis=0, keepdims=True)
+                dh[rows, cols] = (d * vec[2:3, cols]).astype(BF16)
+
+            columns(model, TILE, back)
+
+        def grad_inner(cols):
+            h2 = (n[:, cols].astype(F32) * vec[2:3, cols] + vec[3:4, cols]).astype(BF16)
+            dwi[cols, :] = dot(h2, du[...], TN).astype(BF16)
+
+        columns(model, TILE, grad_inner)
+        tick(1, 1)
+        tick(0, 1)
+        tick(1, 0)
+        if layer > 0:
+            load(layer - 1, ["w1", "k7"])
+        need(layer, ["k1", "k2", "k3", "w0"])
+
+        for stage in range(tn):
+            pivot = jnp.where(up, stage, tn - 1 - stage)
+
+            def step(j, carry):
+                pair(jnp.where(up, pivot + j, pivot), jnp.where(up, pivot, pivot - j))
+                return carry
+
+            lax.fori_loop(0, tn - stage, step, 0)
+            rows = rows_of(pivot, size)
+            cos, sine = ctab[rows, :], stab[rows, :]
+            dt[rows, 0:width] = turn(dq[rows, :] * (1.0 / math.sqrt(HD)), cos, sine, -1.0).astype(BF16)
+            dt[rows, width : 2 * width] = turn(dk[rows, :], cos, sine, -1.0).astype(BF16)
+            dt[rows, 2 * width : 3 * width] = dv[rows, :].astype(BF16)
+            block = dt[rows, :]
+            dbt[...] += jnp.sum(block.astype(F32), axis=0, keepdims=True)
+            chip, core = pivot // 2, lax.rem(pivot, 2)
+
+            def back(cols):
+                d = dot(block, wt[cols, :], NT)
+                flat[0:1, cols] += jnp.sum(d * n[rows, cols].astype(F32), axis=0, keepdims=True)
+                flat[1:2, cols] += jnp.sum(d, axis=0, keepdims=True)
+                value = dh[rows, cols].astype(F32) + d * vec[0:1, cols]
+
+                @pl.when(core != co)
+                def _():
+                    gather.tocore[chip, :, cols] = value.astype(BF16)
+
+                @pl.when((core == co) & (chip != zc))
+                def _():
+                    gather.toici[chip, :, cols] = value.astype(BF16)
+
+                @pl.when(pivot == t)
+                def _():
+                    keep[:, cols] = value
+
+            columns(model, TILE, back)
+
+            @pl.when(core != co)
             def _():
-                pltpu.make_async_copy(src.at[pl.ds(s * half, half)], dst.at[place.h], ms.at[slot, s]).wait()
-
-            @pl.when(to != c)
-            def _():
-                remote(
-                    src.at[pl.ds(s * half, half)], dst.at[place.h], ms.at[slot, s], mr.at[slot, place.h], place.line(to)
-                ).wait_send()
-
-        for i in range(2):
-
-            @pl.when(i * tn + c // 2 != c)
-            def _():
-                remote(
-                    src.at[pl.ds(0, half)], dst.at[i], ms.at[slot, 0], mr.at[slot, i], place.line(c)
-                ).wait_recv()
-
-    move(grad_in, grad_o, 0)
-    move(out_in, out_o, 1)
-    orders = bit_orders(place)
-    chunks, slot = [], 0
-    plans = []
+                gather.send_core(chip)
+
+            if stage % 2 == 1:
+
+                @pl.when(chip != zc)
+                def _():
+                    gather.send_link(chip)
+
+            if stage == 0:
+                tick(1, 1)
+                tick(0, 1)
+            if stage == 1:
+                tick(2, 0)
+                tick(3, 0)
+            if stage == 2:
+                tick(0, 1)
+        tick(1, 0)
+
+        wide = width
+        for i in range(3):
+            start = pl.multiple_of(t * wide, 128)
+            flat[5 + i : 6 + i, pl.ds(start, wide)] = dbt[:, i * wide : (i + 1) * wide]
+        for i in range(gn):
+            row, start = divmod(i * tn * 128, model)
+            flat[8 + row : 9 + row, pl.ds(pl.multiple_of(start + t * 128, 128), 128)] = dbi[:, i * 128 : (i + 1) * 128]
+        if layer > 0:
+            load(layer - 1, ["w0", "k1", "k2", "k3", "k4", "k5", "k6"])
+
+        def grad_triple(cols):
+            h1 = (n[:, cols].astype(F32) * vec[0:1, cols] + vec[1:2, cols]).astype(BF16)
+            dwt[cols, :] = dot(h1, dt[...], TN).astype(BF16)
+
+        columns(model, TILE, grad_triple)
+        if layer > 0:
+            load(layer - 1, ["k0"])
+        tick(0, 0)
+        tick(2, 0)
+        tick(3, 0)
+        if layer == 0:
+            flat_turn(0, 0)
+        need(layer, ["x"])
+        own_n, inverse = norm_stats(x[...])
+        e = keep[...] + gather.total()
+        inner = e - jnp.mean(e, axis=-1, keepdims=True) - own_n * jnp.mean(e * own_n, axis=-1, keepdims=True)
+        dy[...] = dy[...] + inner * inverse
+        if layer > 0:
+            load(layer - 1, ["x"])
+        gather.finish()
+
+    low = gb.at[pl.ds(0, size)]
+    low[...] = dy[...].astype(BF16)
+    move(low, grad_o, 1)
+    rest = [(1, 0), (0, 0), (2, 0), (3, 0), (1, 0), (0, 0), (0, 0)]
+    for i, (kind, layer) in enumerate(rest):
+        if i + 1 <= len(exchanges):
+            flat_turn(0, i + 1)
+        reducing.advance(kind, layer)
     for layer in reversed(range(layers)):
         for kind in range(4):
-            plans.append((kind, layer))
-    for kind, layer in plans:
-        i = kind * layers + layer
-        acc = accs[i]
-        block = acc.shape[0] // gn
-        parts = []
-        for k, cols in enumerate(halves(acc.shape[1])):
-            parts.append(Halving(place, acc, boxes[kind].at[layer], block, cols, orders[k], (hs, hr), slot))
-            slot += 1
-        chunks.append(parts)
-
-    tbits = [1 << i for i in range(tn.bit_length() - 1)]
-    exchanges = [("g", bit) for bit in place.bits] + [("t", bit) for bit in tbits]
-    flat_o[...] = flat[...]
-
-    def exchange(k):
-        kind, bit = exchanges[k]
-        to = place.group(flip(g, bit)) if kind == "g" else {"t": flip(t, bit)}
-        return remote(flatbox.at[0, k], flatbox.at[1, k], fs.at[k], fr.at[k], to)
-
-    def flat_turn(k):
-        if k > 0 and k <= len(exchanges):
-            exchange(k - 1).wait_recv()
-            flat_o[...] += flatbox[1, k - 1]
-        if k < len(exchanges):
-            flatbox[0, k] = flat_o[...]
-            exchange(k).start()
-
-    steps = len(place.bits) + 1
-
-    def cross_copy(kind, layer, to, slot_of):
-        acc = accs[kind * layers + layer]
-        rows = acc.shape[0] // (gn * tn)
-        src = acc.at[pl.ds(pl.multiple_of((g * tn + to) * rows, rows), rows)]
-        return remote(
-            src, cross[kind].at[layer, t], cs.at[kind, layer, slot_of], cr.at[kind, layer, t], {"t": to}
-        )
-
-    def proj_copy(layer):
-        acc = accs[3 * layers + layer]
-        rows = acc.shape[0] // gn
-        src = acc.at[pl.ds(pl.multiple_of(g * rows, rows), rows)]
-        return src, remote(src, projbox.at[layer], ps.at[layer], pr.at[layer], source)
-
-    def owned(kind, layer):
-        acc = accs[kind * layers + layer]
-        if kind < 2:
-            rows = acc.shape[0] // (gn * tn)
-            for k in range(1, tn):
-                cross_copy(kind, layer, place.other(k), k).start()
-            cross[kind][layer, t] = acc[pl.ds(pl.multiple_of((g * tn + t) * rows, rows), rows), :]
-        elif kind == 2:
-            rows = acc.shape[0] // gn
-            outer_o[layer] = acc[pl.ds(pl.multiple_of(g * rows, rows), rows), :].astype(F32)
-        else:
-
-            @pl.when(moved)
-            def _():
-                proj_copy(layer)[1].start()
-
-            @pl.when(jnp.logical_not(moved))
-            def _():
-                rows = acc.shape[0] // gn
-                projbox[layer] = acc[pl.ds(pl.multiple_of(g * rows, rows), rows), :]
-
-    def settle(kind, layer):
-        if kind < 2:
-            for k in range(1, tn):
-                frm = place.other(k)
-                remote(
-                    cross[kind].at[layer, frm], cross[kind].at[layer, frm], cs.at[kind, layer, k],
-                    cr.at[kind, layer, frm], {"t": frm},
-                ).wait_recv()
-            groups = 3 if kind == 0 else gn
-            out = triple_o if kind == 0 else inner_o
-            wide = cross[kind].shape[3] // groups
-            for s in range(tn):
-                for i in range(groups):
-                    at = (i * tn + s) * wide
-                    out[layer, :, at : at + wide] = cross[kind][layer, s, :, i * wide : (i + 1) * wide].astype(F32)
-        elif kind == 3:
-
-            @pl.when(moved)
-            def _():
-                proj_copy(layer)[1].wait_recv()
-
-            proj_o[layer] = projbox[layer].astype(F32)
-
-    turns = len(chunks) + SKEW * (steps + 1)
-    for turn in range(max(turns, len(exchanges) + 1)):
-        if turn <= len(exchanges):
-            flat_turn(turn)
-        for step in reversed(range(steps + 2)):
-            i = turn - SKEW * step
-            if 0 <= i < len(chunks):
-                kind, layer = plans[i]
-                if step == 0:
-                    loads[kind * layers + layer].wait()
-                if step < steps:
-                    for part in chunks[i]:
-                        part.advance(step)
-                if step == steps - 1:
-                    owned(kind, layer)
-                if step == steps + 1:
-                    settle(kind, layer)
-    for k in range(len(exchanges)):
-        exchange(k).wait_send()
-    for (kind, layer), parts in zip(plans, chunks):
-        for part in parts:
-            part.finish()
-        if kind < 2:
-            for k in range(1, tn):
-                cross_copy(kind, layer, place.other(k), k).wait_send()
-        elif kind == 3:
-
-            @pl.when(moved)
-            def _():
-                proj_copy(layer)[1].wait_send()
-
-    moved_in(grad_in, grad_o, 0)
-    moved_in(out_in, out_o, 1)
-
-
-def close_call(gn, tn, output, grad, flat, mats):
-    layers = len(mats)
+            while reducing.taken[kind, layer] < reducing.steps:
+                reducing.advance(kind, layer)
+    reducing.finish()
+    moved_in(out_in, out_o, 0)
+    moved_in(low, grad_o, 1)
+
+
+def descend_call(gn, tn, cot, output, segcol, segrow, vecs, tables, xs, ws, kepts):
+    layers = len(xs)
     size, model = output.shape
-    dwts, dwis, dwos, dwps = ([m[k] for m in mats] for k in range(4))
+    length = size * tn
+    shapes = [ws[i][0].shape for i in range(4)]
+    width, units, chips = shapes[3][0], shapes[2][0], tn // 2
+    kept = kept_shapes(length, model, width, units)
     dma = pltpu.SemaphoreType.DMA
-    width3, units = dwts[0].shape[1], dwis[0].shape[1]
-    shard = dwts[0].shape[0] // (gn * tn)
-    prows, orows = dwps[0].shape[0] // gn, dwos[0].shape[0] // gn
-    every = dwts + dwis + dwos + dwps
-    boxes = [
-        pltpu.VMEM((layers, (gn - 1) * m.shape[0] // gn, m.shape[1]), BF16)
-        for m in (dwts[0], dwis[0], dwos[0], dwps[0])
-    ]
+    shard = shapes[0][0] // (gn * tn)
+    prows, orows = shapes[3][0] // gn, shapes[2][0] // gn
     exchanges = (gn * tn).bit_length() - 1
-
-    def body(out_in, grad_in, flat_in, *rest):
-        refs = list(rest)
-        groups = [refs[i * layers : (i + 1) * layers] for i in range(4)]
-        outs = refs[4 * layers : 4 * layers + 7]
-        rest = refs[4 * layers + 7 :]
-        accs, rest = rest[: 4 * layers], rest[4 * layers :]
-        box, rest = rest[:4], rest[4:]
-        cross, rest = rest[:2], rest[2:]
-        close_kernel(gn, tn, layers, out_in, grad_in, flat_in, *groups, *outs, accs, box, cross, *rest)
-
     outs = (
         shape((2, size // 2, model), BF16),
         shape((2, size // 2, model), BF16),
-        shape(flat.shape, F32),
-        shape((layers, shard, width3 * tn), F32),
-        shape((layers, prows, model), F32),
-        shape((layers, shard, units * tn), F32),
-        shape((layers, orows, model), F32),
+        shape((layers, 16, model), F32),
+        shape((layers, tn, shard, 3 * width), BF16),
+        shape((layers, tn, shard, units), BF16),
+        shape((layers, prows, model), BF16),
+        shape((layers, orows, model), BF16),
     )
+    scratch = [pltpu.VMEM(dims, BF16) for dims in shapes]
+    scratch += [pltpu.VMEM(*item) for item in kept]
+    scratch += [
+        pltpu.VMEM((size, model), F32),
+        pltpu.VMEM((size, model), F32),
+        pltpu.VMEM((length, model), BF16),
+        pltpu.VMEM((length, width), BF16),
+        pltpu.VMEM((length, 3 * width), BF16),
+        pltpu.VMEM((length, width), F32),
+        pltpu.VMEM((length, width), F32),
+        pltpu.VMEM((size, model), F32),
+        pltpu.VMEM((1, 3 * width), F32),
+        pltpu.VMEM((1, units), F32),
+    ]
+    scratch += group_buffers(chips, size, model)
+    for dims in shapes:
+        scratch += [pltpu.VMEM(dims, BF16)] * layers
+    scratch += [pltpu.VMEM((layers, (gn - 1) * dims[0] // gn, dims[1]), BF16) for dims in shapes]
+    scratch += [pltpu.VMEM((layers, exchanges, 16, model), F32)]
+    for _ in range(layers):
+        scratch += group_sems(chips, tn)
     slots = 8 * layers
+    scratch += [
+        dma((slots, gn)), dma((slots, gn)), dma((2, layers, tn)), dma((2, layers, tn)), dma((layers,)), dma((layers,)),
+        dma((3, layers)),
+        dma((14 * layers,)), dma((2, 2)), dma((2, 2)), dma((layers, exchanges)), dma((layers, exchanges)),
+    ]
+
+    def body(*refs):
+        refs = list(refs)
+
+        def take(count):
+            out, refs[:] = refs[:count], refs[count:]
+            return out
+
+        ins = take(7)
+        x_in = take(layers)
+        w_in = [take(layers) for _ in range(4)]
+        kept_in = [take(8) for _ in range(layers)]
+        results = take(7)
+        w, kept_s = take(4), take(8)
+        work = take(10)
+        bufs = take(4)
+        accs = [take(layers) for _ in range(4)]
+        boxes = take(4)
+        flatbox = take(1)[0]
+        group = [take(7) for _ in range(layers)]
+        reduce_sems = take(7)
+        descend_kernel(
+            gn, tn, layers, size, *ins, x_in, w_in, kept_in, *results, w, kept_s, *work, bufs, accs, boxes,
+            flatbox, group, reduce_sems, *take(5),
+        )
+
+    flat_ws = [ws[i][layer] for i in range(4) for layer in range(layers)]
+    flat_kept = [ref for layer in range(layers) for ref in kepts[layer]]
     return pl.pallas_call(
         body,
         out_shape=outs,
-        in_specs=[ANY, ANY, VM] + [ANY] * (4 * layers),
-        out_specs=(ANY, ANY, VM, VM, VM, VM, VM),
-        scratch_shapes=[pltpu.VMEM(m.shape, BF16) for m in every]
-        + boxes
-        + [
-            pltpu.VMEM((layers, tn, shard, width3), BF16),
-            pltpu.VMEM((layers, tn, shard, units), BF16),
-            pltpu.VMEM((layers, prows, model), BF16),
-            pltpu.VMEM((2, exchanges) + flat.shape, F32),
-            dma((4 * layers,)),
-            dma((slots, gn)), dma((slots, gn)),
-            dma((2, layers, tn)), dma((2, layers, tn)),
-            dma((layers,)), dma((layers,)),
-            dma((2, 2)), dma((2, 2)),
-            dma((exchanges,)), dma((exchanges,)),
-        ],
+        in_specs=[ANY, ANY] + [VM] * 5 + [ANY] * (layers + len(flat_ws) + len(flat_kept)),
+        out_specs=(ANY, ANY, VM, ANY, ANY, ANY, ANY),
+        scratch_shapes=scratch,
         compiler_params=params_of(3),
-        name="closing",
-    )(output, grad, flat, *dwts, *dwis, *dwos, *dwps)
+        name="descend",
+    )(cot, output, segcol, segrow, vecs, *tables, *xs, *flat_ws, *flat_kept)
 
 
 GROUPS = ("dp", "h")
@@ -1559,7 +1810,7 @@
     rows = triple_weight.shape[1]
     block = tokens.shape[1]
     tables = constant_tables(span, shards, model)
-    direct = rows % 16 == 0 and block == 128 and layers * 4 <= 16
+    direct = rows % 16 == 0 and block == 128 and layers * 4 <= 16 and units == model
     if direct:
         head = jnp.stack(
             [
@@ -1583,8 +1834,14 @@
         inputs = opened[7 : 7 + layers]
         weights = [tuple(opened[7 + layers + k * layers + layer] for k in range(4)) for layer in range(layers)]
         kept = [opened[7 + 5 * layers + 8 * i : 7 + 5 * layers + 8 * (i + 1)] for i in range(layers)]
-        cot = cot.astype(F32)
-        tables = (segcol, segrow) + tables
+        output, tokens_grad, summed, triple, inner, proj, outer = descend_call(
+            gn, tn, cot, output, segcol, segrow, vecs, tables, inputs,
+            [[weights[layer][k] for layer in range(layers)] for k in range(4)], kept,
+        )
+        summed = summed.reshape(layers, -1)
+        triple = triple.reshape(layers, tn, rows, 3, -1).transpose(0, 2, 3, 1, 4).reshape(layers, rows, -1).astype(F32)
+        inner = inner.reshape(layers, tn, rows, gn, -1).transpose(0, 2, 3, 1, 4).reshape(layers, rows, -1).astype(F32)
+        proj, outer = proj.astype(F32), outer.astype(F32)
     else:
         small = (triple_bias, inner_bias, proj_bias, outer_bias, first_gain, first_shift, second_gain, second_shift)
         starts = [0]
@@ -1625,32 +1882,23 @@
             )
             kept.append(saved)
         output = x.astype(BF16)
-    grad = cot
-    mats, flats = [None] * layers, [None] * layers
-    for layer in reversed(range(layers)):
-        grad, dwt, dwi, dwo, dwp, dvec, dbt, dbi = backward_layer(
-            tn, grad, inputs[layer], weights[layer], vecs[layer], tables, kept[layer]
-        )
-        mats[layer] = (dwt, dwi, dwo, dwp)
-        triple = lax.dynamic_update_slice(
-            jnp.zeros((3, tn, heads_wide), F32), dbt.reshape(3, 1, heads_wide), (0, t, 0)
-        )
-        inner = lax.dynamic_update_slice(
-            jnp.zeros((gn, tn, units // gn), F32), dbi.reshape(gn, 1, units // gn), (0, t, 0)
-        )
-        flats[layer] = jnp.concatenate([dvec[:5].reshape(-1), triple.reshape(-1), inner.reshape(-1)])
-    tokens_grad = grad.astype(BF16)
-    flat = jnp.stack(flats)
-    if direct:
-        output, tokens_grad, summed, triple, proj, inner, outer = close_call(
-            gn, tn, output, tokens_grad, flat.reshape(-1, 1024), mats
-        )
-        summed = summed.reshape(flat.shape)
-    else:
-        output, tokens_grad = from_group(tn, output), from_group(tn, tokens_grad)
-        done = [reduce_weights(gn, tn, *m) for m in mats]
-        triple, proj, inner, outer = (jnp.stack([m[k] for m in done]) for k in range(4))
-        summed = lax.psum(flat, EVERY)
+        grad = cot
+        mats, flats = [None] * layers, [None] * layers
+        for layer in reversed(range(layers)):
+            grad, dwt, dwi, dwo, dwp, dvec, dbt, dbi = backward_layer(
+                tn, grad, inputs[layer], weights[layer], vecs[layer], tables, kept[layer]
+            )
+            mats[layer] = reduce_weights(gn, tn, dwt, dwi, dwo, dwp)
+            part = lax.dynamic_update_slice(
+                jnp.zeros((3, tn, heads_wide), F32), dbt.reshape(3, 1, heads_wide), (0, t, 0)
+            )
+            side = lax.dynamic_update_slice(
+                jnp.zeros((gn, tn, units // gn), F32), dbi.reshape(gn, 1, units // gn), (0, t, 0)
+            )
+            flats[layer] = jnp.concatenate([dvec[:5].reshape(-1), part.reshape(-1), side.reshape(-1)])
+        output, tokens_grad = from_group(tn, output), from_group(tn, grad.astype(BF16))
+        triple, proj, inner, outer = (jnp.stack([m[k] for m in mats]) for k in range(4))
+        summed = lax.psum(jnp.stack(flats), EVERY)
 
     def own(start, length):
         piece = length // shards

time: 512 us -> 418 us (0.82)
  Pallas kernels: 477 us -> 390 us
  local copies, waits for them, and re-layouts: 20.7 us -> 15 us
    pallas_call x3 -> x1, Pallas kernels: 285 us -> 206 us  [descend_call(): pl.pallas_call(body, out_shape=outs, in_specs=[ANY, ANY] + [VM] * 5 + [AN...]
    pallas_call x1, Pallas kernels: 192 us -> 183 us  [ascend_call(): pl.pallas_call(body, out_shape=tuple((o for o, _ in outs)), in_specs=[ANY...]
where the time goes in v4:
time: 418 us; the launch traced here: 410 us
  Pallas kernels  390 us (93%)
  local copies, waits for them, and re-layouts  15 us (4%)
    pallas_call x1, Pallas kernels, descend_call(): pl.pallas_call(body, out_shape=outs, in_specs=[ANY, ANY] + [VM] * 5 + [AN...  206 us
    pallas_call x1, Pallas kernels, ascend_call(): pl.pallas_call(body, out_shape=tuple((o for o, _ in outs)), in_specs=[ANY...  183 us

profile of v4, /device:TPU:5, one launch (start us, length us, event | category | flops | bytes accessed | tf_op | source)
XLA Modules:
  0.0 410.0 jit_solution(16893775587513113708)
XLA Ops:
  0.6 0.0 copy-start.3
  0.7 0.8 maximum_bitcast_fusion
  1.5 0.7 fusion.3
  2.3 0.7 pad_maximum_fusion
  2.9 0.6 pad.19.refs_3_
  3.5 1.4 reshape.63
  4.9 0.1 copy.54
  5.0 0.0 copy-start.8
  5.0 1.0 reshape.64.refs_5_
  6.0 0.3 reshape.61
  6.3 0.2 copy.55
  6.5 1.2 reshape.62.refs_4_
  7.7 0.6 pad.16.refs_2_
  8.3 183.3 %ascend.1 = (bf16[256,1024]{1,0:T(8,128)(2,1)}, bf16[256,1024]{1,0:T(8,128)(2,1)}, f32[1024,1]{1,0:T(8,128)}, f32[1,1024]{1,0:T(1,128)}, f32[2,8,1024]{2,1,0:T(8...) custom-call(bf16[2,128,1024]{2,1,0:T(8,128)(2,1)} %refs_0_.1, ...), custom_call_target="tpu_custom_call" | custom-call | tf_op jit(solution)/shard_map/ascend/pallas_call | solution.py:1166
  191.7 206.4 %descend.1 = (bf16[2,128,1024]{2,1,0:T(8,128)(2,1)}, bf16[2,128,1024]{2,1,0:T(8,128)(2,1)}, f32[2,16,1024]{2,1,0:T(8,128)}, bf16[2,4,32,768]{3,2,1,0:T(8,128)(2,...) custom-call(bf16[256,1024]{1,0:T(8,128)(2,1)} %get-tuple-element.53.refs_0_, ...), custom_call_target="tpu_custom_call" | custom-call | tf_op jit(solution)/shard_map/descend/pallas_call | solution.py:1708
  398.1 1.2 copy.51
  399.3 0.7 copy.49
  400.0 1.4 reshape.67
  401.4 0.4 reshape.68
  401.8 0.0 copy-start.6
  401.8 0.5 copy.48
  402.3 1.3 reshape.66
  403.6 1.1 convert_element_type.45
  404.7 0.1 copy.50
  404.8 0.7 constant_dynamic-slice_fusion
  405.5 0.0 copy-done.5
  405.5 0.7 convert_element_type.40
  406.2 0.6 constant_dynamic-slice_fusion.4
  406.8 0.6 constant_dynamic-slice_fusion.7
  407.4 0.6 copy.59
  408.0 0.8 copy.60
  408.8 0.8 copy.61
  (15 shorter events, 0.0 us)
Async XLA Ops:
  0.6 5.4 %copy-start.3 = (bf16[2,32,3072]{2,1,0:T(8,128)(2,1)S(1)}, bf16[2,32,3072]{2,1,0:T(8,128)(2,1)}, u32[]{:S(2)}) copy-start(bf16[2,32,3072]{2,1,0:T(8,128)(2,1)} %param.24) | copy-start | bytes 1179652
  5.0 2.7 copy-start.8
  399.3 2.1 copy-start.4
  401.4 2.3 copy-start
  401.8 2.9 copy-start.6
  402.3 3.2 copy-start.5
  402.3 5.7 %copy-start.2 = (bf16[2,128,1024]{2,1,0:T(8,128)(2,1)S(1)}, bf16[2,128,1024]{2,1,0:T(8,128)(2,1)}, u32[]{:S(2)}) copy-start(bf16[2,128,1024]{2,1,0:T(8,128)(2,1)} %get-tuple-element.144) | copy-start | bytes 1572868
  403.6 5.2 %copy-start.1 = (bf16[2,128,1024]{2,1,0:T(8,128)(2,1)S(1)}, bf16[2,128,1024]{2,1,0:T(8,128)(2,1)}, u32[]{:S(2)}) copy-start(bf16[2,128,1024]{2,1,0:T(8,128)(2,1)} %get-tuple-element.145) | copy-start | bytes 1572868
  405.5 4.1 copy-start.7
